TPU v7x, 512 devices: a whole 4x8x8 slice. The times are simulated.
512 devices in a mesh: seq: 64 (over x, y, core), head: 8 (over z).
Axes of the slice: x: 4, y: 8, z: 8, core: 2. Of those that a mesh axis runs over, the one named last changes fastest.
Arguments:
- x_stream: bfloat16 [16384, 8192], P(('seq', 'head')), may hold values from -0.59765625 to 0.59765625
- z_stream: bfloat16 [16384, 8192], P(('seq', 'head')), may hold values from -6 to 6
- b_stream: bfloat16 [16384, 1024], P(('seq', 'head')), may hold values from -1.5 to 1.5
- c_stream: bfloat16 [16384, 1024], P(('seq', 'head')), may hold values from -6 to 6
- dt_stream: bfloat16 [16384, 128], P(('seq', 'head')), may hold values from 0 to 1, as said below
- decay_stream: bfloat16 [16384, 128], P(('seq', 'head')), may hold values from -1 to 0, as said below
- kernel_x: bfloat16 [4, 8192], P(None, 'head'), may hold values from -3 to 3
- kernel_b: bfloat16 [4, 1024], P(None, 'head'), may hold values from -3 to 3
- kernel_c: bfloat16 [4, 1024], P(None, 'head'), may hold values from -3 to 3
- skip_gain: float32 [128], P('head'), may hold values from 0.25 to 1.75
- norm_gain: bfloat16 [8192], replicated, may hold values from 0.5 to 1.5
Outputs:
- layer_out: bfloat16 [16384, 8192], P(('seq', 'head'))
Inputs may be any that keep to these rules, and one draw needn't show every extreme that they name: `dt_stream`: positive step sizes. `decay_stream`: non-positive log-decays.
All inputs are finite; a program needn't handle non-finite values.
Results may differ from a plain program's by a relative error of at most 0.012.
Values may be sent and summed in bfloat16 or wider, within the bound.
No kernel may reach another device: no remote copies, remote signals or barrier semaphores. Data moves between devices by JAX's collectives and lax.ppermute only.
A program may use at most 128 MiB of HBM per device.

v0:
```python
import jax
import jax.numpy as jnp
from jax import lax
from jax.sharding import PartitionSpec as P

MIXER_HEADS = 128
HEAD_DIM = 64
STATE = 128
GROUPS = 8
SPAN = 128


def shifted(x, axis, by):
    peers = lax.axis_size(axis)
    pairs = [(i, i + by) for i in range(peers) if 0 <= i + by < peers]
    return lax.ppermute(x, axis, pairs)


def carried_in(x, axis, combine, identity):
    peers, place = (lax.axis_size(axis), lax.axis_index(axis))
    everything = jax.tree.map(
        lambda part, kind: lax.all_gather(part.astype(kind), axis), x, (jnp.bfloat16, jnp.bfloat16)
    )
    start = jax.tree.map(
        lambda part, zero: jnp.broadcast_to(jnp.asarray(zero, part.dtype), part.shape), x, identity
    )

    def step(k, before):
        reached = k < place
        new = combine(
            before, jax.tree.map(lambda part, own: part[k].astype(own.dtype), everything, x)
        )
        return jax.tree.map(lambda a, b: jnp.where(reached, a, b), new, before)

    return lax.fori_loop(0, peers, step, start)


def conv_silu(values, border, kernel):
    row_count = values.shape[0]
    padded = jnp.concatenate([border, values], 0).astype(jnp.float32)
    taps = kernel.astype(jnp.float32)
    total = padded[0:row_count] * taps[0]
    for offset in range(1, kernel.shape[0]):
        total = total + padded[offset : offset + row_count] * taps[offset]
    return jax.nn.silu(total).astype(jnp.bfloat16)


def gated_norm(values, gate_in, gain, group_width):
    gated = values.astype(jnp.float32) * jax.nn.silu(gate_in.astype(jnp.float32))
    row_count, width = gated.shape
    grouped = gated.reshape(row_count, width // group_width, group_width)
    scale = lax.rsqrt(jnp.mean(grouped * grouped, axis=-1, keepdims=True) + 1e-05)
    return ((grouped * scale).reshape(row_count, width) * gain.astype(jnp.float32)).astype(
        jnp.bfloat16
    )


def chain_combine(earlier, later):
    return (earlier[0] + later[0], jnp.exp(later[0])[:, None, None] * earlier[1] + later[1])


def shards(
    x_stream,
    z_stream,
    b_stream,
    c_stream,
    dt_stream,
    decay_stream,
    kernel_x,
    kernel_b,
    kernel_c,
    skip_gain,
    norm_gain,
):
    x_head, z_head, b_head, c_head, dt_head, decay_head = (
        lax.all_to_all(x_stream, "head", split_axis=1, concat_axis=0, tiled=True),
        lax.all_to_all(z_stream, "head", split_axis=1, concat_axis=0, tiled=True),
        lax.all_to_all(b_stream, "head", split_axis=1, concat_axis=0, tiled=True),
        lax.all_to_all(c_stream, "head", split_axis=1, concat_axis=0, tiled=True),
        lax.all_to_all(dt_stream, "head", split_axis=1, concat_axis=0, tiled=True),
        lax.all_to_all(decay_stream, "head", split_axis=1, concat_axis=0, tiled=True),
    )
    border = kernel_x.shape[0] - 1
    rim_x, rim_b, rim_c = shifted((x_head[-border:], b_head[-border:], c_head[-border:]), "seq", 1)
    x_conv = conv_silu(x_head, rim_x, kernel_x)
    b_conv = conv_silu(b_head, rim_b, kernel_b)
    c_conv = conv_silu(c_head, rim_c, kernel_c)
    row_count = x_conv.shape[0]
    spans = row_count // SPAN
    head_count = x_conv.shape[1] // HEAD_DIM
    group_count = b_conv.shape[1] // STATE
    per_group = MIXER_HEADS // GROUPS
    x_blocks = x_conv.reshape(spans, SPAN, group_count, per_group, HEAD_DIM)
    b_blocks = b_conv.reshape(spans, SPAN, group_count, STATE)
    c_blocks = c_conv.reshape(spans, SPAN, group_count, STATE)
    dt_blocks = dt_head.astype(jnp.float32).reshape(spans, SPAN, head_count)
    running = jnp.cumsum(decay_head.astype(jnp.float32).reshape(spans, SPAN, head_count), axis=1)
    causal = jnp.arange(SPAN)[:, None] >= jnp.arange(SPAN)[None, :]
    scores = jnp.einsum("ctgn,csgn->cgts", c_blocks, b_blocks, preferred_element_type=jnp.float32)
    run_heads = jnp.swapaxes(running, 1, 2)
    gap = run_heads[:, :, :, None] - run_heads[:, :, None, :]
    decay_matrix = jnp.where(causal, jnp.exp(jnp.where(causal, gap, 0.0)), 0.0)
    decay_matrix = decay_matrix * jnp.swapaxes(dt_blocks, 1, 2)[:, :, None, :]
    weights = (
        decay_matrix.reshape(spans, group_count, per_group, SPAN, SPAN) * scores[:, :, None]
    ).astype(jnp.bfloat16)
    intra = jnp.einsum("cgkts,csgkp->ctgkp", weights, x_blocks, preferred_element_type=jnp.float32)
    tail = jnp.exp(running[:, -1:, :] - running) * dt_blocks
    weighted_input = (
        x_blocks.astype(jnp.float32) * tail.reshape(spans, SPAN, group_count, per_group, 1)
    ).astype(jnp.bfloat16)
    fresh = jnp.einsum(
        "csgkp,csgn->cgkpn", weighted_input, b_blocks, preferred_element_type=jnp.float32
    )
    fresh = fresh.reshape(spans, head_count, HEAD_DIM, STATE)
    totals = running[:, -1, :]

    def advance(state, inputs):
        total, contribution = inputs
        return (jnp.exp(total)[:, None, None] * state + contribution, state)

    empty_state = jnp.zeros((head_count, HEAD_DIM, STATE), jnp.float32)
    final_state, starts = lax.scan(advance, empty_state, (totals, fresh))
    device_total = jnp.sum(totals, axis=0)
    identity = (jnp.zeros((head_count,), jnp.float32), empty_state)
    _, incoming = carried_in((device_total, final_state), "seq", chain_combine, identity)
    before = jnp.cumsum(totals, axis=0) - totals
    c_float = c_blocks.astype(jnp.float32)
    states = starts + jnp.exp(before)[:, :, None, None] * incoming[None]
    inter = jnp.einsum(
        "ctgn,cgkpn->ctgkp",
        c_float,
        states.reshape(spans, group_count, per_group, HEAD_DIM, STATE),
        precision=lax.Precision.HIGHEST,
    )
    inter = inter * jnp.exp(running).reshape(spans, SPAN, group_count, per_group, 1)
    skip_rows = skip_gain.reshape(1, 1, group_count, per_group, 1)
    head_output = (
        (intra + inter + skip_rows * x_blocks.astype(jnp.float32))
        .reshape(row_count, head_count * HEAD_DIM)
        .astype(jnp.bfloat16)
    )
    group_width = per_group * HEAD_DIM
    width = head_count * HEAD_DIM
    gain_slice = lax.dynamic_slice_in_dim(norm_gain, lax.axis_index("head") * width, width)
    normed = gated_norm(head_output, z_head, gain_slice, group_width)
    result = lax.all_to_all(normed, "head", split_axis=0, concat_axis=1, tiled=True)
    return result


def solution(mesh):
    in_specs = (
        P(("seq", "head"), None),
        P(("seq", "head"), None),
        P(("seq", "head"), None),
        P(("seq", "head"), None),
        P(("seq", "head"), None),
        P(("seq", "head"), None),
        P(None, "head"),
        P(None, "head"),
        P(None, "head"),
        P("head"),
        P(),
    )
    out_specs = P(("seq", "head"), None)
    return jax.shard_map(shards, mesh=mesh, in_specs=in_specs, out_specs=out_specs, check_vma=False)
```

profile of v0, /device:TPU:1, one launch (start us, length us, event | category | flops | bytes accessed | tf_op | source)
XLA Modules:
  0.0 390.0 jit_solution(12541164260312601166)
XLA Ops:
  8.1 10.9 %all-to-all-start.1 = ((bf16[8,2,256]{2,1,0:T(2,128)(2,1)}), bf16[8,2,256]{2,1,0:T(2,128)(2,1)S(1)}, u32[]{:S(2)}, u32[]{:S(2)}) async-start(bf16[8,2,256]{2,1,0:T(2,128)(2,1)} %reshape.251), calls=%async_computation.1 | async-start | bytes 16384 | tf_op jit(solution)/shard_map/all_to_all | solution.py:81
  21.1 4.4 %all-to-all-done.1 = bf16[8,2,256]{2,1,0:T(2,128)(2,1)S(1)} async-done(((bf16[8,2,256]{2,1,0:T(2,128)(2,1)}), bf16[8,2,256]{2,1,0:T(2,128)(2,1)S(1)}, u32[]{:S(2)}, u32[]{:S(2)}) %all-to-all-start.1) | async-done | bytes 8224 | tf_op jit(solution)/shard_map/all_to_all | solution.py:81
  25.5 3.3 all-to-all-start.2
  29.7 1.9 copy.103
  32.3 3.1 all-to-all-done.2
  35.4 3.5 all-to-all-start.4
  39.0 7.1 %all-to-all-done.4 = bf16[32,8,128]{2,0,1:T(8,128)(2,1)S(1)} async-done(((bf16[32,8,128]{2,0,1:T(8,128)(2,1)}), bf16[32,8,128]{2,0,1:T(8,128)(2,1)S(1)}, u32[]{:S(2)}, u32[]{:S(2)}) %all-to-all-start.4) | async-done | bytes 65568 | tf_op jit(solution)/shard_map/all_to_all | solution.py:78
  46.1 3.5 all-to-all-start
  50.7 7.3 %collective-permute-start.2 = (bf16[3,128]{1,0:T(4,128)(2,1)S(1)}, bf16[3,128]{1,0:T(4,128)(2,1)S(1)}, u32[]{:S(2)}, u32[]{:S(2)}) collective-permute-start(bf16[3,128]{1,0:T(4,128)(2,1)S(1)} %slice.127), channel_id=1, source_target_pairs={{0,8},{8,16},{16,24},{24,32},{32,40},{40,48},{48,56},{56,64},{64,7... | collective-permute-start | bytes 2312 | tf_op jit(solution)/shard_map/ppermute | solution.py:16
  58.8 3.5 all-to-all-done
  62.3 8.7 %collective-permute-start = (bf16[3,1024]{1,0:T(4,128)(2,1)S(1)}, bf16[3,1024]{1,0:T(4,128)(2,1)S(1)}, u32[]{:S(2)}, u32[]{:S(2)}) collective-permute-start(bf16[3,1024]{1,0:T(4,128)(2,1)S(1)} %slice.113), channel_id=1, source_target_pairs={{0,8},{8,16},{16,24},{24,32},{32,40},{40,48},{48,56},{56,64},{64,7... | collective-permute-start | bytes 18440 | tf_op jit(solution)/shard_map/ppermute | solution.py:16
  74.1 1.7 while.27
  76.6 1.5 copy_bitcast_fusion.3
  78.1 3.3 all-to-all-start.3
  81.5 1.9 copy.102
  83.4 5.2 %all-to-all-done.3 = bf16[32,8,128]{2,0,1:T(8,128)(2,1)S(1)} async-done(((bf16[32,8,128]{2,0,1:T(8,128)(2,1)}), bf16[32,8,128]{2,0,1:T(8,128)(2,1)S(1)}, u32[]{:S(2)}, u32[]{:S(2)}) %all-to-all-start.3) | async-done | bytes 65568 | tf_op jit(solution)/shard_map/all_to_all | solution.py:79
  88.6 3.5 all-to-all-start.5
  92.1 1.3 dynamic-slice_convert_fusion
  93.4 1.3 dynamic-slice
  96.9 5.3 %collective-permute-start.1 = (bf16[3,128]{1,0:T(4,128)(2,1)S(1)}, bf16[3,128]{1,0:T(4,128)(2,1)S(1)}, u32[]{:S(2)}, u32[]{:S(2)}) collective-permute-start(bf16[3,128]{1,0:T(4,128)(2,1)S(1)} %slice.122), channel_id=1, source_target_pairs={{0,8},{8,16},{16,24},{24,32},{32,40},{40,48},{48,56},{56,64},{64,7... | collective-permute-start | bytes 2312 | tf_op jit(solution)/shard_map/ppermute | solution.py:16
  102.2 124.1 %all-reduce = bf16[1024]{0:T(1024)(128)(2,1)S(1)} all-reduce(bf16[1024]{0:T(1024)(128)(2,1)S(1)} %dynamic-update-slice), channel_id=2, replica_groups=mesh['seq'=64,'head'=8] {'seq'}, use_global_device_ids=true, to_apply=%add | all-reduce | flops 1024 | bytes 4096
  231.0 1.7 reshape.239
  232.7 1.8 copy.79
  235.0 1.8 copy.75
  236.8 114.9 %while.28 = (s32[]{:T(128)}, f32[16,64,128]{2,1,0:T(8,128)S(1)}, s32[]{:T(128)}, bf16[64,16]{1,0:T(8,128)(2,1)}, bf16[64,16,64,128]{3,2,1,0:T(8,128)(2,1)}, /*index=5*/s32[]{:T(128)}, s32[]{:T(128)}) while((s32[]{:T(128)}, f32[16,64,128]{2,1,0:T(8,128)S(1)}, s32[]{:T(128)}, bf16[64,16]{1,0:T(8,128)(2,1)}, ...), condition=%wide.region_6.7_spmd.clone, body=%wide.region_5.6_spmd.clone.sunk | while | flops 655380 | bytes 1310985 | solution.py:35
  237.6 1.1 fusion.43
  239.4 1.1 fusion.43
  241.2 1.1 fusion.43
  243.0 1.1 fusion.43
  244.8 1.1 fusion.43
  246.6 1.1 fusion.43
  248.4 1.1 fusion.43
  250.2 1.1 fusion.43
  252.0 1.1 fusion.43
  253.8 1.1 fusion.43
  255.6 1.1 fusion.43
  257.4 1.1 fusion.43
  259.2 1.1 fusion.43
  261.0 1.1 fusion.43
  262.8 1.1 fusion.43
  264.6 1.1 fusion.43
  266.4 1.1 fusion.43
  268.2 1.1 fusion.43
  270.0 1.1 fusion.43
  271.8 1.1 fusion.43
  275.3 1.1 fusion.43
  277.1 1.1 fusion.43
  291.4 1.1 fusion.43
  293.2 1.1 fusion.43
  295.0 1.1 fusion.43
  320.2 1.1 fusion.43
  322.0 1.1 fusion.43
  323.8 1.1 fusion.43
  332.7 1.1 fusion.43
  334.5 1.1 fusion.43
  338.1 1.1 fusion.43
  339.9 1.1 fusion.43
  348.9 1.1 fusion.43
  350.7 1.1 fusion.43
  353.5 2.1 multiply_reduce_fusion
  355.6 2.2 copy.76
  357.8 1.5 reshape.238
  359.4 1.6 multiply_convert_fusion.2
  361.0 21.4 %all_to_all.112 = bf16[8,32,1024]{2,1,0:T(8,128)(2,1)S(1)} all-to-all(bf16[8,32,1024]{2,1,0:T(8,128)(2,1)S(1)} %multiply_convert_fusion.2), channel_id=1, replica_groups=mesh['seq'=64,'head'=8] {'head'}, dimensions={0} | all-to-all | bytes 1048576 | tf_op jit(solution)/shard_map/all_to_all | solution.py:147
  (204 shorter events, 98.5 us)
Async XLA Ops:
  6.5 12.4 %copy-start = (bf16[32,1024]{1,0:T(8,128)(2,1)S(1)}, bf16[32,1024]{1,0:T(8,128)(2,1)}, u32[]{:S(2)}) copy-start(bf16[32,1024]{1,0:T(8,128)(2,1)} %param.17) | copy-start | bytes 196612
  8.1 17.4 %all-to-all-start.1 = ((bf16[8,2,256]{2,1,0:T(2,128)(2,1)}), bf16[8,2,256]{2,1,0:T(2,128)(2,1)S(1)}, u32[]{:S(2)}, u32[]{:S(2)}) async-start(bf16[8,2,256]{2,1,0:T(2,128)(2,1)} %reshape.251), calls=%async_computation.1 | async-start | bytes 16384 | tf_op jit(solution)/shard_map/all_to_all | solution.py:81
  25.5 9.8 %all-to-all-start.2 = ((bf16[8,2,256]{2,1,0:T(2,128)(2,1)}), bf16[8,2,256]{2,1,0:T(2,128)(2,1)S(1)}, u32[]{:S(2)}, u32[]{:S(2)}) async-start(bf16[8,2,256]{2,1,0:T(2,128)(2,1)} %reshape.253), calls=%async_computation.2 | async-start | bytes 16384 | tf_op jit(solution)/shard_map/all_to_all | solution.py:80
  35.4 10.7 %all-to-all-start.4 = ((bf16[32,8,128]{2,0,1:T(8,128)(2,1)}), bf16[32,8,128]{2,0,1:T(8,128)(2,1)S(1)}, u32[]{:S(2)}, u32[]{:S(2)}) async-start(bf16[32,8,128]{2,0,1:T(8,128)(2,1)} %copy_bitcast_fusion.2), calls=%async_computation.4 | async-start | bytes 131072 | tf_op jit(solution)/shard_map/all_to_all | solution.py:78
  46.1 16.2 %all-to-all-start = ((bf16[32,8,1024]{2,0,1:T(8,128)(2,1)}), bf16[32,8,1024]{2,0,1:T(8,128)(2,1)S(1)}, u32[]{:S(2)}, u32[]{:S(2)}) async-start(bf16[32,8,1024]{2,0,1:T(8,128)(2,1)} %bitcast.123), calls=%async_computation | async-start | bytes 1048576 | tf_op jit(solution)/shard_map/all_to_all | solution.py:76
  49.6 187.2 %all-gather.4.cloned.1.call-start = ((), (), s32[]{:S(2)}) async-start(), calls=%async_computation.7 | async-start | bytes 17039360 | tf_op jit(solution)/shard_map/all_gather | solution.py:22
  50.7 8.0 %copy-start.13 = (f32[2,1,16]{2,1,0:T(1,128)}, f32[2,1,16]{2,1,0:T(1,128)S(1)}, u32[]{:S(2)}) copy-start(f32[2,1,16]{2,1,0:T(1,128)S(1)} %get-tuple-element.187) | copy-start | bytes 388
  50.7 8.0 %collective-permute-start.2 = (bf16[3,128]{1,0:T(4,128)(2,1)S(1)}, bf16[3,128]{1,0:T(4,128)(2,1)S(1)}, u32[]{:S(2)}, u32[]{:S(2)}) collective-permute-start(bf16[3,128]{1,0:T(4,128)(2,1)S(1)} %slice.127), channel_id=1, source_target_pairs={{0,8},{8,16},{16,24},{24,32},{32,40},{40,48},{48,56},{56,64},{64,7... | collective-permute-start | bytes 2312 | tf_op jit(solution)/shard_map/ppermute | solution.py:16
  62.3 9.5 %collective-permute-start = (bf16[3,1024]{1,0:T(4,128)(2,1)S(1)}, bf16[3,1024]{1,0:T(4,128)(2,1)S(1)}, u32[]{:S(2)}, u32[]{:S(2)}) collective-permute-start(bf16[3,1024]{1,0:T(4,128)(2,1)S(1)} %slice.113), channel_id=1, source_target_pairs={{0,8},{8,16},{16,24},{24,32},{32,40},{40,48},{48,56},{56,64},{64,7... | collective-permute-start | bytes 18440 | tf_op jit(solution)/shard_map/ppermute | solution.py:16
  73.0 0.8 copy-start.3
  74.0 7.4 %copy-start.19 = (bf16[4,128]{1,0:T(4,128)(2,1)S(1)}, bf16[4,128]{1,0:T(4,128)(2,1)}, u32[]{:S(2)}) copy-start(bf16[4,128]{1,0:T(4,128)(2,1)} %param.23) | copy-start | bytes 3076
  75.8 152.7 %copy-start.5 = (f32[2,16,64,128]{3,2,1,0:T(8,128)}, f32[2,16,64,128]{3,2,1,0:T(8,128)S(1)}, u32[]{:S(2)}) copy-start(f32[2,16,64,128]{3,2,1,0:T(8,128)S(1)} %get-tuple-element.127) | copy-start | bytes 3145732
  75.8 20.2 %copy-start.14 = (f32[2,16]{1,0:T(2,128)S(1)}, f32[2,16]{1,0:T(2,128)}, u32[]{:S(2)}) copy-start(f32[2,16]{1,0:T(2,128)} %get-tuple-element.318) | copy-start | bytes 388
  75.8 20.2 %copy-start.20 = (bf16[16]{0:T(256)(128)(2,1)S(1)}, bf16[16]{0:T(256)(128)(2,1)}, u32[]{:S(2)}) copy-start(bf16[16]{0:T(256)(128)(2,1)} %get-tuple-element.186) | copy-start | bytes 100
  75.8 151.1 %copy-start.11 = (f32[2,128,16]{2,1,0:T(8,128)S(1)}, f32[2,128,16]{2,1,0:T(8,128)}, u32[]{:S(2)}) copy-start(f32[2,128,16]{2,1,0:T(8,128)} %get-tuple-element.188) | copy-start | bytes 49156
  78.1 10.5 %all-to-all-start.3 = ((bf16[32,8,128]{2,0,1:T(8,128)(2,1)}), bf16[32,8,128]{2,0,1:T(8,128)(2,1)S(1)}, u32[]{:S(2)}, u32[]{:S(2)}) async-start(bf16[32,8,128]{2,0,1:T(8,128)(2,1)} %copy_bitcast_fusion.3), calls=%async_computation.3 | async-start | bytes 131072 | tf_op jit(solution)/shard_map/all_to_all | solution.py:79
  88.6 140.1 %all-to-all-start.5 = ((bf16[32,8,1024]{2,0,1:T(8,128)(2,1)}), bf16[32,8,1024]{2,0,1:T(8,128)(2,1)S(1)}, u32[]{:S(2)}, u32[]{:S(2)}) async-start(bf16[32,8,1024]{2,0,1:T(8,128)(2,1)} %bitcast.122), calls=%async_computation.5 | async-start | bytes 1048576 | tf_op jit(solution)/shard_map/all_to_all | solution.py:77
  96.9 131.5 %collective-permute-start.1 = (bf16[3,128]{1,0:T(4,128)(2,1)S(1)}, bf16[3,128]{1,0:T(4,128)(2,1)S(1)}, u32[]{:S(2)}, u32[]{:S(2)}) collective-permute-start(bf16[3,128]{1,0:T(4,128)(2,1)S(1)} %slice.122), channel_id=1, source_target_pairs={{0,8},{8,16},{16,24},{24,32},{32,40},{40,48},{48,56},{56,64},{64,7... | collective-permute-start | bytes 2312 | tf_op jit(solution)/shard_map/ppermute | solution.py:16
  228.5 0.6 copy-start.9
  229.1 0.8 copy-start.1
  236.8 115.0 %copy-start.6 = (f32[2,16,64,128]{3,2,1,0:T(8,128)S(1)}, f32[2,16,64,128]{3,2,1,0:T(8,128)}, u32[]{:S(2)}) copy-start(f32[2,16,64,128]{3,2,1,0:T(8,128)} %copy-done.5) | copy-start | bytes 3145732
  236.8 115.0 %copy-start.10 = (bf16[256,128]{1,0:T(8,128)(2,1)S(1)}, bf16[256,128]{1,0:T(8,128)(2,1)}, u32[]{:S(2)}) copy-start(bf16[256,128]{1,0:T(8,128)(2,1)} %copy-done.9) | copy-start | bytes 196612
  236.8 115.1 %copy-start.18 = (f32[2,16]{1,0:T(2,128)S(1)}, f32[2,16]{1,0:T(2,128)}, u32[]{:S(2)}) copy-start(f32[2,16]{1,0:T(2,128)} %subtract_exponential_fusion) | copy-start | bytes 388
  351.8 1.0 copy-start.4
  351.8 1.4 copy-start.7
  351.8 1.7 copy-start.8
  351.8 1.7 copy-start.15
  351.8 1.7 copy-start.16
  351.8 1.7 copy-start.17
  351.8 1.7 copy-start.21
  357.7 1.6 copy-start.2
  357.8 1.6 copy-start.12
Sparse Core Ops, SparseCore 0:
  76.7 103.5 all-gather.3
where the time goes:
time: 395 us; the launch traced here: 390 us
  blocking collectives  145 us (37%)
  other arithmetic  124 us (31%)
  starting transfers between devices  49.4 us (13%)
  local copies, waits for them, and re-layouts  28.4 us (7%)
  waiting for transfers between devices  24.1 us (6%)
  between operations  14.5 us (4%)
    unnamed x1, blocking collectives  124 us
    select_n x64, other arithmetic, step(): return jax.tree.map(lambda a, b: jnp.where(reached, a, b), new, before)  69.9 us
    exp x64, other arithmetic, chain_combine(): jnp.exp(later[0])[:, None, None] * earlier[1] + later[1]  43.9 us
    all_to_all x1, blocking collectives, shards(): lax.all_to_all(normed, 'head', split_axis=0, concat_axis=1, tiled=True)  21.4 us
    ppermute x3, starting transfers between devices, shifted(): return lax.ppermute(x, axis, pairs)  21.3 us
    all_to_all x1, starting transfers between devices, shards(): lax.all_to_all(decay_stream, 'head', split_axis=1, concat_axis=0, tiled=T...  10.9 us
  transfers between devices with their start and end apart: 10, of which 6 were waited for; matrix products, arithmetic and copies ran while one was open for 6% of the time, Pallas kernels for 0%

commit v1 on v0

v1 whole, which is shorter than its diff:
```python
import functools

import jax
import jax.numpy as jnp
from jax import lax
from jax.experimental import pallas as pl
from jax.experimental.pallas import tpu as pltpu
from jax.sharding import Mesh
from jax.sharding import PartitionSpec as P

HEADS = 128
HEAD_DIM = 64
STATE = 128
GROUPS = 8
SPAN = 128
CORES = 2
RING = 8
PEERS = CORES * RING
ROWS = 32
TOKENS = PEERS * ROWS
SPANS = TOKENS // SPAN
FROM = SPAN // ROWS
MINE = HEADS // PEERS
WIDE = MINE * HEAD_DIM
TILES = WIDE // 128
RUNS = 32
PACK = ROWS * (TILES + 2) + 2 * MINE
CUT = STATE * TILES // RUNS
F32 = jnp.float32
BF16 = jnp.bfloat16
VMEM_LIMIT = 24 * 1024 * 1024


def call(body, outs, flops, moved, scratch=()):
    return pl.pallas_call(
        body,
        out_shape=outs,
        scratch_shapes=list(scratch),
        compiler_params=pltpu.CompilerParams(vmem_limit_bytes=VMEM_LIMIT),
        cost_estimate=pl.CostEstimate(flops=flops, bytes_accessed=moved, transcendentals=0),
    )


def like(shape, dtype):
    return jax.ShapeDtypeStruct(shape, dtype)


def silu(x):
    return x / (1.0 + jnp.exp(-x))


def pack_kernel(x_ref, b_ref, c_ref, dt_ref, decay_ref, out_ref):
    steps = jnp.transpose(dt_ref[...].astype(F32))
    decays = jnp.transpose(decay_ref[...].astype(F32))
    for core in range(CORES):
        for ring in range(RING):
            peer = core * RING + ring
            for tile in range(TILES):
                column = ring * CORES * WIDE + core * WIDE + tile * 128
                out_ref[peer, tile * ROWS : (tile + 1) * ROWS, :] = x_ref[:, column : column + 128]
            at = TILES * ROWS
            out_ref[peer, at : at + ROWS, :] = b_ref[:, ring * 128 : (ring + 1) * 128]
            out_ref[peer, at + ROWS : at + 2 * ROWS, :] = c_ref[:, ring * 128 : (ring + 1) * 128]
            head = (ring * CORES + core) * MINE
            both = jnp.concatenate([steps[head : head + MINE], decays[head : head + MINE]], 0)
            both = jnp.concatenate([both, jnp.zeros((2 * MINE, 128 - ROWS), F32)], 1)
            out_ref[peer, at + 2 * ROWS :, :] = both.astype(BF16)


def raw(r_ref, span, tile):
    return r_ref[span * FROM : (span + 1) * FROM, tile * ROWS : (tile + 1) * ROWS, :].reshape(SPAN, 128)


def conv_silu(r_ref, halo_ref, taps_ref, pad_ref, span, tile):
    lanes = slice(tile * 128, (tile + 1) * 128)
    if span == 0:
        pad_ref[0:8, :] = halo_ref[tile].astype(F32)
    else:
        pad_ref[0:8, :] = r_ref[span * FROM - 1, (tile + 1) * ROWS - 16 : (tile + 1) * ROWS, :].astype(F32)[8:16]
    pad_ref[8 : 8 + SPAN, :] = raw(r_ref, span, tile).astype(F32)
    total = pad_ref[5 : 5 + SPAN, :] * taps_ref[0:1, lanes]
    for tap in range(1, 4):
        total = total + pad_ref[5 + tap : 5 + tap + SPAN, :] * taps_ref[tap : tap + 1, lanes]
    return silu(total).astype(BF16)


def decays_of(r_ref, span):
    at = (TILES + 2) * ROWS
    both = jnp.concatenate([r_ref[span * FROM + m, at : at + 2 * MINE, 0:ROWS] for m in range(FROM)], 1)
    both = both.astype(F32)
    steps, decays = both[0:MINE], both[MINE : 2 * MINE]
    row = lax.broadcasted_iota(jnp.int32, (SPAN, SPAN), 0)
    column = lax.broadcasted_iota(jnp.int32, (SPAN, SPAN), 1)
    lower = (row >= column).astype(F32).astype(BF16)
    same = (row == column).astype(F32).astype(BF16)
    upper = (row <= column).astype(F32).astype(BF16)
    last = (((1,), (1,)), ((), ()))
    running = lax.dot_general(lower, decays.astype(BF16), last, preferred_element_type=F32)
    steps_column = lax.dot_general(same, steps.astype(BF16), last, preferred_element_type=F32)
    running_row = jnp.dot(decays.astype(BF16), upper, preferred_element_type=F32)
    return running, steps_column, running_row, steps


def spread(per_head, tile):
    low = lax.broadcasted_iota(jnp.int32, (per_head.shape[0], 128), 1) < HEAD_DIM
    return jnp.where(low, per_head[:, 2 * tile : 2 * tile + 1], per_head[:, 2 * tile + 1 : 2 * tile + 2])


def span_state(r_ref, halo_ref, taps_ref, pad_ref, span):
    running, steps, _, _ = decays_of(r_ref, span)
    tail = jnp.exp(running[SPAN - 1 : SPAN] - running) * steps
    b_conv = conv_silu(r_ref, halo_ref, taps_ref, pad_ref, span, TILES)
    parts, weighted = [], []
    for tile in range(TILES):
        part = conv_silu(r_ref, halo_ref, taps_ref, pad_ref, span, tile)
        parts.append(part)
        weighted.append((part.astype(F32) * spread(tail, tile)).astype(BF16))
    fresh = jnp.dot(
        jnp.transpose(b_conv.astype(F32)).astype(BF16),
        jnp.concatenate(weighted, 1),
        preferred_element_type=F32,
    )
    return jnp.concatenate(parts, 1), b_conv, fresh


def later_kernel(r_ref, taps_ref, x_ref, b_ref, fresh_ref, pad_ref):
    for span in range(1, SPANS):
        x_conv, b_conv, fresh = span_state(r_ref, None, taps_ref, pad_ref, span)
        x_ref[span - 1] = x_conv
        b_ref[span - 1] = b_conv
        fresh_ref[span - 1] = fresh


def first_kernel(r_ref, halo_ref, taps_ref, fresh_ref, x_ref, b_ref, own_ref, message_ref, pad_ref):
    x_conv, b_conv, state = span_state(r_ref, halo_ref, taps_ref, pad_ref, 0)
    x_ref[...] = x_conv
    b_ref[...] = b_conv
    own_ref[...] = state
    totals = [decays_of(r_ref, span)[0][SPAN - 1 : SPAN] for span in range(SPANS)]
    factor = jnp.exp(sum(totals[1:], totals[0]))
    for tile in range(TILES):
        lanes = slice(tile * 128, (tile + 1) * 128)
        here = state[:, lanes]
        for span in range(1, SPANS):
            here = here * spread(jnp.exp(totals[span]), tile) + fresh_ref[span - 1, :, lanes]
        scale = spread(factor, tile)
        coarse = scale.astype(BF16).astype(F32)
        tail = jnp.concatenate([coarse, scale - coarse, jnp.zeros((6, 128), F32)], 0)
        for cut in range(STATE // CUT):
            whole = jnp.concatenate([here[cut * CUT : (cut + 1) * CUT], tail], 0)
            message_ref[tile * (STATE // CUT) + cut] = whole.astype(BF16)


def local_kernel(
    r_ref, halo_ref, taps_ref, x0_ref, b0_ref, fresh0_ref, x_ref, b_ref, fresh_ref, part_ref, c_ref, scale_ref, pad_ref
):
    row = lax.broadcasted_iota(jnp.int32, (SPAN, SPAN), 0)
    column = lax.broadcasted_iota(jnp.int32, (SPAN, SPAN), 1)
    causal = row >= column
    low = lax.broadcasted_iota(jnp.int32, (SPAN, 128), 1) < HEAD_DIM
    before = jnp.zeros((1, MINE), F32)
    state = None
    for span in range(SPANS):
        running, _, running_row, steps_row = decays_of(r_ref, span)
        c_conv = conv_silu(r_ref, halo_ref, taps_ref, pad_ref, span, TILES + 1)
        c_ref[span] = c_conv
        x_conv = x0_ref[...] if span == 0 else x_ref[span - 1]
        b_conv = b0_ref[...] if span == 0 else b_ref[span - 1]
        scores = lax.dot_general(c_conv, b_conv, (((1,), (1,)), ((), ())), preferred_element_type=F32)
        grown = jnp.exp(running)
        scale_ref[span] = jnp.exp(running + before)
        for tile in range(TILES):
            lanes = slice(tile * 128, (tile + 1) * 128)
            pair = []
            for head in (2 * tile, 2 * tile + 1):
                gap = running[:, head : head + 1] - running_row[head : head + 1, :]
                decay = jnp.exp(jnp.where(causal, gap, -1e30)) * steps_row[head : head + 1, :]
                pair.append((decay * scores).astype(BF16))
            values = x_conv[:, lanes]
            both = jnp.dot(jnp.concatenate(pair, 0), values, preferred_element_type=F32)
            out = jnp.where(low, both[:SPAN], both[SPAN:])
            out = out + values.astype(F32) * taps_ref[4:5, lanes]
            if span:
                inter = jnp.dot(c_conv, state[:, lanes].astype(BF16), preferred_element_type=F32)
                out = out + inter * spread(grown, tile)
            part_ref[span, :, lanes] = out
        total = running[SPAN - 1 : SPAN]
        before = before + total
        if span == 0:
            state = fresh0_ref[...]
        elif span < SPANS - 1:
            factor = jnp.exp(total)
            kept = [state[:, t * 128 : (t + 1) * 128] * spread(factor, t) for t in range(TILES)]
            state = jnp.concatenate(kept, 1) + fresh_ref[span - 1]


def chain_kernel(all_ref, out_ref):
    state = jnp.zeros((CUT, 128), F32)
    for run in range(RUNS):
        out_ref[run] = state.astype(BF16)
        if run < RUNS - 1:
            here = all_ref[run].astype(F32)
            state = state * (here[CUT : CUT + 1] + here[CUT + 1 : CUT + 2]) + here[:CUT]


def finish_kernel(part_ref, c_ref, scale_ref, state_ref, out_ref):
    for span in range(SPANS):
        scale = scale_ref[span]
        for tile in range(TILES):
            lanes = slice(tile * 128, (tile + 1) * 128)
            inter = jnp.dot(c_ref[span], state_ref[tile], preferred_element_type=F32)
            out = part_ref[span, :, lanes] + inter * spread(scale, tile)
            out_ref[span * SPAN : (span + 1) * SPAN, lanes] = out.astype(BF16)


def norm_kernel(values_ref, z_ref, gain_ref, out_ref):
    for group in range(GROUPS):
        gated, square = [], None
        for core in range(CORES):
            lanes = slice((group * CORES + core) * WIDE, (group * CORES + core + 1) * WIDE)
            here = values_ref[core * RING + group].astype(F32) * silu(z_ref[:, lanes].astype(F32))
            gated.append((lanes, here))
            summed = jnp.sum(here * here, axis=1, keepdims=True)
            square = summed if square is None else square + summed
        scale = lax.rsqrt(square * (1.0 / (CORES * WIDE)) + 1e-05)
        for lanes, here in gated:
            out_ref[:, lanes] = (here * scale * gain_ref[:, lanes].astype(F32)).astype(BF16)


def shards(
    x_stream,
    z_stream,
    b_stream,
    c_stream,
    dt_stream,
    decay_stream,
    kernel_x,
    kernel_b,
    kernel_c,
    skip_gain,
    norm_gain,
):
    core = lax.axis_index("core")
    packed = call(pack_kernel, like((PEERS, PACK, 128), BF16), 0, 2 * PEERS * PACK * 256)(
        x_stream, b_stream, c_stream, dt_stream, decay_stream
    )
    got = lax.all_to_all(packed, ("core", "head"), split_axis=0, concat_axis=0, tiled=True)
    edge = got[PEERS - 1, : ROWS * (TILES + 2)].reshape(TILES + 2, ROWS, 128)[:, ROWS - 8 :]
    halo = lax.ppermute(edge, "seq", [(i, i + 1) for i in range(RUNS - 1)])
    taps_x = lax.dynamic_slice_in_dim(kernel_x, core * WIDE, WIDE, 1)
    skip = jnp.repeat(lax.dynamic_slice_in_dim(skip_gain, core * MINE, MINE), HEAD_DIM)
    taps = jnp.concatenate([taps_x, kernel_b, kernel_c], 1).astype(F32)
    skip_row = jnp.pad(skip, (0, 2 * STATE))[None]
    taps = jnp.concatenate([taps, skip_row, jnp.zeros((3, WIDE + 2 * STATE), F32)], 0)
    pad = pltpu.VMEM((SPAN + 8, 128), F32)
    x_later, b_later, fresh_later = call(
        later_kernel,
        (
            like((SPANS - 1, SPAN, WIDE), BF16),
            like((SPANS - 1, SPAN, STATE), BF16),
            like((SPANS - 1, STATE, WIDE), F32),
        ),
        10**9,
        4 * 10**6,
        [pad],
    )(got, taps)
    x_first, b_first, fresh_first, message = call(
        first_kernel,
        (
            like((SPAN, WIDE), BF16),
            like((SPAN, STATE), BF16),
            like((STATE, WIDE), F32),
            like((RUNS, CUT + 8, 128), BF16),
        ),
        10**9,
        4 * 10**6,
        [pad],
    )(got, halo, taps, fresh_later)
    slices = lax.all_to_all(message, "seq", split_axis=0, concat_axis=0, tiled=True)
    part, c_conv, scale = call(
        local_kernel,
        (
            like((SPANS, SPAN, WIDE), F32),
            like((SPANS, SPAN, STATE), BF16),
            like((SPANS, SPAN, MINE), F32),
        ),
        10**9,
        8 * 10**6,
        [pad],
    )(got, halo, taps, x_first, b_first, fresh_first, x_later, b_later, fresh_later)
    chained = call(chain_kernel, like((RUNS, CUT, 128), BF16), 10**7, 10**6)(slices)
    state = lax.all_to_all(chained, "seq", split_axis=0, concat_axis=0, tiled=True)
    values = call(finish_kernel, like((TOKENS, WIDE), BF16), 10**8, 3 * 10**6)(
        part, c_conv, scale, state.reshape(TILES, STATE, 128)
    )
    home = lax.all_to_all(
        values.reshape(PEERS, ROWS, WIDE), ("core", "head"), split_axis=0, concat_axis=0, tiled=True
    )
    return call(norm_kernel, like((ROWS, HEADS * HEAD_DIM), BF16), 10**7, 2 * 10**6)(
        home, z_stream, norm_gain.reshape(1, HEADS * HEAD_DIM)
    )


def solution(mesh):
    finer = Mesh(mesh.devices.reshape(RUNS, CORES, RING), ("seq", "core", "head"))
    rows = P(("seq", "core", "head"), None)
    in_specs = (rows,) * 6 + (P(None, "head"),) * 3 + (P("head"), P())
    return jax.shard_map(shards, mesh=finer, in_specs=in_specs, out_specs=rows, check_vma=False)
```

time: 395 us -> 106 us (0.27); the launches traced: 390 us -> 105 us
  blocking collectives: 145 us -> 19 us
  other arithmetic: 124 us -> 0.08 us
  starting transfers between devices: 49.4 us -> 27.8 us
  local copies, waits for them, and re-layouts: 28.4 us -> 9.25 us
  waiting for transfers between devices: 24.1 us -> 39.7 us
  between operations: 14.5 us -> 0.11 us
  Pallas kernels: 0 us -> 9.36 us
    unnamed x1 -> x0, blocking collectives: 124 us -> none
    select_n x64 -> x0, other arithmetic: 69.9 us -> none  [step(): return jax.tree.map(lambda a, b: jnp.where(reached, a, b), new, before)]
    exp x66 -> x0, other arithmetic: 45.1 us -> none  [the longest x64 43.9 us: chain_combine(): jnp.exp(later[0])[:, None, None] * earlier[1] + later[1]]
    ppermute x3 -> x1, starting transfers between devices: 21.3 us -> 3.2 us  [shards(): halo = lax.ppermute(edge, 'seq', [(i, i + 1) for i in range(RUNS - 1)])]
    all_to_all x6 -> x3, waiting for transfers between devices: 23.4 us -> 39.7 us  [the longest x1 20.8 us: shards(): lax.all_to_all(packed, ('core', 'head'), split_axis=0, concat_axis=0, til...]
    convert_element_type x9 -> x0, local copies, waits for them, and re-layouts: 9.85 us -> none  [the longest x2 3.69 us: gated_norm(): values.astype(jnp.float32) * jax.nn.silu(gate_in.astype(jnp.float32))]
    pallas_call x0 -> x7, Pallas kernels: none -> 9.36 us  [the longest x1 2.21 us: shards(): call(local_kernel, (like((SPANS, SPAN, WIDE), F32), like((SPANS, SPAN, ST...]
    convert_element_type x15 -> x1, other arithmetic: 6.94 us -> 0.01 us  [shards(): taps = jnp.concatenate([taps_x, kernel_b, kernel_c], 1).astype(F32)]
  transfers between devices with their start and end apart: 10 -> 4, of which waited for: 6 -> 3; matrix products, arithmetic and copies ran while one was open for 6% -> 0% of each run, Pallas kernels for 0% -> 4%
where the time goes in v1:
time: 106 us; the launch traced here: 105 us
  waiting for transfers between devices  39.7 us (37%)
  starting transfers between devices  27.8 us (26%)
  blocking collectives  19 us (18%)
  Pallas kernels  9.36 us (9%)
  local copies, waits for them, and re-layouts  9.25 us (9%)
    all_to_all x1, waiting for transfers between devices, shards(): lax.all_to_all(packed, ('core', 'head'), split_axis=0, concat_axis=0, til...  20.8 us
    all_to_all x1, blocking collectives, shards(): lax.all_to_all(message, 'seq', split_axis=0, concat_axis=0, tiled=True)  19 us
    all_to_all x1, waiting for transfers between devices, shards(): lax.all_to_all(values.reshape(PEERS, ROWS, WIDE), ('core', 'head'), split...  14.7 us
    all_to_all x1, starting transfers between devices, shards(): lax.all_to_all(packed, ('core', 'head'), split_axis=0, concat_axis=0, til...  11.8 us
    unnamed x34, local copies, waits for them, and re-layouts  8.9 us
    all_to_all x1, starting transfers between devices, shards(): lax.all_to_all(values.reshape(PEERS, ROWS, WIDE), ('core', 'head'), split...  7.35 us
    all_to_all x1, starting transfers between devices, shards(): lax.all_to_all(chained, 'seq', split_axis=0, concat_axis=0, tiled=True)  5.46 us
    all_to_all x1, waiting for transfers between devices, shards(): lax.all_to_all(chained, 'seq', split_axis=0, concat_axis=0, tiled=True)  4.15 us
  transfers between devices with their start and end apart: 4, of which 3 were waited for; matrix products, arithmetic and copies ran while one was open for 0% of the time, Pallas kernels for 4%

profile of v1, /device:TPU:1, one launch (start us, length us, event | category | flops | bytes accessed | tf_op | source)
XLA Modules:
  0.0 105.4 jit_solution(17350357032147866930)
XLA Ops:
  0.0 0.0 copy-start
  0.0 0.0 copy-start.1
  0.0 1.1 copy-done.1
  1.1 0.0 copy-start.3
  1.1 0.8 copy-done.3
  1.9 0.0 copy-start.4
  1.9 0.8 copy-done.4
  2.7 0.0 copy-start.5
  2.7 0.7 copy-done.5
  3.4 0.0 copy-start.6
  3.4 0.7 copy-done.6
  4.1 1.1 %shard_map.109 = bf16[16,208,128]{2,1,0:T(8,128)(2,1)} custom-call(bf16[32,8192]{1,0:T(8,128)(2,1)S(1)} %copy-done.1, bf16[32,1024]{1,0:T(8,128)(2,1)S(1)} %copy-done.3, bf16[32,1024]{1,0:T(8,128)(2,1)S(1)} %copy-done.4, bf16[32,128]{1,0:T(8,128)(2,1)S(1)} %copy-done.5, bf16[32,128]{1,0:T(8,128)(2,1)S(1)} %copy-done.6), custom_call_target="tpu_custom_call" | custom-call | bytes 1703936 | tf_op jit(solution)/shard_map/pallas_call | solution.py:244
  5.2 11.8 %all-to-all-start = ((bf16[16,208,128]{2,1,0:T(8,128)(2,1)}), bf16[16,208,128]{2,1,0:T(8,128)(2,1)S(1)}, u32[]{:S(2)}, u32[]{:S(2)}) async-start(bf16[16,208,128]{2,1,0:T(8,128)(2,1)} %shard_map.109), calls=%async_computation | async-start | bytes 1703936 | tf_op jit(solution)/shard_map/all_to_all | solution.py:247
  17.0 0.0 copy-start.16
  17.0 0.6 copy-done.16
  17.7 0.1 dynamic_slice.7
  17.8 0.1 broadcast_in_dim.9
  17.8 0.1 reshape.12
  17.9 0.1 pad.7.clone
  18.0 0.0 copy-done
  18.0 0.0 copy-start.14
  18.0 0.0 copy-start.15
  18.0 0.7 copy-done.14
  18.7 0.0 copy-done.15
  18.7 0.1 maximum_maximum_fusion.taps_ref
  18.8 20.8 %all-to-all-done.r_ref = bf16[16,208,128]{2,1,0:T(8,128)(2,1)S(1)} async-done(((bf16[16,208,128]{2,1,0:T(8,128)(2,1)}), bf16[16,208,128]{2,1,0:T(8,128)(2,1)S(1)}, u32[]{:S(2)}, u32[]{:S(2)}) %all-to-all-start) | async-done | bytes 852000 | tf_op jit(solution)/shard_map/all_to_all | solution.py:247
  39.6 3.2 %collective-permute-start = (bf16[6,8,128]{2,1,0:T(8,128)(2,1)S(1)}, bf16[6,8,128]{2,1,0:T(8,128)(2,1)S(1)}, u32[]{:S(2)}, u32[]{:S(2)}) collective-permute-start(bf16[6,8,128]{2,1,0:T(8,128)(2,1)S(1)} %slice.9), channel_id=1, source_target_pairs={{0,16},{16,32},{32,48},{48,64},{64,80},{80,96},{96,112},{112,128},... | collective-permute-start | bytes 36872 | tf_op jit(solution)/shard_map/ppermute | solution.py:249
  42.8 1.6 %shard_map.110 = (bf16[3,128,512]{2,1,0:T(8,128)(2,1)S(1)}, bf16[3,128,128]{2,1,0:T(8,128)(2,1)S(1)}, f32[3,128,512]{2,1,0:T(8,128)S(1)}) custom-call(bf16[16,208,128]{2,1,0:T(8,128)(2,1)S(1)} %all-to-all-done.r_ref, f32[8,768]{1,0:T(8,128)S(1)} %maximum_maximum_fusion.taps_ref), custom_call_target="tpu_custom_call" | custom-call | flops 1000000000 | bytes 4000000 | tf_op jit(solution)/shard_map/pallas_call | solution.py:256
  44.5 0.0 copy-start.11
  44.5 0.6 copy-done.11
  45.1 0.0 copy-start.7
  45.1 0.0 collective-permute-done.halo_ref
  45.1 0.9 shard_map.111
  46.0 0.0 copy-done.7
  46.0 0.0 copy-start.9
  46.0 19.0 %all_to_all.20.all_ref = bf16[32,24,128]{2,1,0:T(8,128)(2,1)S(1)} all-to-all(bf16[32,24,128]{2,1,0:T(8,128)(2,1)S(1)} %get-tuple-element.24), channel_id=1, replica_groups=mesh['seq'=32,'core'=2,'head'=8] {'seq'}, dimensions={0} | all-to-all | bytes 393216 | tf_op jit(solution)/shard_map/all_to_all | solution.py:279
  65.1 0.0 copy-done.9
  65.1 0.7 shard_map.113
  65.8 5.5 %all-to-all-start.2 = ((bf16[32,16,128]{2,1,0:T(8,128)(2,1)}), bf16[32,16,128]{2,1,0:T(8,128)(2,1)S(1)}, u32[]{:S(2)}, u32[]{:S(2)}) async-start(bf16[32,16,128]{2,1,0:T(8,128)(2,1)} %shard_map.113), calls=%async_computation.2 | async-start | bytes 262144 | tf_op jit(solution)/shard_map/all_to_all | solution.py:292
  71.2 0.0 copy-start.8
  71.3 1.0 copy-done.8
  72.2 0.0 copy-start.10
  72.2 0.9 copy-done.10
  73.1 0.0 copy-start.12
  73.2 0.9 copy-done.12
  74.0 2.2 %shard_map.112 = (f32[4,128,512]{2,1,0:T(8,128)S(1)}, bf16[4,128,128]{2,1,0:T(8,128)(2,1)S(1)}, f32[4,128,8]{2,1,0:T(8,128)S(1)}) custom-call(bf16[16,208,128]{2,1,0:T(8,128)(2,1)S(1)} %all-to-all-done.r_ref, bf16[6,8,128]{2,1,0:T(8,128)(2,1)S(1)} %collective-permute-done.halo_ref, f32[8,768]{1,0:T(8,128)S(1)} %maximum_maximum_fusion.taps_ref, ...), custom_call_target="tpu_custom_call" | custom-call | flops 1000000000 | bytes 8000000 | tf_op jit(solution)/shard_map/pallas_call | solution.py:280
  76.2 4.1 %all-to-all-done.2 = bf16[32,16,128]{2,1,0:T(8,128)(2,1)S(1)} async-done(((bf16[32,16,128]{2,1,0:T(8,128)(2,1)}), bf16[32,16,128]{2,1,0:T(8,128)(2,1)S(1)}, u32[]{:S(2)}, u32[]{:S(2)}) %all-to-all-start.2) | async-done | bytes 131104 | tf_op jit(solution)/shard_map/all_to_all | solution.py:292
  80.4 1.5 %shard_map.114 = bf16[512,512]{1,0:T(8,128)(2,1)} custom-call(f32[4,128,512]{2,1,0:T(8,128)S(1)} %get-tuple-element.21.part_ref, bf16[4,128,128]{2,1,0:T(8,128)(2,1)S(1)} %get-tuple-element.22.c_ref, f32[4,128,8]{2,1,0:T(8,128)S(1)} %get-tuple-element.23.scale_ref, bf16[4,128,128]{2,1,0:T(8,128)(2,1)S(1)} %bitcast.3), custom_call_target="tpu_custom_call" | custom-call | flops 100000000 | bytes 3000000 | tf_op jit(solution)/shard_map/pallas_call | solution.py:293
  81.9 0.0 copy-start.13
  81.9 0.0 copy-start.2
  81.9 7.4 %all-to-all-start.3 = ((bf16[16,32,512]{2,1,0:T(8,128)(2,1)}), bf16[16,32,512]{2,1,0:T(8,128)(2,1)S(1)}, u32[]{:S(2)}, u32[]{:S(2)}) async-start(bf16[16,32,512]{2,1,0:T(8,128)(2,1)} %bitcast.2), calls=%async_computation.3 | async-start | bytes 1048576 | tf_op jit(solution)/shard_map/all_to_all | solution.py:296
  89.3 0.0 copy-done.13
  89.3 14.7 %all-to-all-done.3.values_ref = bf16[16,32,512]{2,1,0:T(8,128)(2,1)S(1)} async-done(((bf16[16,32,512]{2,1,0:T(8,128)(2,1)}), bf16[16,32,512]{2,1,0:T(8,128)(2,1)S(1)}, u32[]{:S(2)}, u32[]{:S(2)}) %all-to-all-start.3) | async-done | bytes 524320 | tf_op jit(solution)/shard_map/all_to_all | solution.py:296
  104.1 0.0 copy-done.2
  104.1 1.3 %shard_map.115 = bf16[32,8192]{1,0:T(8,128)(2,1)} custom-call(bf16[16,32,512]{2,1,0:T(8,128)(2,1)S(1)} %all-to-all-done.3.values_ref, bf16[32,8192]{1,0:T(8,128)(2,1)S(1)} %copy-done.2, bf16[1,8192]{1,0:T(2,128)(2,1)S(1)} %reshape.15.gain_ref), custom_call_target="tpu_custom_call" | custom-call | flops 10000000 | bytes 2000000 | tf_op jit(solution)/shard_map/pallas_call | solution.py:299
  (8 shorter events, 0.1 us)
Async XLA Ops:
  0.0 18.0 %copy-start = (bf16[4,1024]{1,0:T(4,128)(2,1)S(1)}, bf16[4,1024]{1,0:T(4,128)(2,1)}, u32[]{:S(2)}) copy-start(bf16[4,1024]{1,0:T(4,128)(2,1)} %param.17) | copy-start | bytes 24580
  0.0 1.1 %copy-start.1 = (bf16[32,8192]{1,0:T(8,128)(2,1)S(1)}, bf16[32,8192]{1,0:T(8,128)(2,1)}, u32[]{:S(2)}) copy-start(bf16[32,8192]{1,0:T(8,128)(2,1)} %x_ref.1) | copy-start | bytes 1572868
  1.1 0.8 copy-start.3
  1.9 0.8 copy-start.4
  2.7 0.7 copy-start.5
  3.4 0.7 copy-start.6
  5.2 34.4 %all-to-all-start = ((bf16[16,208,128]{2,1,0:T(8,128)(2,1)}), bf16[16,208,128]{2,1,0:T(8,128)(2,1)S(1)}, u32[]{:S(2)}, u32[]{:S(2)}) async-start(bf16[16,208,128]{2,1,0:T(8,128)(2,1)} %shard_map.109), calls=%async_computation | async-start | bytes 1703936 | tf_op jit(solution)/shard_map/all_to_all | solution.py:247
  17.0 0.7 copy-start.16
  18.0 0.7 copy-start.14
  18.0 0.7 copy-start.15
  39.6 5.5 %collective-permute-start = (bf16[6,8,128]{2,1,0:T(8,128)(2,1)S(1)}, bf16[6,8,128]{2,1,0:T(8,128)(2,1)S(1)}, u32[]{:S(2)}, u32[]{:S(2)}) collective-permute-start(bf16[6,8,128]{2,1,0:T(8,128)(2,1)S(1)} %slice.9), channel_id=1, source_target_pairs={{0,16},{16,32},{32,48},{48,64},{64,80},{80,96},{96,112},{112,128},... | collective-permute-start | bytes 36872 | tf_op jit(solution)/shard_map/ppermute | solution.py:249
  44.5 0.6 copy-start.11
  45.1 0.9 copy-start.7
  46.0 19.0 %copy-start.9 = (bf16[128,512]{1,0:T(8,128)(2,1)}, bf16[128,512]{1,0:T(8,128)(2,1)S(1)}, u32[]{:S(2)}) copy-start(bf16[128,512]{1,0:T(8,128)(2,1)S(1)} %get-tuple-element.16.x0_ref) | copy-start | bytes 393220
  65.8 14.6 %all-to-all-start.2 = ((bf16[32,16,128]{2,1,0:T(8,128)(2,1)}), bf16[32,16,128]{2,1,0:T(8,128)(2,1)S(1)}, u32[]{:S(2)}, u32[]{:S(2)}) async-start(bf16[32,16,128]{2,1,0:T(8,128)(2,1)} %shard_map.113), calls=%async_computation.2 | async-start | bytes 262144 | tf_op jit(solution)/shard_map/all_to_all | solution.py:292
  71.2 1.0 copy-start.8
  72.2 0.9 copy-start.10
  73.1 0.9 copy-start.12
  81.9 7.4 %copy-start.13 = (bf16[8192]{0:T(1024)(128)(2,1)S(1)}, bf16[8192]{0:T(1024)(128)(2,1)}, u32[]{:S(2)}) copy-start(bf16[8192]{0:T(1024)(128)(2,1)} %param.21) | copy-start | bytes 49156
  81.9 22.1 %copy-start.2 = (bf16[32,8192]{1,0:T(8,128)(2,1)S(1)}, bf16[32,8192]{1,0:T(8,128)(2,1)}, u32[]{:S(2)}) copy-start(bf16[32,8192]{1,0:T(8,128)(2,1)} %z_ref.1) | copy-start | bytes 1572868
  81.9 22.1 %all-to-all-start.3 = ((bf16[16,32,512]{2,1,0:T(8,128)(2,1)}), bf16[16,32,512]{2,1,0:T(8,128)(2,1)S(1)}, u32[]{:S(2)}, u32[]{:S(2)}) async-start(bf16[16,32,512]{2,1,0:T(8,128)(2,1)} %bitcast.2), calls=%async_computation.3 | async-start | bytes 1048576 | tf_op jit(solution)/shard_map/all_to_all | solution.py:296

commit v2 on v1

v2 whole, which is shorter than its diff:
```python
import functools

import jax
import jax.numpy as jnp
from jax import lax
from jax.experimental import pallas as pl
from jax.experimental.pallas import tpu as pltpu
from jax.sharding import Mesh
from jax.sharding import PartitionSpec as P

HEADS = 128
HEAD_DIM = 64
STATE = 128
GROUPS = 8
SPAN = 128
CORES = 2
RING = 8
PEERS = CORES * RING
ROWS = 32
TOKENS = PEERS * ROWS
SPANS = TOKENS // SPAN
FROM = SPAN // ROWS
MINE = HEADS // PEERS
WIDE = MINE * HEAD_DIM
TILES = WIDE // 128
LEADERS = 4
MEMBERS = PEERS // LEADERS
RIM = 8 * (TILES + 2)
RUNS = 32
PACK = ROWS * (TILES + 2) + MINE
CUT = STATE * TILES // RUNS
F32 = jnp.float32
BF16 = jnp.bfloat16
MIB = 1024 * 1024


def call(body, outs, flops, moved, scratch=(), vmem=16, **specs):
    return pl.pallas_call(
        body,
        **specs,
        out_shape=outs,
        scratch_shapes=list(scratch),
        compiler_params=pltpu.CompilerParams(vmem_limit_bytes=vmem * MIB),
        cost_estimate=pl.CostEstimate(flops=flops, bytes_accessed=moved, transcendentals=0),
    )


def like(shape, dtype):
    return jax.ShapeDtypeStruct(shape, dtype)


def silu(x):
    return x / (1.0 + jnp.exp(-x))


def pack_kernel(x_hbm, b_hbm, c_hbm, dt_hbm, decay_hbm, out_ref, *rest):
    rims, (x_ref, b_ref, c_ref, dt_ref, decay_ref, arrived) = rest[:LEADERS], rest[LEADERS:]
    pairs = ((dt_hbm, dt_ref), (decay_hbm, decay_ref), (b_hbm, b_ref), (c_hbm, c_ref), (x_hbm, x_ref))
    copies = [pltpu.make_async_copy(a, b, arrived.at[i]) for i, (a, b) in enumerate(pairs)]
    for copy in copies:
        copy.start()
    copies[0].wait()
    copies[1].wait()
    steps = jnp.transpose(dt_ref[...].astype(F32))
    decays = jnp.transpose(decay_ref[...].astype(F32))
    at = TILES * ROWS
    for copy in copies[2:4]:
        copy.wait()
    for core in range(CORES):
        for ring in range(RING):
            peer = core * RING + ring
            out_ref[peer, at : at + ROWS, :] = b_ref[:, ring * 128 : (ring + 1) * 128]
            out_ref[peer, at + ROWS : at + 2 * ROWS, :] = c_ref[:, ring * 128 : (ring + 1) * 128]
            head = (ring * CORES + core) * MINE
            rest = jnp.zeros((MINE, 128 - 2 * ROWS), F32)
            both = jnp.concatenate([steps[head : head + MINE], decays[head : head + MINE], rest], 1)
            out_ref[peer, at + 2 * ROWS :, :] = both.astype(BF16)
    copies[4].wait()
    for core in range(CORES):
        for ring in range(RING):
            for tile in range(TILES):
                column = ring * CORES * WIDE + core * WIDE + tile * 128
                out_ref[core * RING + ring, tile * ROWS : (tile + 1) * ROWS, :] = x_ref[:, column : column + 128]
    for leader in range(LEADERS):
        for member in range(MEMBERS):
            core, ring = divmod(leader * MEMBERS + member, RING)
            column = (ring * CORES + core) * WIDE
            rows = slice(ROWS - 16, ROWS)
            pieces = [x_ref[rows, column + tile * 128 : column + (tile + 1) * 128] for tile in range(TILES)]
            pieces += [ref[rows, ring * 128 : (ring + 1) * 128] for ref in (b_ref, c_ref)]
            whole = jnp.concatenate([piece.astype(F32)[8:] for piece in pieces], 0)
            rims[leader][member] = whole.astype(BF16)


def raw(r_ref, span, tile):
    return r_ref[span * FROM : (span + 1) * FROM, tile * ROWS : (tile + 1) * ROWS, :].reshape(SPAN, 128)


def conv_silu(r_ref, rim_ref, taps_ref, pad_ref, span, tile):
    lanes = slice(tile * 128, (tile + 1) * 128)
    if span == 0:
        pad_ref[0:8, :] = rim_ref[tile * 8 : (tile + 1) * 8]
    else:
        pad_ref[0:8, :] = r_ref[span * FROM - 1, (tile + 1) * ROWS - 16 : (tile + 1) * ROWS, :].astype(F32)[8:16]
    pad_ref[8 : 8 + SPAN, :] = raw(r_ref, span, tile).astype(F32)
    total = pad_ref[5 : 5 + SPAN, :] * taps_ref[0:1, lanes]
    for tap in range(1, 4):
        total = total + pad_ref[5 + tap : 5 + tap + SPAN, :] * taps_ref[tap : tap + 1, lanes]
    return silu(total).astype(BF16)


def decays_of(r_ref, span):
    at = (TILES + 2) * ROWS
    parts = [r_ref[span * FROM + m, at : at + MINE, :].astype(F32) for m in range(FROM)]
    steps = jnp.concatenate([part[:, :ROWS] for part in parts], 1)
    decays = jnp.concatenate([part[:, ROWS : 2 * ROWS] for part in parts], 1)
    row = lax.broadcasted_iota(jnp.int32, (SPAN, SPAN), 0)
    column = lax.broadcasted_iota(jnp.int32, (SPAN, SPAN), 1)
    lower = (row >= column).astype(F32).astype(BF16)
    same = (row == column).astype(F32).astype(BF16)
    upper = (row <= column).astype(F32).astype(BF16)
    last = (((1,), (1,)), ((), ()))
    running = lax.dot_general(lower, decays.astype(BF16), last, preferred_element_type=F32)
    steps_column = lax.dot_general(same, steps.astype(BF16), last, preferred_element_type=F32)
    running_row = jnp.dot(decays.astype(BF16), upper, preferred_element_type=F32)
    return running, steps_column, running_row, steps


def spread(per_head, tile):
    low = lax.broadcasted_iota(jnp.int32, (per_head.shape[0], 128), 1) < HEAD_DIM
    return jnp.where(low, per_head[:, 2 * tile : 2 * tile + 1], per_head[:, 2 * tile + 1 : 2 * tile + 2])


def span_state(r_ref, rim_ref, taps_ref, pad_ref, span):
    running, steps, _, _ = decays_of(r_ref, span)
    tail = jnp.exp(running[SPAN - 1 : SPAN] - running) * steps
    b_conv = conv_silu(r_ref, rim_ref, taps_ref, pad_ref, span, TILES)
    parts, weighted = [], []
    for tile in range(TILES):
        part = conv_silu(r_ref, rim_ref, taps_ref, pad_ref, span, tile)
        parts.append(part)
        weighted.append((part.astype(F32) * spread(tail, tile)).astype(BF16))
    fresh = jnp.dot(
        jnp.transpose(b_conv.astype(F32)).astype(BF16),
        jnp.concatenate(weighted, 1),
        preferred_element_type=F32,
    )
    return jnp.concatenate(parts, 1), b_conv, fresh, running


def gather_rim(rims, rim_ref):
    total = rims[0][0].astype(F32)
    for ref in rims[1:]:
        total = total + ref[...].astype(F32)
    rim_ref[...] = total


def state_kernel(r_ref, taps_ref, *rest):
    rims, (message_ref, rim_ref, pad_ref) = rest[:MEMBERS], rest[MEMBERS:]
    gather_rim(rims, rim_ref)
    total, state = None, None
    for span in range(SPANS):
        _, _, fresh, running = span_state(r_ref, rim_ref, taps_ref, pad_ref, span)
        last = running[SPAN - 1 : SPAN]
        if span == 0:
            total, state = last, fresh
        else:
            factor = jnp.exp(last)
            kept = [state[:, t * 128 : (t + 1) * 128] * spread(factor, t) for t in range(TILES)]
            total, state = total + last, jnp.concatenate(kept, 1) + fresh
    factor = jnp.exp(total)
    for tile in range(TILES):
        here = state[:, tile * 128 : (tile + 1) * 128]
        scale = spread(factor, tile)
        coarse = scale.astype(BF16).astype(F32)
        tail = jnp.concatenate([coarse, scale - coarse, jnp.zeros((6, 128), F32)], 0)
        for cut in range(STATE // CUT):
            whole = jnp.concatenate([here[cut * CUT : (cut + 1) * CUT], tail], 0)
            message_ref[tile * (STATE // CUT) + cut] = whole.astype(BF16)


def local_kernel(r_ref, taps_ref, *rest):
    rims, (part_ref, c_ref, scale_ref, rim_ref, pad_ref) = rest[:MEMBERS], rest[MEMBERS:]
    gather_rim(rims, rim_ref)
    row = lax.broadcasted_iota(jnp.int32, (SPAN, SPAN), 0)
    column = lax.broadcasted_iota(jnp.int32, (SPAN, SPAN), 1)
    causal = row >= column
    low = lax.broadcasted_iota(jnp.int32, (SPAN, 128), 1) < HEAD_DIM
    before = jnp.zeros((1, MINE), F32)
    state = None
    for span in range(SPANS):
        running, _, running_row, steps_row = decays_of(r_ref, span)
        c_conv = conv_silu(r_ref, rim_ref, taps_ref, pad_ref, span, TILES + 1)
        c_ref[span] = c_conv
        x_conv, b_conv, fresh, _ = span_state(r_ref, rim_ref, taps_ref, pad_ref, span)
        scores = lax.dot_general(c_conv, b_conv, (((1,), (1,)), ((), ())), preferred_element_type=F32)
        grown = jnp.exp(running)
        scale = jnp.exp(running + before)
        for tile in range(TILES):
            lanes = slice(tile * 128, (tile + 1) * 128)
            pair = []
            for head in (2 * tile, 2 * tile + 1):
                gap = running[:, head : head + 1] - running_row[head : head + 1, :]
                decay = jnp.exp(jnp.where(causal, gap, -1e30)) * steps_row[head : head + 1, :]
                pair.append((decay * scores).astype(BF16))
            values = x_conv[:, lanes]
            both = jnp.dot(jnp.concatenate(pair, 0), values, preferred_element_type=F32)
            out = jnp.where(low, both[:SPAN], both[SPAN:])
            out = out + values.astype(F32) * taps_ref[4:5, lanes]
            if span:
                inter = jnp.dot(c_conv, state[:, lanes].astype(BF16), preferred_element_type=F32)
                out = out + inter * spread(grown, tile)
            part_ref[span, :, lanes] = out
            scale_ref[span, :, lanes] = spread(scale, tile)
        total = running[SPAN - 1 : SPAN]
        before = before + total
        if span == 0:
            state = fresh
        elif span < SPANS - 1:
            factor = jnp.exp(total)
            kept = [state[:, t * 128 : (t + 1) * 128] * spread(factor, t) for t in range(TILES)]
            state = jnp.concatenate(kept, 1) + fresh


def chain_kernel(all_ref, out_ref):
    state = jnp.zeros((CUT, 128), F32)
    for run in range(RUNS):
        out_ref[run] = state.astype(BF16)
        if run < RUNS - 1:
            here = all_ref[run].astype(F32)
            state = state * (here[CUT : CUT + 1] + here[CUT + 1 : CUT + 2]) + here[:CUT]


def finish_kernel(part_ref, c_ref, scale_ref, state_ref, out_ref):
    for span in range(SPANS):
        for tile in range(TILES):
            lanes = slice(tile * 128, (tile + 1) * 128)
            inter = jnp.dot(c_ref[span], state_ref[tile], preferred_element_type=F32)
            out = part_ref[span, :, lanes] + inter * scale_ref[span, :, lanes]
            out_ref[span * SPAN : (span + 1) * SPAN, lanes] = out.astype(BF16)


def norm_kernel(values_ref, z_ref, gain_ref, out_ref):
    for group in range(GROUPS):
        gated, square = [], None
        for core in range(CORES):
            lanes = slice((group * CORES + core) * WIDE, (group * CORES + core + 1) * WIDE)
            here = values_ref[core * RING + group].astype(F32) * silu(z_ref[:, lanes].astype(F32))
            gated.append((lanes, here))
            summed = jnp.sum(here * here, axis=1, keepdims=True)
            square = summed if square is None else square + summed
        scale = lax.rsqrt(square * (1.0 / (CORES * WIDE)) + 1e-05)
        for lanes, here in gated:
            out_ref[:, lanes] = (here * scale * gain_ref[:, lanes].astype(F32)).astype(BF16)


def shards(
    x_stream,
    z_stream,
    b_stream,
    c_stream,
    dt_stream,
    decay_stream,
    kernel_x,
    kernel_b,
    kernel_c,
    skip_gain,
    norm_gain,
):
    core = lax.axis_index("core")
    streams = (x_stream, b_stream, c_stream, dt_stream, decay_stream)
    packed, *rims = call(
        pack_kernel,
        (like((PEERS, PACK, 128), BF16),) + (like((MEMBERS, RIM, 128), BF16),) * LEADERS,
        0,
        2 * PEERS * PACK * 256,
        [pltpu.VMEM(stream.shape, BF16) for stream in streams] + [pltpu.SemaphoreType.DMA((5,))],
        vmem=60,
        in_specs=[pl.BlockSpec(memory_space=pltpu.HBM)] * 5,
    )(*streams)
    got = lax.all_to_all(packed, ("core", "head"), split_axis=0, concat_axis=0, tiled=True)
    everyone = ("seq", "core", "head")
    led = None
    for leader, rim in enumerate(rims):
        pairs = [(i * PEERS + PEERS - 1, (i + 1) * PEERS + leader * MEMBERS) for i in range(RUNS - 1)]
        came = lax.ppermute(rim, everyone, pairs)
        led = came if led is None else led + came
    handed = [led]
    for member in range(1, MEMBERS):
        pairs = [(i, i + member) for i in range(0, RUNS * PEERS, MEMBERS)]
        handed.append(lax.ppermute(led[member], everyone, pairs))
    taps_x = lax.dynamic_slice_in_dim(kernel_x, core * WIDE, WIDE, 1)
    skip = jnp.repeat(lax.dynamic_slice_in_dim(skip_gain, core * MINE, MINE), HEAD_DIM)
    taps = jnp.concatenate([taps_x, kernel_b, kernel_c], 1).astype(F32)
    skip_row = jnp.pad(skip, (0, 2 * STATE))[None]
    taps = jnp.concatenate([taps, skip_row, jnp.zeros((3, WIDE + 2 * STATE), F32)], 0)
    pad = pltpu.VMEM((SPAN + 8, 128), F32)
    rim = pltpu.VMEM((RIM, 128), F32)
    message = call(state_kernel, like((RUNS, CUT + 8, 128), BF16), 10**9, 2 * 10**6, [rim, pad])(got, taps, *handed)
    slices = lax.all_to_all(message, "seq", split_axis=0, concat_axis=0, tiled=True)
    part, c_conv, scale = call(
        local_kernel,
        (
            like((SPANS, SPAN, WIDE), F32),
            like((SPANS, SPAN, STATE), BF16),
            like((SPANS, SPAN, WIDE), F32),
        ),
        10**9,
        8 * 10**6,
        [rim, pad],
    )(got, taps, *handed)
    slices, part = lax.optimization_barrier((slices, part))
    chained = call(chain_kernel, like((RUNS, CUT, 128), BF16), 10**7, 10**6)(slices)
    state = lax.all_to_all(chained, "seq", split_axis=0, concat_axis=0, tiled=True)
    values = call(finish_kernel, like((TOKENS, WIDE), BF16), 10**8, 3 * 10**6)(
        part, c_conv, scale, state.reshape(TILES, STATE, 128)
    )
    home = lax.all_to_all(
        values.reshape(PEERS, ROWS, WIDE), ("core", "head"), split_axis=0, concat_axis=0, tiled=True
    )
    return call(norm_kernel, like((ROWS, HEADS * HEAD_DIM), BF16), 10**7, 2 * 10**6)(
        home, z_stream, norm_gain.reshape(1, HEADS * HEAD_DIM)
    )


def solution(mesh):
    finer = Mesh(mesh.devices.reshape(RUNS, CORES, RING), ("seq", "core", "head"))
    rows = P(("seq", "core", "head"), None)
    in_specs = (rows,) * 6 + (P(None, "head"),) * 3 + (P("head"), P())
    return jax.shard_map(shards, mesh=finer, in_specs=in_specs, out_specs=rows, check_vma=False)
```

time: 106 us -> 98.5 us (0.929)
  starting transfers between devices: 27.8 us -> 38.1 us
  waiting for transfers between devices: 39.7 us -> 32 us
  local copies, waits for them, and re-layouts: 9.25 us -> 1.7 us
  blocking collectives: 19 us -> 14.4 us
  Pallas kernels: 9.36 us -> 11.4 us
    all_to_all x1, waiting for transfers between devices: 20.8 us -> 6.06 us  [shards(): lax.all_to_all(packed, ('core', 'head'), split_axis=0, concat_axis=0, til...]
    unnamed x34 -> x20, local copies, waits for them, and re-layouts: 8.9 us -> 1.34 us
    ppermute x1 -> x7, starting transfers between devices: 3.2 us -> 9.06 us  [the longest x3 6.41 us: shards(): handed.append(lax.ppermute(led[member], everyone, pairs))]
    ppermute x1 -> x7, waiting for transfers between devices: 0.01 us -> 4.9 us  [the longest x3 4.89 us: shards(): handed.append(lax.ppermute(led[member], everyone, pairs))]
    all_to_all x1, blocking collectives: 19 us -> 14.4 us  [shards(): lax.all_to_all(chained, 'seq', split_axis=0, concat_axis=0, tiled=True)]
    all_to_all x1, starting transfers between devices: 5.46 us -> 10 us  [shards(): lax.all_to_all(message, 'seq', split_axis=0, concat_axis=0, tiled=True)]
    all_to_all x1, waiting for transfers between devices: 4.15 us -> 6.28 us  [shards(): lax.all_to_all(message, 'seq', split_axis=0, concat_axis=0, tiled=True)]
    pallas_call x1, Pallas kernels: 2.21 us -> 3.9 us  [shards(): call(local_kernel, (like((SPANS, SPAN, WIDE), F32), like((SPANS, SPAN, ST...]
  transfers between devices with their start and end apart: 4 -> 10, of which waited for: 3 -> 6; matrix products, arithmetic and copies ran while one was open for 0% -> 0% of each run, Pallas kernels for 4% -> 4%
where the time goes in v2:
time: 98.5 us; the launch traced here: 97.9 us
  starting transfers between devices  38.1 us (39%)
  waiting for transfers between devices  32 us (32%)
  blocking collectives  14.4 us (15%)
  Pallas kernels  11.4 us (12%)
  local copies, waits for them, and re-layouts  1.7 us (2%)
    all_to_all x1, waiting for transfers between devices, shards(): lax.all_to_all(values.reshape(PEERS, ROWS, WIDE), ('core', 'head'), split...  14.7 us
    all_to_all x1, blocking collectives, shards(): lax.all_to_all(chained, 'seq', split_axis=0, concat_axis=0, tiled=True)  14.4 us
    all_to_all x1, starting transfers between devices, shards(): lax.all_to_all(packed, ('core', 'head'), split_axis=0, concat_axis=0, til...  12 us
    all_to_all x1, starting transfers between devices, shards(): lax.all_to_all(message, 'seq', split_axis=0, concat_axis=0, tiled=True)  10 us
    all_to_all x1, starting transfers between devices, shards(): lax.all_to_all(values.reshape(PEERS, ROWS, WIDE), ('core', 'head'), split...  6.98 us
    ppermute x3, starting transfers between devices, shards(): handed.append(lax.ppermute(led[member], everyone, pairs))  6.41 us
    all_to_all x1, waiting for transfers between devices, shards(): lax.all_to_all(message, 'seq', split_axis=0, concat_axis=0, tiled=True)  6.28 us
    all_to_all x1, waiting for transfers between devices, shards(): lax.all_to_all(packed, ('core', 'head'), split_axis=0, concat_axis=0, til...  6.06 us
  transfers between devices with their start and end apart: 10, of which 6 were waited for; matrix products, arithmetic and copies ran while one was open for 0% of the time, Pallas kernels for 4%

profile of v2, /device:TPU:1, one launch (start us, length us, event | category | flops | bytes accessed | tf_op | source)
XLA Modules:
  0.0 97.9 jit_solution(11725698994938628893)
XLA Ops:
  0.0 0.0 copy-start
  0.0 2.2 %shard_map.109 = (bf16[16,200,128]{2,1,0:T(8,128)(2,1)}, bf16[4,48,128]{2,1,0:T(8,128)(2,1)}, bf16[4,48,128]{2,1,0:T(8,128)(2,1)}, bf16[4,48,128]{2,1,0:T(8,128)(2,1)}, bf16[4,48,128]{2,1,0:T(8,128)(2,1)}) custom-call(bf16[32,8192]{1,0:T(8,128)(2,1)} %x_hbm.1, bf16[32,1024]{1,0:T(8,128)(2,1)} %b_hbm.1, bf16[32,1024]{1,0:T(8,128)(2,1)} %c_hbm.1, ...), custom_call_target="tpu_custom_call" | custom-call | bytes 1638400 | tf_op jit(solution)/shard_map/pallas_call | solution.py:272
  2.3 0.0 copy-start.8
  2.3 0.0 copy-start.7
  2.3 0.0 copy-start.6
  2.3 0.0 copy-start.5
  2.3 12.0 %all-to-all-start = ((bf16[16,200,128]{2,1,0:T(8,128)(2,1)}), bf16[16,200,128]{2,1,0:T(8,128)(2,1)S(1)}, u32[]{:S(2)}, u32[]{:S(2)}) async-start(bf16[16,200,128]{2,1,0:T(8,128)(2,1)} %get-tuple-element.15), calls=%async_computation | async-start | bytes 1638400 | tf_op jit(solution)/shard_map/all_to_all | solution.py:281
  14.3 0.0 copy-done.8
  14.3 0.7 collective-permute-start
  15.0 0.0 copy-done.7
  15.0 0.7 collective-permute-start.1
  15.6 0.0 copy-done.6
  15.6 0.7 collective-permute-start.2
  16.3 0.0 copy-done.5
  16.3 0.7 collective-permute-start.3
  17.0 0.0 copy-done
  17.0 0.0 copy-start.3
  17.0 0.0 copy-start.4
  17.1 0.6 copy-done.3
  17.7 0.0 copy-done.4
  17.7 0.0 copy-start.9
  17.7 0.6 copy-done.9
  18.4 0.1 dynamic_slice.7
  18.4 0.1 broadcast_in_dim.9
  18.5 0.1 reshape.12
  18.6 0.1 pad.7.clone
  18.7 0.0 collective-permute-done
  18.7 0.0 collective-permute-done.1
  18.7 0.0 collective-permute-done.2
  18.7 0.0 collective-permute-done.3
  18.8 3.3 %collective-permute-start.4 = (bf16[48,128]{1,0:T(8,128)(2,1)S(1)}, bf16[48,128]{1,0:T(8,128)(2,1)S(1)}, u32[]{:S(2)}, u32[]{:S(2)}) collective-permute-start(bf16[48,128]{1,0:T(8,128)(2,1)S(1)} %get-tuple-element.27), channel_id=1, source_target_pairs={{0,1},{4,5},{8,9},{12,13},{16,17},{20,21},{24,25},{28,29},{32,33},... | collective-permute-start | bytes 36872 | tf_op jit(solution)/shard_map/ppermute | solution.py:291
  22.0 1.6 %collective-permute-start.5 = (bf16[48,128]{1,0:T(8,128)(2,1)S(1)}, bf16[48,128]{1,0:T(8,128)(2,1)S(1)}, u32[]{:S(2)}, u32[]{:S(2)}) collective-permute-start(bf16[48,128]{1,0:T(8,128)(2,1)S(1)} %get-tuple-element.26), channel_id=1, source_target_pairs={{0,2},{4,6},{8,10},{12,14},{16,18},{20,22},{24,26},{28,30},{32,34}... | collective-permute-start | bytes 36872 | tf_op jit(solution)/shard_map/ppermute | solution.py:291
  23.6 1.6 %collective-permute-start.6 = (bf16[48,128]{1,0:T(8,128)(2,1)S(1)}, bf16[48,128]{1,0:T(8,128)(2,1)S(1)}, u32[]{:S(2)}, u32[]{:S(2)}) collective-permute-start(bf16[48,128]{1,0:T(8,128)(2,1)S(1)} %get-tuple-element.25), channel_id=1, source_target_pairs={{0,3},{4,7},{8,11},{12,15},{16,19},{20,23},{24,27},{28,31},{32,35}... | collective-permute-start | bytes 36872 | tf_op jit(solution)/shard_map/ppermute | solution.py:291
  25.2 0.1 maximum_maximum_fusion.taps_ref
  25.3 3.7 %collective-permute-done.4.rest_1_ = bf16[48,128]{1,0:T(8,128)(2,1)S(1)} collective-permute-done((bf16[48,128]{1,0:T(8,128)(2,1)S(1)}, bf16[48,128]{1,0:T(8,128)(2,1)S(1)}, u32[]{:S(2)}, u32[]{:S(2)}) %collective-permute-start.4) | collective-permute-done | bytes 12320 | tf_op jit(solution)/shard_map/ppermute | solution.py:291
  28.9 0.7 collective-permute-done.5.rest_2_
  29.7 0.5 collective-permute-done.6.rest_3_
  30.1 6.1 %all-to-all-done.r_ref = bf16[16,200,128]{2,1,0:T(8,128)(2,1)S(1)} async-done(((bf16[16,200,128]{2,1,0:T(8,128)(2,1)}), bf16[16,200,128]{2,1,0:T(8,128)(2,1)S(1)}, u32[]{:S(2)}, u32[]{:S(2)}) %all-to-all-start) | async-done | bytes 819232 | tf_op jit(solution)/shard_map/all_to_all | solution.py:281
  36.2 2.8 %shard_map.110 = bf16[32,24,128]{2,1,0:T(8,128)(2,1)} custom-call(bf16[16,200,128]{2,1,0:T(8,128)(2,1)S(1)} %all-to-all-done.r_ref, f32[8,768]{1,0:T(8,128)S(1)} %maximum_maximum_fusion.taps_ref, bf16[4,48,128]{2,1,0:T(8,128)(2,1)S(1)} %add_add_fusion.rest_0_, bf16[48,128]{1,0:T(8,128)(2,1)S(1)} %collective-permute-done.4.rest_1_, ...), custom_call_target="tpu_custom_call" | custom-call | flops 1000000000 | bytes 2000000 | tf_op jit(solution)/shard_map/pallas_call | solution.py:299
  39.0 10.0 %all-to-all-start.1 = ((bf16[32,24,128]{2,1,0:T(8,128)(2,1)}), bf16[32,24,128]{2,1,0:T(8,128)(2,1)S(1)}, u32[]{:S(2)}, u32[]{:S(2)}) async-start(bf16[32,24,128]{2,1,0:T(8,128)(2,1)} %shard_map.110), calls=%async_computation.1 | async-start | bytes 393216 | tf_op jit(solution)/shard_map/all_to_all | solution.py:300
  49.1 3.9 %shard_map.111 = (f32[4,128,512]{2,1,0:T(8,128)S(1)}, bf16[4,128,128]{2,1,0:T(8,128)(2,1)S(1)}, f32[4,128,512]{2,1,0:T(8,128)S(1)}) custom-call(bf16[16,200,128]{2,1,0:T(8,128)(2,1)S(1)} %all-to-all-done.r_ref, f32[8,768]{1,0:T(8,128)S(1)} %maximum_maximum_fusion.taps_ref, bf16[4,48,128]{2,1,0:T(8,128)(2,1)S(1)} %add_add_fusion.rest_0_, ...), custom_call_target="tpu_custom_call" | custom-call | flops 1000000000 | bytes 8000000 | tf_op jit(solution)/shard_map/pallas_call | solution.py:301
  53.0 6.3 %all-to-all-done.1.all_ref = bf16[32,24,128]{2,1,0:T(8,128)(2,1)S(1)} async-done(((bf16[32,24,128]{2,1,0:T(8,128)(2,1)}), bf16[32,24,128]{2,1,0:T(8,128)(2,1)S(1)}, u32[]{:S(2)}, u32[]{:S(2)}) %all-to-all-start.1) | async-done | bytes 196640 | tf_op jit(solution)/shard_map/all_to_all | solution.py:300
  59.2 0.1 shard_map.112
  59.3 14.4 %all_to_all.20 = bf16[32,16,128]{2,1,0:T(8,128)(2,1)S(1)} all-to-all(bf16[32,16,128]{2,1,0:T(8,128)(2,1)S(1)} %shard_map.112), channel_id=1, replica_groups=mesh['seq'=32,'core'=2,'head'=8] {'seq'}, dimensions={0} | all-to-all | bytes 262144 | tf_op jit(solution)/shard_map/all_to_all | solution.py:314
  73.7 1.1 %shard_map.113 = bf16[512,512]{1,0:T(8,128)(2,1)} custom-call(f32[4,128,512]{2,1,0:T(8,128)S(1)} %get-tuple-element.21.part_ref, bf16[4,128,128]{2,1,0:T(8,128)(2,1)S(1)} %get-tuple-element.22.c_ref, f32[4,128,512]{2,1,0:T(8,128)S(1)} %get-tuple-element.23.scale_ref, bf16[4,128,128]{2,1,0:T(8,128)(2,1)S(1)} %bitcast.8), custom_call_target="tpu_custom_call" | custom-call | flops 100000000 | bytes 3000000 | tf_op jit(solution)/shard_map/pallas_call | solution.py:315
  74.8 0.0 copy-start.2
  74.8 0.0 copy-start.1
  74.8 7.0 %all-to-all-start.3 = ((bf16[16,32,512]{2,1,0:T(8,128)(2,1)}), bf16[16,32,512]{2,1,0:T(8,128)(2,1)S(1)}, u32[]{:S(2)}, u32[]{:S(2)}) async-start(bf16[16,32,512]{2,1,0:T(8,128)(2,1)} %bitcast.4), calls=%async_computation.3 | async-start | bytes 1048576 | tf_op jit(solution)/shard_map/all_to_all | solution.py:318
  81.8 0.0 copy-done.2
  81.8 14.7 %all-to-all-done.3.values_ref = bf16[16,32,512]{2,1,0:T(8,128)(2,1)S(1)} async-done(((bf16[16,32,512]{2,1,0:T(8,128)(2,1)}), bf16[16,32,512]{2,1,0:T(8,128)(2,1)S(1)}, u32[]{:S(2)}, u32[]{:S(2)}) %all-to-all-start.3) | async-done | bytes 524320 | tf_op jit(solution)/shard_map/all_to_all | solution.py:318
  96.6 0.0 copy-done.1
  96.6 1.3 %shard_map.114 = bf16[32,8192]{1,0:T(8,128)(2,1)} custom-call(bf16[16,32,512]{2,1,0:T(8,128)(2,1)S(1)} %all-to-all-done.3.values_ref, bf16[32,8192]{1,0:T(8,128)(2,1)S(1)} %copy-done.1, bf16[1,8192]{1,0:T(2,128)(2,1)S(1)} %reshape.15.gain_ref), custom_call_target="tpu_custom_call" | custom-call | flops 10000000 | bytes 2000000 | tf_op jit(solution)/shard_map/pallas_call | solution.py:321
  (8 shorter events, 0.1 us)
Async XLA Ops:
  0.0 17.0 %copy-start = (bf16[4,1024]{1,0:T(4,128)(2,1)S(1)}, bf16[4,1024]{1,0:T(4,128)(2,1)}, u32[]{:S(2)}) copy-start(bf16[4,1024]{1,0:T(4,128)(2,1)} %param.17) | copy-start | bytes 24580
  2.3 12.0 %copy-start.8 = (bf16[4,48,128]{2,1,0:T(8,128)(2,1)S(1)}, bf16[4,48,128]{2,1,0:T(8,128)(2,1)}, u32[]{:S(2)}) copy-start(bf16[4,48,128]{2,1,0:T(8,128)(2,1)} %get-tuple-element.16) | copy-start | bytes 147460
  2.3 12.7 %copy-start.7 = (bf16[4,48,128]{2,1,0:T(8,128)(2,1)S(1)}, bf16[4,48,128]{2,1,0:T(8,128)(2,1)}, u32[]{:S(2)}) copy-start(bf16[4,48,128]{2,1,0:T(8,128)(2,1)} %get-tuple-element.17) | copy-start | bytes 147460
  2.3 13.4 %copy-start.6 = (bf16[4,48,128]{2,1,0:T(8,128)(2,1)S(1)}, bf16[4,48,128]{2,1,0:T(8,128)(2,1)}, u32[]{:S(2)}) copy-start(bf16[4,48,128]{2,1,0:T(8,128)(2,1)} %get-tuple-element.18) | copy-start | bytes 147460
  2.3 14.0 %copy-start.5 = (bf16[4,48,128]{2,1,0:T(8,128)(2,1)S(1)}, bf16[4,48,128]{2,1,0:T(8,128)(2,1)}, u32[]{:S(2)}) copy-start(bf16[4,48,128]{2,1,0:T(8,128)(2,1)} %get-tuple-element.19) | copy-start | bytes 147460
  2.3 33.9 %all-to-all-start = ((bf16[16,200,128]{2,1,0:T(8,128)(2,1)}), bf16[16,200,128]{2,1,0:T(8,128)(2,1)S(1)}, u32[]{:S(2)}, u32[]{:S(2)}) async-start(bf16[16,200,128]{2,1,0:T(8,128)(2,1)} %get-tuple-element.15), calls=%async_computation | async-start | bytes 1638400 | tf_op jit(solution)/shard_map/all_to_all | solution.py:281
  14.3 4.4 %collective-permute-start = (bf16[4,48,128]{2,1,0:T(8,128)(2,1)S(1)}, bf16[4,48,128]{2,1,0:T(8,128)(2,1)S(1)}, u32[]{:S(2)}, u32[]{:S(2)}) collective-permute-start(bf16[4,48,128]{2,1,0:T(8,128)(2,1)S(1)} %copy-done.8), channel_id=1, source_target_pairs={{15,16},{31,32},{47,48},{63,64},{79,80},{95,96},{111,112},{127,128... | collective-permute-start | bytes 147464 | tf_op jit(solution)/shard_map/ppermute | solution.py:286
  15.0 3.7 %collective-permute-start.1 = (bf16[4,48,128]{2,1,0:T(8,128)(2,1)S(1)}, bf16[4,48,128]{2,1,0:T(8,128)(2,1)S(1)}, u32[]{:S(2)}, u32[]{:S(2)}) collective-permute-start(bf16[4,48,128]{2,1,0:T(8,128)(2,1)S(1)} %copy-done.7), channel_id=1, source_target_pairs={{15,20},{31,36},{47,52},{63,68},{79,84},{95,100},{111,116},{127,13... | collective-permute-start | bytes 147464 | tf_op jit(solution)/shard_map/ppermute | solution.py:286
  15.6 3.1 %collective-permute-start.2 = (bf16[4,48,128]{2,1,0:T(8,128)(2,1)S(1)}, bf16[4,48,128]{2,1,0:T(8,128)(2,1)S(1)}, u32[]{:S(2)}, u32[]{:S(2)}) collective-permute-start(bf16[4,48,128]{2,1,0:T(8,128)(2,1)S(1)} %copy-done.6), channel_id=1, source_target_pairs={{15,24},{31,40},{47,56},{63,72},{79,88},{95,104},{111,120},{127,13... | collective-permute-start | bytes 147464 | tf_op jit(solution)/shard_map/ppermute | solution.py:286
  16.3 2.4 %collective-permute-start.3 = (bf16[4,48,128]{2,1,0:T(8,128)(2,1)S(1)}, bf16[4,48,128]{2,1,0:T(8,128)(2,1)S(1)}, u32[]{:S(2)}, u32[]{:S(2)}) collective-permute-start(bf16[4,48,128]{2,1,0:T(8,128)(2,1)S(1)} %copy-done.5), channel_id=1, source_target_pairs={{15,28},{31,44},{47,60},{63,76},{79,92},{95,108},{111,124},{127,14... | collective-permute-start | bytes 147464 | tf_op jit(solution)/shard_map/ppermute | solution.py:286
  17.0 0.7 copy-start.3
  17.0 0.7 copy-start.4
  17.7 0.7 copy-start.9
  18.8 10.2 %collective-permute-start.4 = (bf16[48,128]{1,0:T(8,128)(2,1)S(1)}, bf16[48,128]{1,0:T(8,128)(2,1)S(1)}, u32[]{:S(2)}, u32[]{:S(2)}) collective-permute-start(bf16[48,128]{1,0:T(8,128)(2,1)S(1)} %get-tuple-element.27), channel_id=1, source_target_pairs={{0,1},{4,5},{8,9},{12,13},{16,17},{20,21},{24,25},{28,29},{32,33},... | collective-permute-start | bytes 36872 | tf_op jit(solution)/shard_map/ppermute | solution.py:291
  22.0 7.6 %collective-permute-start.5 = (bf16[48,128]{1,0:T(8,128)(2,1)S(1)}, bf16[48,128]{1,0:T(8,128)(2,1)S(1)}, u32[]{:S(2)}, u32[]{:S(2)}) collective-permute-start(bf16[48,128]{1,0:T(8,128)(2,1)S(1)} %get-tuple-element.26), channel_id=1, source_target_pairs={{0,2},{4,6},{8,10},{12,14},{16,18},{20,22},{24,26},{28,30},{32,34}... | collective-permute-start | bytes 36872 | tf_op jit(solution)/shard_map/ppermute | solution.py:291
  23.6 6.5 %collective-permute-start.6 = (bf16[48,128]{1,0:T(8,128)(2,1)S(1)}, bf16[48,128]{1,0:T(8,128)(2,1)S(1)}, u32[]{:S(2)}, u32[]{:S(2)}) collective-permute-start(bf16[48,128]{1,0:T(8,128)(2,1)S(1)} %get-tuple-element.25), channel_id=1, source_target_pairs={{0,3},{4,7},{8,11},{12,15},{16,19},{20,23},{24,27},{28,31},{32,35}... | collective-permute-start | bytes 36872 | tf_op jit(solution)/shard_map/ppermute | solution.py:291
  39.0 20.2 %all-to-all-start.1 = ((bf16[32,24,128]{2,1,0:T(8,128)(2,1)}), bf16[32,24,128]{2,1,0:T(8,128)(2,1)S(1)}, u32[]{:S(2)}, u32[]{:S(2)}) async-start(bf16[32,24,128]{2,1,0:T(8,128)(2,1)} %shard_map.110), calls=%async_computation.1 | async-start | bytes 393216 | tf_op jit(solution)/shard_map/all_to_all | solution.py:300
  74.8 7.0 %copy-start.2 = (bf16[8192]{0:T(1024)(128)(2,1)S(1)}, bf16[8192]{0:T(1024)(128)(2,1)}, u32[]{:S(2)}) copy-start(bf16[8192]{0:T(1024)(128)(2,1)} %param.21) | copy-start | bytes 49156
  74.8 21.8 %copy-start.1 = (bf16[32,8192]{1,0:T(8,128)(2,1)S(1)}, bf16[32,8192]{1,0:T(8,128)(2,1)}, u32[]{:S(2)}) copy-start(bf16[32,8192]{1,0:T(8,128)(2,1)} %z_ref.1) | copy-start | bytes 1572868
  74.8 21.8 %all-to-all-start.3 = ((bf16[16,32,512]{2,1,0:T(8,128)(2,1)}), bf16[16,32,512]{2,1,0:T(8,128)(2,1)S(1)}, u32[]{:S(2)}, u32[]{:S(2)}) async-start(bf16[16,32,512]{2,1,0:T(8,128)(2,1)} %bitcast.4), calls=%async_computation.3 | async-start | bytes 1048576 | tf_op jit(solution)/shard_map/all_to_all | solution.py:318

commit v3 on v2

v3 whole, which is shorter than its diff:
```python
import functools

import jax
import jax.numpy as jnp
from jax import lax
from jax.experimental import pallas as pl
from jax.experimental.pallas import tpu as pltpu
from jax.sharding import Mesh
from jax.sharding import PartitionSpec as P

HEADS = 128
HEAD_DIM = 64
STATE = 128
GROUPS = 8
SPAN = 128
CORES = 2
RING = 8
PEERS = CORES * RING
ROWS = 32
TOKENS = PEERS * ROWS
SPANS = TOKENS // SPAN
FROM = SPAN // ROWS
MINE = HEADS // PEERS
WIDE = MINE * HEAD_DIM
TILES = WIDE // 128
LEADERS = 4
MEMBERS = PEERS // LEADERS
RIM = 8 * (TILES + 2)
RUNS = 32
HALF = ROWS // CORES
PACK = ROWS * (TILES + 1) + HALF + MINE
CUT = STATE * TILES // RUNS
F32 = jnp.float32
BF16 = jnp.bfloat16
MIB = 1024 * 1024


def call(body, outs, flops, moved, scratch=(), vmem=16, **specs):
    return pl.pallas_call(
        body,
        **specs,
        out_shape=outs,
        scratch_shapes=list(scratch),
        compiler_params=pltpu.CompilerParams(vmem_limit_bytes=vmem * MIB),
        cost_estimate=pl.CostEstimate(flops=flops, bytes_accessed=moved, transcendentals=0),
    )


def like(shape, dtype):
    return jax.ShapeDtypeStruct(shape, dtype)


def silu(x):
    half = 0.5 * x
    return half * jnp.tanh(half) + half


def pack_kernel(x_hbm, b_hbm, c_hbm, dt_hbm, decay_hbm, out_ref, *rest):
    rims, (x_ref, b_ref, c_ref, dt_ref, decay_ref, arrived) = rest[:LEADERS], rest[LEADERS:]
    pairs = ((dt_hbm, dt_ref), (decay_hbm, decay_ref), (b_hbm, b_ref), (c_hbm, c_ref), (x_hbm, x_ref))
    copies = [pltpu.make_async_copy(a, b, arrived.at[i]) for i, (a, b) in enumerate(pairs)]
    for copy in copies:
        copy.start()
    copies[0].wait()
    copies[1].wait()
    steps = jnp.transpose(dt_ref[...].astype(F32))
    decays = jnp.transpose(decay_ref[...].astype(F32))
    at = TILES * ROWS
    for copy in copies[2:4]:
        copy.wait()
    for core in range(CORES):
        for ring in range(RING):
            peer = core * RING + ring
            out_ref[peer, at : at + ROWS, :] = b_ref[:, ring * 128 : (ring + 1) * 128]
            rows = slice(core * HALF, (core + 1) * HALF)
            out_ref[peer, at + ROWS : at + ROWS + HALF, :] = c_ref[rows, ring * 128 : (ring + 1) * 128]
            head = (ring * CORES + core) * MINE
            rest = jnp.zeros((MINE, 128 - 2 * ROWS), F32)
            both = jnp.concatenate([steps[head : head + MINE], decays[head : head + MINE], rest], 1)
            out_ref[peer, at + ROWS + HALF :, :] = both.astype(BF16)
    copies[4].wait()
    for core in range(CORES):
        for ring in range(RING):
            for tile in range(TILES):
                column = ring * CORES * WIDE + core * WIDE + tile * 128
                out_ref[core * RING + ring, tile * ROWS : (tile + 1) * ROWS, :] = x_ref[:, column : column + 128]
    for leader in range(LEADERS):
        for member in range(MEMBERS):
            core, ring = divmod(leader * MEMBERS + member, RING)
            column = (ring * CORES + core) * WIDE
            rows = slice(ROWS - 16, ROWS)
            pieces = [x_ref[rows, column + tile * 128 : column + (tile + 1) * 128] for tile in range(TILES)]
            pieces += [ref[rows, ring * 128 : (ring + 1) * 128] for ref in (b_ref, c_ref)]
            whole = jnp.concatenate([piece.astype(F32)[8:] for piece in pieces], 0)
            rims[leader][member] = whole.astype(BF16)


def raw(r_ref, span, tile):
    return r_ref[span * FROM : (span + 1) * FROM, tile * ROWS : (tile + 1) * ROWS, :].reshape(SPAN, 128)


def c_rows(r_ref):
    at = (TILES + 1) * ROWS
    return r_ref[:, at : at + HALF, :]


def fill(r_ref, rims, pad_ref, tiles):
    for tile in tiles:
        rows = slice(tile * 8, (tile + 1) * 8)
        edge = rims[0][0, rows, :].astype(F32)
        for ref in rims[1:]:
            edge = edge + ref[rows, :].astype(F32)
        pad_ref[tile, 0:8, :] = edge
        if tile > TILES:
            continue
        for span in range(SPANS):
            pad_ref[tile, 8 + span * SPAN : 8 + (span + 1) * SPAN, :] = raw(r_ref, span, tile).astype(F32)


def conv_silu(taps_ref, pad_ref, span, tile):
    lanes = slice(tile * 128, (tile + 1) * 128)
    at = span * SPAN
    whole = pad_ref[tile, at : at + SPAN + 8, :]
    total = whole[8:] * taps_ref[3:4, lanes]
    for tap in range(3):
        total = total + pltpu.roll(whole, 3 - tap, 0)[8:] * taps_ref[tap : tap + 1, lanes]
    return silu(total).astype(BF16)


def rows_of(r_ref):
    at = (TILES + 1) * ROWS + HALF
    steps, decays = [], []
    for span in range(SPANS):
        parts = [r_ref[span * FROM + m, at : at + MINE, :].astype(F32) for m in range(FROM)]
        steps.append(jnp.concatenate([part[:, :ROWS] for part in parts], 1))
        decays.append(jnp.concatenate([part[:, ROWS : 2 * ROWS] for part in parts], 1))
    decays = jnp.concatenate(decays, 0)
    row = lax.broadcasted_iota(jnp.int32, (SPAN, SPAN), 0)
    column = lax.broadcasted_iota(jnp.int32, (SPAN, SPAN), 1)
    upper = (row <= column).astype(F32).astype(BF16)
    running = jnp.dot(decays.astype(BF16), upper, preferred_element_type=F32)
    return jnp.concatenate(steps, 0), running


def terms(x, count):
    parts = []
    for _ in range(count):
        parts.append(x.astype(BF16))
        x = x - parts[-1].astype(F32)
    return parts


def own_lanes(count):
    row = lax.broadcasted_iota(jnp.int32, (count * MINE, WIDE), 0)
    column = lax.broadcasted_iota(jnp.int32, (count * MINE, WIDE), 1)
    return (lax.rem(row, MINE) == lax.div(column, HEAD_DIM)).astype(F32).astype(BF16)


def widen(per_head, lanes, count):
    stack = jnp.concatenate([part.astype(F32) for part in terms(per_head, count)], 0).astype(BF16)
    return lax.dot_general(stack, lanes, (((0,), (0,)), ((), ())), preferred_element_type=F32)


def span_state(taps_ref, pad_ref, span, tail):
    b_conv = conv_silu(taps_ref, pad_ref, span, TILES)
    parts = [conv_silu(taps_ref, pad_ref, span, tile) for tile in range(TILES)]
    x_conv = jnp.concatenate(parts, 1)
    weighted = (x_conv.astype(F32) * tail).astype(BF16)
    b_turned = jnp.transpose(b_conv.astype(F32)).astype(BF16)
    return x_conv, b_conv, jnp.dot(b_turned, weighted, preferred_element_type=F32)


def of_span(x, span):
    return x[span * MINE : (span + 1) * MINE]


def state_kernel(r_ref, taps_ref, *rest):
    rims, (message_ref, half_ref, pad_ref) = rest[:MEMBERS], rest[MEMBERS:]
    half_ref[...] = c_rows(r_ref)
    fill(r_ref, rims, pad_ref, range(TILES + 1))
    steps, running = rows_of(r_ref)
    lanes = own_lanes(2)
    tails = jnp.exp(running[:, SPAN - 1 :] - running) * steps
    last = [of_span(running, span)[:, SPAN - 1 :] for span in range(SPANS)]
    factors = jnp.exp(jnp.concatenate(last + [last[0] + last[1] + last[2] + last[3]], 1))
    factors = jnp.concatenate([factors, jnp.zeros((MINE, SPAN - SPANS - 1), F32)], 1)
    factors = widen(factors, lanes, 2)
    state = None
    for span in range(SPANS):
        _, _, fresh = span_state(taps_ref, pad_ref, span, widen(of_span(tails, span), lanes, 2))
        state = fresh if span == 0 else state * factors[span : span + 1] + fresh
    scale = factors[SPANS : SPANS + 1]
    coarse = scale.astype(BF16).astype(F32)
    tail = jnp.concatenate([coarse, scale - coarse, jnp.zeros((6, WIDE), F32)], 0)
    for tile in range(TILES):
        here = slice(tile * 128, (tile + 1) * 128)
        for cut in range(STATE // CUT):
            whole = jnp.concatenate([state[cut * CUT : (cut + 1) * CUT, here], tail[:, here]], 0)
            message_ref[tile * (STATE // CUT) + cut] = whole.astype(BF16)


def local_kernel(core_ref, r_ref, other_ref, taps_ref, *rest):
    rims, (part_ref, c_ref, scale_ref, pad_ref) = rest[:MEMBERS], rest[MEMBERS:]
    fill(r_ref, rims, pad_ref, range(TILES + 2))
    first = core_ref[0] == 0
    own, other = c_rows(r_ref).astype(F32), other_ref[...].astype(F32)
    whole = jnp.concatenate([jnp.where(first, own, other), jnp.where(first, other, own)], 1)
    pad_ref[TILES + 1, 8:, :] = whole.reshape(TOKENS, 128)
    row = lax.broadcasted_iota(jnp.int32, (SPAN, SPAN), 0)
    column = lax.broadcasted_iota(jnp.int32, (SPAN, SPAN), 1)
    causal = row >= column
    low = lax.broadcasted_iota(jnp.int32, (SPAN, 128), 1) < HEAD_DIM
    steps, running = rows_of(r_ref)
    lanes_two, lanes_three = own_lanes(2), own_lanes(3)
    tails = jnp.exp(running[:, SPAN - 1 :] - running) * steps
    turned = jnp.transpose(jnp.concatenate([running, jnp.zeros((SPAN - SPANS * MINE, SPAN), F32)], 0))
    before = jnp.zeros((MINE, 1), F32)
    state = None
    for span in range(SPANS):
        c_conv = conv_silu(taps_ref, pad_ref, span, TILES + 1)
        c_ref[span] = c_conv
        x_conv, b_conv, fresh = span_state(taps_ref, pad_ref, span, widen(of_span(tails, span), lanes_two, 2))
        scores = lax.dot_general(c_conv, b_conv, (((1,), (1,)), ((), ())), preferred_element_type=F32)
        here = of_span(running, span)
        grown = widen(jnp.exp(here), lanes_two, 2)
        scale_ref[span] = grown if span == 0 else widen(jnp.exp(here + before), lanes_two, 2)
        outs = []
        for tile in range(TILES):
            lanes = slice(tile * 128, (tile + 1) * 128)
            pair = []
            for head in (2 * tile, 2 * tile + 1):
                at = span * MINE + head
                gap = turned[:, at : at + 1] - running[at : at + 1]
                decay = jnp.exp(jnp.where(causal, gap, -1e30)) * steps[at : at + 1]
                pair.append((decay * scores).astype(BF16))
            both = jnp.dot(jnp.concatenate(pair, 0), x_conv[:, lanes], preferred_element_type=F32)
            outs.append(jnp.where(low, both[:SPAN], both[SPAN:]))
        out = jnp.concatenate(outs, 1) + x_conv.astype(F32) * taps_ref[4:5, :WIDE]
        if span:
            out = out + jnp.dot(c_conv, state.astype(BF16), preferred_element_type=F32) * grown
        part_ref[span] = out
        before = before + here[:, SPAN - 1 :]
        if span == 0:
            state = fresh
        elif span < SPANS - 1:
            state = state * grown[SPAN - 1 :] + fresh


def chain_kernel(all_ref, out_ref):
    state = jnp.zeros((CUT, 128), F32)
    for run in range(RUNS):
        out_ref[run] = state.astype(BF16)
        if run < RUNS - 1:
            here = all_ref[run].astype(F32)
            state = state * (here[CUT : CUT + 1] + here[CUT + 1 : CUT + 2]) + here[:CUT]


def finish_kernel(part_ref, c_ref, scale_ref, state_ref, out_hbm, out_ref, sent):
    state = jnp.concatenate([state_ref[tile] for tile in range(TILES)], 1)
    copies = []
    for span in range(SPANS):
        rows = slice(span * SPAN, (span + 1) * SPAN)
        inter = jnp.dot(c_ref[span], state, preferred_element_type=F32)
        out_ref[rows, :] = (part_ref[span] + inter * scale_ref[span]).astype(BF16)
        copies.append(pltpu.make_async_copy(out_ref.at[rows, :], out_hbm.at[rows, :], sent.at[span]))
        copies[-1].start()
    for copy in copies:
        copy.wait()


def gate_kernel(z_ref, out_ref):
    out_ref[...] = silu(z_ref[...].astype(F32))


def norm_kernel(values_ref, gate_ref, gain_ref, out_hbm, out_ref, sent):
    copies = []
    for group in range(GROUPS):
        whole = slice(group * CORES * WIDE, (group + 1) * CORES * WIDE)
        here = jnp.concatenate([values_ref[core * RING + group] for core in range(CORES)], 1)
        here = here.astype(F32) * gate_ref[:, whole]
        square = jnp.sum(here * here, axis=1, keepdims=True)
        scale = lax.rsqrt(square * (1.0 / (CORES * WIDE)) + 1e-05)
        out_ref[:, whole] = (here * scale * gain_ref[:, whole].astype(F32)).astype(BF16)
        copies.append(pltpu.make_async_copy(out_ref.at[:, whole], out_hbm.at[:, whole], sent.at[group]))
        copies[-1].start()
    for copy in copies:
        copy.wait()


def shards(
    x_stream,
    z_stream,
    b_stream,
    c_stream,
    dt_stream,
    decay_stream,
    kernel_x,
    kernel_b,
    kernel_c,
    skip_gain,
    norm_gain,
):
    core = lax.axis_index("core")
    streams = (x_stream, b_stream, c_stream, dt_stream, decay_stream)
    packed, *rims = call(
        pack_kernel,
        (like((PEERS, PACK, 128), BF16),) + (like((MEMBERS, RIM, 128), BF16),) * LEADERS,
        0,
        2 * PEERS * PACK * 256,
        [pltpu.VMEM(stream.shape, BF16) for stream in streams] + [pltpu.SemaphoreType.DMA((5,))],
        vmem=60,
        in_specs=[pl.BlockSpec(memory_space=pltpu.HBM)] * 5,
    )(*streams)
    got = lax.all_to_all(packed, ("core", "head"), split_axis=0, concat_axis=0, tiled=True)
    everyone = ("seq", "core", "head")
    led = None
    for leader, rim in enumerate(rims):
        pairs = [(i * PEERS + PEERS - 1, (i + 1) * PEERS + leader * MEMBERS) for i in range(RUNS - 1)]
        came = lax.ppermute(rim, everyone, pairs)
        led = came if led is None else led + came
    handed = [led]
    for member in range(1, MEMBERS):
        pairs = [(i, i + member) for i in range(0, RUNS * PEERS, MEMBERS)]
        handed.append(lax.ppermute(led[member], everyone, pairs))
    taps_x = lax.dynamic_slice_in_dim(kernel_x, core * WIDE, WIDE, 1)
    skip = jnp.repeat(lax.dynamic_slice_in_dim(skip_gain, core * MINE, MINE), HEAD_DIM)
    taps = jnp.concatenate([taps_x, kernel_b, kernel_c], 1).astype(F32)
    skip_row = jnp.pad(skip, (0, 2 * STATE))[None]
    taps = jnp.concatenate([taps, skip_row, jnp.zeros((3, WIDE + 2 * STATE), F32)], 0)
    pad = pltpu.VMEM((TILES + 2, TOKENS + 8, 128), F32)
    message, half = call(
        state_kernel,
        (like((RUNS, CUT + 8, 128), BF16), like((PEERS, HALF, 128), BF16)),
        10**9,
        2 * 10**6,
        [pad],
    )(got, taps, *handed)
    slices = lax.all_to_all(message, "seq", split_axis=0, concat_axis=0, tiled=True)
    other = lax.ppermute(half, "core", [(0, 1), (1, 0)])
    vmem = pl.BlockSpec(memory_space=pltpu.VMEM)
    part, c_conv, scale = call(
        local_kernel,
        (
            like((SPANS, SPAN, WIDE), F32),
            like((SPANS, SPAN, STATE), BF16),
            like((SPANS, SPAN, WIDE), F32),
        ),
        10**9,
        8 * 10**6,
        [pad],
        in_specs=[pl.BlockSpec(memory_space=pltpu.SMEM)] + [vmem] * (3 + MEMBERS),
    )(core.astype(jnp.int32).reshape(1), got, other, taps, *handed)
    chained = call(chain_kernel, like((RUNS, CUT, 128), BF16), 10**7, 10**6)(slices)
    state = lax.all_to_all(chained, "seq", split_axis=0, concat_axis=0, tiled=True)
    hbm = pl.BlockSpec(memory_space=pltpu.HBM)
    values = call(
        finish_kernel,
        like((TOKENS, WIDE), BF16),
        10**8,
        3 * 10**6,
        [pltpu.VMEM((TOKENS, WIDE), BF16), pltpu.SemaphoreType.DMA((SPANS,))],
        out_specs=hbm,
    )(part, c_conv, scale, state.reshape(TILES, STATE, 128))
    home = lax.all_to_all(
        values.reshape(PEERS, ROWS, WIDE), ("core", "head"), split_axis=0, concat_axis=0, tiled=True
    )
    width = HEADS * HEAD_DIM
    gate = call(gate_kernel, like((ROWS, width), F32), 10**7, 2 * 10**6)(z_stream)
    return call(
        norm_kernel,
        like((ROWS, width), BF16),
        10**7,
        2 * 10**6,
        [pltpu.VMEM((ROWS, width), BF16), pltpu.SemaphoreType.DMA((GROUPS,))],
        out_specs=hbm,
    )(home, gate, norm_gain.reshape(1, width))


def solution(mesh):
    finer = Mesh(mesh.devices.reshape(RUNS, CORES, RING), ("seq", "core", "head"))
    rows = P(("seq", "core", "head"), None)
    in_specs = (rows,) * 6 + (P(None, "head"),) * 3 + (P("head"), P())
    return jax.shard_map(shards, mesh=finer, in_specs=in_specs, out_specs=rows, check_vma=False)
```

time: 98.5 us -> 96.2 us (0.977)
  blocking collectives: 14.4 us -> 20.3 us
  waiting for transfers between devices: 32 us -> 27.6 us
  starting transfers between devices: 38.1 us -> 35.9 us
  Pallas kernels: 11.4 us -> 9.73 us
    all_to_all x1, blocking collectives: 14.4 us -> 20.3 us  [shards(): lax.all_to_all(message, 'seq', split_axis=0, concat_axis=0, tiled=True)]
    all_to_all x1, starting transfers between devices: 10 us -> 5.23 us  [shards(): lax.all_to_all(chained, 'seq', split_axis=0, concat_axis=0, tiled=True)]
    all_to_all x1, waiting for transfers between devices: 6.28 us -> 2.71 us  [shards(): lax.all_to_all(chained, 'seq', split_axis=0, concat_axis=0, tiled=True)]
    ppermute x0 -> x1, starting transfers between devices: none -> 2.58 us  [shards(): other = lax.ppermute(half, 'core', [(0, 1), (1, 0)])]
    pallas_call x3 -> x4, Pallas kernels: 5.22 us -> 3.83 us  [the longest x1 1.65 us: shards(): call(state_kernel, (like((RUNS, CUT + 8, 128), BF16), like((PEERS, HALF,...]
    ppermute x3, waiting for transfers between devices: 4.89 us -> 3.61 us  [shards(): handed.append(lax.ppermute(led[member], everyone, pairs))]
  transfers between devices with their start and end apart: 10 -> 11, of which waited for: 6 -> 7; matrix products, arithmetic and copies ran while one was open for 0% -> 0% of each run, Pallas kernels for 4% -> 3%
where the time goes in v3:
time: 96.2 us; the launch traced here: 95.6 us
  starting transfers between devices  35.9 us (37%)
  waiting for transfers between devices  27.6 us (29%)
  blocking collectives  20.3 us (21%)
  Pallas kernels  9.73 us (10%)
  local copies, waits for them, and re-layouts  1.7 us (2%)
    all_to_all x1, blocking collectives, shards(): lax.all_to_all(message, 'seq', split_axis=0, concat_axis=0, tiled=True)  20.3 us
    all_to_all x1, waiting for transfers between devices, shards(): lax.all_to_all(values.reshape(PEERS, ROWS, WIDE), ('core', 'head'), split...  14.5 us
    all_to_all x1, starting transfers between devices, shards(): lax.all_to_all(packed, ('core', 'head'), split_axis=0, concat_axis=0, til...  12 us
    all_to_all x1, starting transfers between devices, shards(): lax.all_to_all(values.reshape(PEERS, ROWS, WIDE), ('core', 'head'), split...  7.05 us
    ppermute x3, starting transfers between devices, shards(): handed.append(lax.ppermute(led[member], everyone, pairs))  6.41 us
    all_to_all x1, waiting for transfers between devices, shards(): lax.all_to_all(packed, ('core', 'head'), split_axis=0, concat_axis=0, til...  5.79 us
    all_to_all x1, starting transfers between devices, shards(): lax.all_to_all(chained, 'seq', split_axis=0, concat_axis=0, tiled=True)  5.23 us
    ppermute x3, waiting for transfers between devices, shards(): handed.append(lax.ppermute(led[member], everyone, pairs))  3.61 us
  transfers between devices with their start and end apart: 11, of which 7 were waited for; matrix products, arithmetic and copies ran while one was open for 0% of the time, Pallas kernels for 3%

profile of v3, /device:TPU:1, one launch (start us, length us, event | category | flops | bytes accessed | tf_op | source)
XLA Modules:
  0.0 95.6 jit_solution(2041010763319377866)
XLA Ops:
  0.0 0.0 copy-start
  0.0 2.2 %shard_map.109 = (bf16[16,184,128]{2,1,0:T(8,128)(2,1)}, bf16[4,48,128]{2,1,0:T(8,128)(2,1)}, bf16[4,48,128]{2,1,0:T(8,128)(2,1)}, bf16[4,48,128]{2,1,0:T(8,128)(2,1)}, bf16[4,48,128]{2,1,0:T(8,128)(2,1)}) custom-call(bf16[32,8192]{1,0:T(8,128)(2,1)} %x_hbm.1, bf16[32,1024]{1,0:T(8,128)(2,1)} %b_hbm.1, bf16[32,1024]{1,0:T(8,128)(2,1)} %c_hbm.1, ...), custom_call_target="tpu_custom_call" | custom-call | bytes 1507328 | tf_op jit(solution)/shard_map/pallas_call | solution.py:305
  2.2 0.0 copy-start.8
  2.2 0.0 copy-start.7
  2.2 0.0 copy-start.6
  2.3 0.0 copy-start.5
  2.3 12.0 %all-to-all-start = ((bf16[16,184,128]{2,1,0:T(8,128)(2,1)}), bf16[16,184,128]{2,1,0:T(8,128)(2,1)S(1)}, u32[]{:S(2)}, u32[]{:S(2)}) async-start(bf16[16,184,128]{2,1,0:T(8,128)(2,1)} %get-tuple-element.15), calls=%async_computation | async-start | bytes 1507328 | tf_op jit(solution)/shard_map/all_to_all | solution.py:314
  14.2 0.0 copy-done.8
  14.3 0.7 collective-permute-start
  14.9 0.0 copy-done.7
  14.9 0.7 collective-permute-start.1
  15.6 0.0 copy-done.6
  15.6 0.7 collective-permute-start.2
  16.3 0.0 copy-done.5
  16.3 0.7 collective-permute-start.3
  17.0 0.0 copy-done
  17.0 0.0 copy-start.3
  17.0 0.0 copy-start.4
  17.0 0.6 copy-done.3
  17.7 0.0 copy-done.4
  17.7 0.0 copy-start.9
  17.7 0.7 copy-done.9
  18.3 0.1 dynamic_slice.7
  18.4 0.1 broadcast_in_dim.9
  18.5 0.1 reshape.16
  18.6 0.1 pad.7.clone
  18.7 0.0 collective-permute-done
  18.7 0.0 collective-permute-done.1
  18.7 0.0 collective-permute-done.2
  18.7 0.0 collective-permute-done.3
  18.7 3.3 %collective-permute-start.4 = (bf16[48,128]{1,0:T(8,128)(2,1)S(1)}, bf16[48,128]{1,0:T(8,128)(2,1)S(1)}, u32[]{:S(2)}, u32[]{:S(2)}) collective-permute-start(bf16[48,128]{1,0:T(8,128)(2,1)S(1)} %get-tuple-element.27), channel_id=1, source_target_pairs={{0,1},{4,5},{8,9},{12,13},{16,17},{20,21},{24,25},{28,29},{32,33},... | collective-permute-start | bytes 36872 | tf_op jit(solution)/shard_map/ppermute | solution.py:324
  22.0 1.6 %collective-permute-start.5 = (bf16[48,128]{1,0:T(8,128)(2,1)S(1)}, bf16[48,128]{1,0:T(8,128)(2,1)S(1)}, u32[]{:S(2)}, u32[]{:S(2)}) collective-permute-start(bf16[48,128]{1,0:T(8,128)(2,1)S(1)} %get-tuple-element.26), channel_id=1, source_target_pairs={{0,2},{4,6},{8,10},{12,14},{16,18},{20,22},{24,26},{28,30},{32,34}... | collective-permute-start | bytes 36872 | tf_op jit(solution)/shard_map/ppermute | solution.py:324
  23.6 1.6 %collective-permute-start.6 = (bf16[48,128]{1,0:T(8,128)(2,1)S(1)}, bf16[48,128]{1,0:T(8,128)(2,1)S(1)}, u32[]{:S(2)}, u32[]{:S(2)}) collective-permute-start(bf16[48,128]{1,0:T(8,128)(2,1)S(1)} %get-tuple-element.25), channel_id=1, source_target_pairs={{0,3},{4,7},{8,11},{12,15},{16,19},{20,23},{24,27},{28,31},{32,35}... | collective-permute-start | bytes 36872 | tf_op jit(solution)/shard_map/ppermute | solution.py:324
  25.2 0.1 maximum_maximum_fusion.taps_ref
  25.2 2.5 %collective-permute-done.4.rest_1_ = bf16[48,128]{1,0:T(8,128)(2,1)S(1)} collective-permute-done((bf16[48,128]{1,0:T(8,128)(2,1)S(1)}, bf16[48,128]{1,0:T(8,128)(2,1)S(1)}, u32[]{:S(2)}, u32[]{:S(2)}) %collective-permute-start.4) | collective-permute-done | bytes 12320 | tf_op jit(solution)/shard_map/ppermute | solution.py:324
  27.8 0.5 collective-permute-done.5.rest_2_
  28.2 0.6 collective-permute-done.6.rest_3_
  28.8 5.8 %all-to-all-done.r_ref = bf16[16,184,128]{2,1,0:T(8,128)(2,1)S(1)} async-done(((bf16[16,184,128]{2,1,0:T(8,128)(2,1)}), bf16[16,184,128]{2,1,0:T(8,128)(2,1)S(1)}, u32[]{:S(2)}, u32[]{:S(2)}) %all-to-all-start) | async-done | bytes 753696 | tf_op jit(solution)/shard_map/all_to_all | solution.py:314
  34.6 1.6 %shard_map.110 = (bf16[32,24,128]{2,1,0:T(8,128)(2,1)S(1)}, bf16[16,16,128]{2,1,0:T(8,128)(2,1)S(1)}) custom-call(bf16[16,184,128]{2,1,0:T(8,128)(2,1)S(1)} %all-to-all-done.r_ref, f32[8,768]{1,0:T(8,128)S(1)} %maximum_maximum_fusion.taps_ref, bf16[4,48,128]{2,1,0:T(8,128)(2,1)S(1)} %add_add_fusion.rest_0_, ...), custom_call_target="tpu_custom_call" | custom-call | flops 1000000000 | bytes 2000000 | tf_op jit(solution)/shard_map/pallas_call | solution.py:331
  36.3 20.3 %all_to_all.20.all_ref = bf16[32,24,128]{2,1,0:T(8,128)(2,1)S(1)} all-to-all(bf16[32,24,128]{2,1,0:T(8,128)(2,1)S(1)} %get-tuple-element.24), channel_id=1, replica_groups=mesh['seq'=32,'core'=2,'head'=8] {'seq'}, dimensions={0} | all-to-all | bytes 393216 | tf_op jit(solution)/shard_map/all_to_all | solution.py:338
  56.6 0.7 shard_map.112
  57.3 5.2 %all-to-all-start.2 = ((bf16[32,16,128]{2,1,0:T(8,128)(2,1)}), bf16[32,16,128]{2,1,0:T(8,128)(2,1)S(1)}, u32[]{:S(2)}, u32[]{:S(2)}) async-start(bf16[32,16,128]{2,1,0:T(8,128)(2,1)} %shard_map.112), calls=%async_computation.2 | async-start | bytes 262144 | tf_op jit(solution)/shard_map/all_to_all | solution.py:354
  62.6 2.6 %collective-permute-start.7 = (bf16[16,16,128]{2,1,0:T(8,128)(2,1)S(1)}, bf16[16,16,128]{2,1,0:T(8,128)(2,1)S(1)}, u32[]{:S(2)}, u32[]{:S(2)}) collective-permute-start(bf16[16,16,128]{2,1,0:T(8,128)(2,1)S(1)} %get-tuple-element.20), channel_id=1, source_target_pairs={{0,8},{8,0},{1,9},{9,1},{2,10},{10,2},{3,11},{11,3},{4,12},{12,4},... | collective-permute-start | bytes 196616 | tf_op jit(solution)/shard_map/ppermute | solution.py:339
  65.2 0.9 collective-permute-done.7.other_ref
  66.1 3.0 %shard_map.111 = (f32[4,128,512]{2,1,0:T(8,128)S(1)}, bf16[4,128,128]{2,1,0:T(8,128)(2,1)S(1)}, f32[4,128,512]{2,1,0:T(8,128)S(1)}) custom-call(s32[1]{0:T(128)} %bitcast.core_ref, bf16[16,184,128]{2,1,0:T(8,128)(2,1)S(1)} %all-to-all-done.r_ref, bf16[16,16,128]{2,1,0:T(8,128)(2,1)S(1)} %collective-permute-done.7.other_ref, ...), custom_call_target="tpu_custom_call" | custom-call | flops 1000000000 | bytes 8000000 | tf_op jit(solution)/shard_map/pallas_call | solution.py:341
  69.0 2.7 %all-to-all-done.2 = bf16[32,16,128]{2,1,0:T(8,128)(2,1)S(1)} async-done(((bf16[32,16,128]{2,1,0:T(8,128)(2,1)}), bf16[32,16,128]{2,1,0:T(8,128)(2,1)S(1)}, u32[]{:S(2)}, u32[]{:S(2)}) %all-to-all-start.2) | async-done | bytes 131104 | tf_op jit(solution)/shard_map/all_to_all | solution.py:354
  71.7 1.0 %shard_map.113 = bf16[512,512]{1,0:T(8,128)(2,1)} custom-call(f32[4,128,512]{2,1,0:T(8,128)S(1)} %get-tuple-element.21.part_ref, bf16[4,128,128]{2,1,0:T(8,128)(2,1)S(1)} %get-tuple-element.22.c_ref, f32[4,128,512]{2,1,0:T(8,128)S(1)} %get-tuple-element.23.scale_ref, bf16[4,128,128]{2,1,0:T(8,128)(2,1)S(1)} %bitcast.9), custom_call_target="tpu_custom_call" | custom-call | flops 100000000 | bytes 3000000 | tf_op jit(solution)/shard_map/pallas_call | solution.py:356
  72.8 0.0 copy-start.2
  72.8 0.0 copy-start.1
  72.8 7.0 %all-to-all-start.3 = ((bf16[16,32,512]{2,1,0:T(8,128)(2,1)}), bf16[16,32,512]{2,1,0:T(8,128)(2,1)S(1)}, u32[]{:S(2)}, u32[]{:S(2)}) async-start(bf16[16,32,512]{2,1,0:T(8,128)(2,1)} %bitcast.5), calls=%async_computation.3 | async-start | bytes 1048576 | tf_op jit(solution)/shard_map/all_to_all | solution.py:364
  79.8 0.0 copy-done.2
  79.9 0.0 copy-done.1
  79.9 0.2 shard_map.114.gate_ref
  80.1 14.5 %all-to-all-done.3.values_ref = bf16[16,32,512]{2,1,0:T(8,128)(2,1)S(1)} async-done(((bf16[16,32,512]{2,1,0:T(8,128)(2,1)}), bf16[16,32,512]{2,1,0:T(8,128)(2,1)S(1)}, u32[]{:S(2)}, u32[]{:S(2)}) %all-to-all-start.3) | async-done | bytes 524320 | tf_op jit(solution)/shard_map/all_to_all | solution.py:364
  94.6 1.0 %shard_map.115 = bf16[32,8192]{1,0:T(8,128)(2,1)} custom-call(bf16[16,32,512]{2,1,0:T(8,128)(2,1)S(1)} %all-to-all-done.3.values_ref, f32[32,8192]{1,0:T(8,128)S(1)} %shard_map.114.gate_ref, bf16[1,8192]{1,0:T(2,128)(2,1)S(1)} %reshape.19.gain_ref), custom_call_target="tpu_custom_call" | custom-call | flops 10000000 | bytes 2000000 | tf_op jit(solution)/shard_map/pallas_call | solution.py:369
  (8 shorter events, 0.1 us)
Async XLA Ops:
  0.0 17.0 %copy-start = (bf16[4,1024]{1,0:T(4,128)(2,1)S(1)}, bf16[4,1024]{1,0:T(4,128)(2,1)}, u32[]{:S(2)}) copy-start(bf16[4,1024]{1,0:T(4,128)(2,1)} %param.17) | copy-start | bytes 24580
  2.2 12.0 %copy-start.8 = (bf16[4,48,128]{2,1,0:T(8,128)(2,1)S(1)}, bf16[4,48,128]{2,1,0:T(8,128)(2,1)}, u32[]{:S(2)}) copy-start(bf16[4,48,128]{2,1,0:T(8,128)(2,1)} %get-tuple-element.16) | copy-start | bytes 147460
  2.2 12.7 %copy-start.7 = (bf16[4,48,128]{2,1,0:T(8,128)(2,1)S(1)}, bf16[4,48,128]{2,1,0:T(8,128)(2,1)}, u32[]{:S(2)}) copy-start(bf16[4,48,128]{2,1,0:T(8,128)(2,1)} %get-tuple-element.17) | copy-start | bytes 147460
  2.2 13.4 %copy-start.6 = (bf16[4,48,128]{2,1,0:T(8,128)(2,1)S(1)}, bf16[4,48,128]{2,1,0:T(8,128)(2,1)}, u32[]{:S(2)}) copy-start(bf16[4,48,128]{2,1,0:T(8,128)(2,1)} %get-tuple-element.18) | copy-start | bytes 147460
  2.3 14.0 %copy-start.5 = (bf16[4,48,128]{2,1,0:T(8,128)(2,1)S(1)}, bf16[4,48,128]{2,1,0:T(8,128)(2,1)}, u32[]{:S(2)}) copy-start(bf16[4,48,128]{2,1,0:T(8,128)(2,1)} %get-tuple-element.19) | copy-start | bytes 147460
  2.3 32.4 %all-to-all-start = ((bf16[16,184,128]{2,1,0:T(8,128)(2,1)}), bf16[16,184,128]{2,1,0:T(8,128)(2,1)S(1)}, u32[]{:S(2)}, u32[]{:S(2)}) async-start(bf16[16,184,128]{2,1,0:T(8,128)(2,1)} %get-tuple-element.15), calls=%async_computation | async-start | bytes 1507328 | tf_op jit(solution)/shard_map/all_to_all | solution.py:314
  14.3 4.4 %collective-permute-start = (bf16[4,48,128]{2,1,0:T(8,128)(2,1)S(1)}, bf16[4,48,128]{2,1,0:T(8,128)(2,1)S(1)}, u32[]{:S(2)}, u32[]{:S(2)}) collective-permute-start(bf16[4,48,128]{2,1,0:T(8,128)(2,1)S(1)} %copy-done.8), channel_id=1, source_target_pairs={{15,16},{31,32},{47,48},{63,64},{79,80},{95,96},{111,112},{127,128... | collective-permute-start | bytes 147464 | tf_op jit(solution)/shard_map/ppermute | solution.py:319
  14.9 3.7 %collective-permute-start.1 = (bf16[4,48,128]{2,1,0:T(8,128)(2,1)S(1)}, bf16[4,48,128]{2,1,0:T(8,128)(2,1)S(1)}, u32[]{:S(2)}, u32[]{:S(2)}) collective-permute-start(bf16[4,48,128]{2,1,0:T(8,128)(2,1)S(1)} %copy-done.7), channel_id=1, source_target_pairs={{15,20},{31,36},{47,52},{63,68},{79,84},{95,100},{111,116},{127,13... | collective-permute-start | bytes 147464 | tf_op jit(solution)/shard_map/ppermute | solution.py:319
  15.6 3.1 %collective-permute-start.2 = (bf16[4,48,128]{2,1,0:T(8,128)(2,1)S(1)}, bf16[4,48,128]{2,1,0:T(8,128)(2,1)S(1)}, u32[]{:S(2)}, u32[]{:S(2)}) collective-permute-start(bf16[4,48,128]{2,1,0:T(8,128)(2,1)S(1)} %copy-done.6), channel_id=1, source_target_pairs={{15,24},{31,40},{47,56},{63,72},{79,88},{95,104},{111,120},{127,13... | collective-permute-start | bytes 147464 | tf_op jit(solution)/shard_map/ppermute | solution.py:319
  16.3 2.4 %collective-permute-start.3 = (bf16[4,48,128]{2,1,0:T(8,128)(2,1)S(1)}, bf16[4,48,128]{2,1,0:T(8,128)(2,1)S(1)}, u32[]{:S(2)}, u32[]{:S(2)}) collective-permute-start(bf16[4,48,128]{2,1,0:T(8,128)(2,1)S(1)} %copy-done.5), channel_id=1, source_target_pairs={{15,28},{31,44},{47,60},{63,76},{79,92},{95,108},{111,124},{127,14... | collective-permute-start | bytes 147464 | tf_op jit(solution)/shard_map/ppermute | solution.py:319
  17.0 0.7 copy-start.3
  17.0 0.7 copy-start.4
  17.7 0.7 copy-start.9
  18.7 9.0 %collective-permute-start.4 = (bf16[48,128]{1,0:T(8,128)(2,1)S(1)}, bf16[48,128]{1,0:T(8,128)(2,1)S(1)}, u32[]{:S(2)}, u32[]{:S(2)}) collective-permute-start(bf16[48,128]{1,0:T(8,128)(2,1)S(1)} %get-tuple-element.27), channel_id=1, source_target_pairs={{0,1},{4,5},{8,9},{12,13},{16,17},{20,21},{24,25},{28,29},{32,33},... | collective-permute-start | bytes 36872 | tf_op jit(solution)/shard_map/ppermute | solution.py:324
  22.0 6.2 %collective-permute-start.5 = (bf16[48,128]{1,0:T(8,128)(2,1)S(1)}, bf16[48,128]{1,0:T(8,128)(2,1)S(1)}, u32[]{:S(2)}, u32[]{:S(2)}) collective-permute-start(bf16[48,128]{1,0:T(8,128)(2,1)S(1)} %get-tuple-element.26), channel_id=1, source_target_pairs={{0,2},{4,6},{8,10},{12,14},{16,18},{20,22},{24,26},{28,30},{32,34}... | collective-permute-start | bytes 36872 | tf_op jit(solution)/shard_map/ppermute | solution.py:324
  23.6 5.3 %collective-permute-start.6 = (bf16[48,128]{1,0:T(8,128)(2,1)S(1)}, bf16[48,128]{1,0:T(8,128)(2,1)S(1)}, u32[]{:S(2)}, u32[]{:S(2)}) collective-permute-start(bf16[48,128]{1,0:T(8,128)(2,1)S(1)} %get-tuple-element.25), channel_id=1, source_target_pairs={{0,3},{4,7},{8,11},{12,15},{16,19},{20,23},{24,27},{28,31},{32,35}... | collective-permute-start | bytes 36872 | tf_op jit(solution)/shard_map/ppermute | solution.py:324
  57.3 14.4 %all-to-all-start.2 = ((bf16[32,16,128]{2,1,0:T(8,128)(2,1)}), bf16[32,16,128]{2,1,0:T(8,128)(2,1)S(1)}, u32[]{:S(2)}, u32[]{:S(2)}) async-start(bf16[32,16,128]{2,1,0:T(8,128)(2,1)} %shard_map.112), calls=%async_computation.2 | async-start | bytes 262144 | tf_op jit(solution)/shard_map/all_to_all | solution.py:354
  62.6 3.5 %collective-permute-start.7 = (bf16[16,16,128]{2,1,0:T(8,128)(2,1)S(1)}, bf16[16,16,128]{2,1,0:T(8,128)(2,1)S(1)}, u32[]{:S(2)}, u32[]{:S(2)}) collective-permute-start(bf16[16,16,128]{2,1,0:T(8,128)(2,1)S(1)} %get-tuple-element.20), channel_id=1, source_target_pairs={{0,8},{8,0},{1,9},{9,1},{2,10},{10,2},{3,11},{11,3},{4,12},{12,4},... | collective-permute-start | bytes 196616 | tf_op jit(solution)/shard_map/ppermute | solution.py:339
  72.8 7.1 %copy-start.2 = (bf16[8192]{0:T(1024)(128)(2,1)S(1)}, bf16[8192]{0:T(1024)(128)(2,1)}, u32[]{:S(2)}) copy-start(bf16[8192]{0:T(1024)(128)(2,1)} %param.21) | copy-start | bytes 49156
  72.8 7.1 %copy-start.1 = (bf16[32,8192]{1,0:T(8,128)(2,1)S(1)}, bf16[32,8192]{1,0:T(8,128)(2,1)}, u32[]{:S(2)}) copy-start(bf16[32,8192]{1,0:T(8,128)(2,1)} %z_ref.1) | copy-start | bytes 1572868
  72.8 21.8 %all-to-all-start.3 = ((bf16[16,32,512]{2,1,0:T(8,128)(2,1)}), bf16[16,32,512]{2,1,0:T(8,128)(2,1)S(1)}, u32[]{:S(2)}, u32[]{:S(2)}) async-start(bf16[16,32,512]{2,1,0:T(8,128)(2,1)} %bitcast.5), calls=%async_computation.3 | async-start | bytes 1048576 | tf_op jit(solution)/shard_map/all_to_all | solution.py:364

commit v4 on v3

--- a/solution.py
+++ b/solution.py
@@ -25,7 +25,8 @@
 TILES = WIDE // 128
 LEADERS = 4
 MEMBERS = PEERS // LEADERS
-RIM = 8 * (TILES + 2)
+BORDER = 3
+RIM = 8 * BORDER
 RUNS = 32
 HALF = ROWS // CORES
 PACK = ROWS * (TILES + 1) + HALF + MINE
@@ -53,6 +54,11 @@
 def silu(x):
     half = 0.5 * x
     return half * jnp.tanh(half) + half
+
+
+def member_of(leader, member):
+    core, side = divmod(leader, 2)
+    return core, member if side else RING - 1 - member
 
 
 def pack_kernel(x_hbm, b_hbm, c_hbm, dt_hbm, decay_hbm, out_ref, *rest):
@@ -84,15 +90,16 @@
             for tile in range(TILES):
                 column = ring * CORES * WIDE + core * WIDE + tile * 128
                 out_ref[core * RING + ring, tile * ROWS : (tile + 1) * ROWS, :] = x_ref[:, column : column + 128]
+    rows = slice(ROWS - 16, ROWS)
     for leader in range(LEADERS):
         for member in range(MEMBERS):
-            core, ring = divmod(leader * MEMBERS + member, RING)
+            core, ring = member_of(leader, member)
             column = (ring * CORES + core) * WIDE
-            rows = slice(ROWS - 16, ROWS)
             pieces = [x_ref[rows, column + tile * 128 : column + (tile + 1) * 128] for tile in range(TILES)]
             pieces += [ref[rows, ring * 128 : (ring + 1) * 128] for ref in (b_ref, c_ref)]
-            whole = jnp.concatenate([piece.astype(F32)[8:] for piece in pieces], 0)
-            rims[leader][member] = whole.astype(BF16)
+            pieces = [piece.astype(F32) for piece in pieces]
+            whole = [piece[16 - BORDER + token :][:1] for token in range(BORDER) for piece in pieces + pieces[:2]]
+            rims[leader][member] = jnp.concatenate(whole, 0).astype(BF16)
 
 
 def raw(r_ref, span, tile):
@@ -105,11 +112,12 @@
 
 
 def fill(r_ref, rims, pad_ref, tiles):
+    rim = rims[0][0].astype(F32)
+    for ref in rims[1:]:
+        rim = rim + ref[...].astype(F32)
     for tile in tiles:
-        rows = slice(tile * 8, (tile + 1) * 8)
-        edge = rims[0][0, rows, :].astype(F32)
-        for ref in rims[1:]:
-            edge = edge + ref[rows, :].astype(F32)
+        tokens = [rim[token * 8 + tile : token * 8 + tile + 1] for token in range(BORDER)]
+        edge = jnp.concatenate([jnp.zeros((8 - BORDER, 128), F32)] + tokens, 0)
         pad_ref[tile, 0:8, :] = edge
         if tile > TILES:
             continue
@@ -314,13 +322,14 @@
     got = lax.all_to_all(packed, ("core", "head"), split_axis=0, concat_axis=0, tiled=True)
     everyone = ("seq", "core", "head")
     led = None
+    place = [[core * RING + ring for core, ring in (member_of(i, j) for j in range(MEMBERS))] for i in range(LEADERS)]
     for leader, rim in enumerate(rims):
-        pairs = [(i * PEERS + PEERS - 1, (i + 1) * PEERS + leader * MEMBERS) for i in range(RUNS - 1)]
+        pairs = [(i * PEERS + PEERS - 1, (i + 1) * PEERS + place[leader][0]) for i in range(RUNS - 1)]
         came = lax.ppermute(rim, everyone, pairs)
         led = came if led is None else led + came
     handed = [led]
     for member in range(1, MEMBERS):
-        pairs = [(i, i + member) for i in range(0, RUNS * PEERS, MEMBERS)]
+        pairs = [(i * PEERS + devices[0], i * PEERS + devices[member]) for i in range(RUNS) for devices in place]
         handed.append(lax.ppermute(led[member], everyone, pairs))
     taps_x = lax.dynamic_slice_in_dim(kernel_x, core * WIDE, WIDE, 1)
     skip = jnp.repeat(lax.dynamic_slice_in_dim(skip_gain, core * MINE, MINE), HEAD_DIM)

time: 96.2 us -> 95.4 us (level)
  no operation moved by 1% of the time
where the time goes in v4:
time: 95.4 us; the launch traced here: 94.7 us
  starting transfers between devices  35.8 us (38%)
  waiting for transfers between devices  27.5 us (29%)
  blocking collectives  19.6 us (21%)
  Pallas kernels  9.72 us (10%)
  local copies, waits for them, and re-layouts  1.7 us (2%)
    all_to_all x1, blocking collectives, shards(): lax.all_to_all(message, 'seq', split_axis=0, concat_axis=0, tiled=True)  19.6 us
    all_to_all x1, waiting for transfers between devices, shards(): lax.all_to_all(values.reshape(PEERS, ROWS, WIDE), ('core', 'head'), split...  14.5 us
    all_to_all x1, starting transfers between devices, shards(): lax.all_to_all(packed, ('core', 'head'), split_axis=0, concat_axis=0, til...  12 us
    all_to_all x1, starting transfers between devices, shards(): lax.all_to_all(values.reshape(PEERS, ROWS, WIDE), ('core', 'head'), split...  6.53 us
    ppermute x3, starting transfers between devices, shards(): handed.append(lax.ppermute(led[member], everyone, pairs))  6.41 us
    all_to_all x1, waiting for transfers between devices, shards(): lax.all_to_all(packed, ('core', 'head'), split_axis=0, concat_axis=0, til...  5.8 us
    all_to_all x1, starting transfers between devices, shards(): lax.all_to_all(chained, 'seq', split_axis=0, concat_axis=0, tiled=True)  5.45 us
    ppermute x3, waiting for transfers between devices, shards(): handed.append(lax.ppermute(led[member], everyone, pairs))  3.63 us
  transfers between devices with their start and end apart: 11, of which 7 were waited for; matrix products, arithmetic and copies ran while one was open for 0% of the time, Pallas kernels for 3%

profile of v4, /device:TPU:1, one launch (start us, length us, event | category | flops | bytes accessed | tf_op | source)
XLA Modules:
  0.0 94.7 jit_solution(5026947979129490247)
XLA Ops:
  0.0 0.0 copy-start
  0.0 2.2 %shard_map.109 = (bf16[16,184,128]{2,1,0:T(8,128)(2,1)}, bf16[4,24,128]{2,1,0:T(8,128)(2,1)}, bf16[4,24,128]{2,1,0:T(8,128)(2,1)}, bf16[4,24,128]{2,1,0:T(8,128)(2,1)}, bf16[4,24,128]{2,1,0:T(8,128)(2,1)}) custom-call(bf16[32,8192]{1,0:T(8,128)(2,1)} %x_hbm.1, bf16[32,1024]{1,0:T(8,128)(2,1)} %b_hbm.1, bf16[32,1024]{1,0:T(8,128)(2,1)} %c_hbm.1, ...), custom_call_target="tpu_custom_call" | custom-call | bytes 1507328 | tf_op jit(solution)/shard_map/pallas_call | solution.py:313
  2.2 0.0 copy-start.8
  2.2 0.0 copy-start.7
  2.2 0.0 copy-start.6
  2.2 0.0 copy-start.5
  2.2 12.0 %all-to-all-start = ((bf16[16,184,128]{2,1,0:T(8,128)(2,1)}), bf16[16,184,128]{2,1,0:T(8,128)(2,1)S(1)}, u32[]{:S(2)}, u32[]{:S(2)}) async-start(bf16[16,184,128]{2,1,0:T(8,128)(2,1)} %get-tuple-element.15), calls=%async_computation | async-start | bytes 1507328 | tf_op jit(solution)/shard_map/all_to_all | solution.py:322
  14.2 0.0 copy-done.8
  14.2 0.7 collective-permute-start
  14.9 0.0 copy-done.7
  14.9 0.7 collective-permute-start.1
  15.6 0.0 copy-done.6
  15.6 0.7 collective-permute-start.2
  16.3 0.0 copy-done.5
  16.3 0.7 collective-permute-start.3
  17.0 0.0 copy-done
  17.0 0.0 copy-start.3
  17.0 0.0 copy-start.4
  17.0 0.6 copy-done.3
  17.6 0.0 copy-done.4
  17.7 0.0 copy-start.9
  17.7 0.7 copy-done.9
  18.3 0.1 dynamic_slice.7
  18.4 0.1 broadcast_in_dim.9
  18.5 0.1 reshape.16
  18.6 0.1 pad.7.clone
  18.6 0.0 collective-permute-done
  18.6 0.0 collective-permute-done.1
  18.6 0.0 collective-permute-done.2
  18.7 0.0 collective-permute-done.3
  18.7 3.3 %collective-permute-start.4 = (bf16[24,128]{1,0:T(8,128)(2,1)S(1)}, bf16[24,128]{1,0:T(8,128)(2,1)S(1)}, u32[]{:S(2)}, u32[]{:S(2)}) collective-permute-start(bf16[24,128]{1,0:T(8,128)(2,1)S(1)} %get-tuple-element.27), channel_id=1, source_target_pairs={{7,6},{0,1},{15,14},{8,9},{23,22},{16,17},{31,30},{24,25},{39,38},... | collective-permute-start | bytes 18440 | tf_op jit(solution)/shard_map/ppermute | solution.py:333
  22.0 1.6 %collective-permute-start.5 = (bf16[24,128]{1,0:T(8,128)(2,1)S(1)}, bf16[24,128]{1,0:T(8,128)(2,1)S(1)}, u32[]{:S(2)}, u32[]{:S(2)}) collective-permute-start(bf16[24,128]{1,0:T(8,128)(2,1)S(1)} %get-tuple-element.26), channel_id=1, source_target_pairs={{7,5},{0,2},{15,13},{8,10},{23,21},{16,18},{31,29},{24,26},{39,37}... | collective-permute-start | bytes 18440 | tf_op jit(solution)/shard_map/ppermute | solution.py:333
  23.6 1.6 %collective-permute-start.6 = (bf16[24,128]{1,0:T(8,128)(2,1)S(1)}, bf16[24,128]{1,0:T(8,128)(2,1)S(1)}, u32[]{:S(2)}, u32[]{:S(2)}) collective-permute-start(bf16[24,128]{1,0:T(8,128)(2,1)S(1)} %get-tuple-element.25), channel_id=1, source_target_pairs={{7,4},{0,3},{15,12},{8,11},{23,20},{16,19},{31,28},{24,27},{39,36}... | collective-permute-start | bytes 18440 | tf_op jit(solution)/shard_map/ppermute | solution.py:333
  25.1 0.1 maximum_maximum_fusion.taps_ref
  25.2 2.9 %collective-permute-done.4.rest_1_ = bf16[24,128]{1,0:T(8,128)(2,1)S(1)} collective-permute-done((bf16[24,128]{1,0:T(8,128)(2,1)S(1)}, bf16[24,128]{1,0:T(8,128)(2,1)S(1)}, u32[]{:S(2)}, u32[]{:S(2)}) %collective-permute-start.4) | collective-permute-done | bytes 6176 | tf_op jit(solution)/shard_map/ppermute | solution.py:333
  28.1 0.2 collective-permute-done.5.rest_2_
  28.4 0.5 collective-permute-done.6.rest_3_
  28.8 5.8 %all-to-all-done.r_ref = bf16[16,184,128]{2,1,0:T(8,128)(2,1)S(1)} async-done(((bf16[16,184,128]{2,1,0:T(8,128)(2,1)}), bf16[16,184,128]{2,1,0:T(8,128)(2,1)S(1)}, u32[]{:S(2)}, u32[]{:S(2)}) %all-to-all-start) | async-done | bytes 753696 | tf_op jit(solution)/shard_map/all_to_all | solution.py:322
  34.6 1.6 %shard_map.110 = (bf16[32,24,128]{2,1,0:T(8,128)(2,1)S(1)}, bf16[16,16,128]{2,1,0:T(8,128)(2,1)S(1)}) custom-call(bf16[16,184,128]{2,1,0:T(8,128)(2,1)S(1)} %all-to-all-done.r_ref, f32[8,768]{1,0:T(8,128)S(1)} %maximum_maximum_fusion.taps_ref, bf16[4,24,128]{2,1,0:T(8,128)(2,1)S(1)} %add_add_fusion.rest_0_, ...), custom_call_target="tpu_custom_call" | custom-call | flops 1000000000 | bytes 2000000 | tf_op jit(solution)/shard_map/pallas_call | solution.py:340
  36.3 19.6 %all_to_all.20.all_ref = bf16[32,24,128]{2,1,0:T(8,128)(2,1)S(1)} all-to-all(bf16[32,24,128]{2,1,0:T(8,128)(2,1)S(1)} %get-tuple-element.24), channel_id=1, replica_groups=mesh['seq'=32,'core'=2,'head'=8] {'seq'}, dimensions={0} | all-to-all | bytes 393216 | tf_op jit(solution)/shard_map/all_to_all | solution.py:347
  55.9 0.7 shard_map.112
  56.7 5.5 %all-to-all-start.2 = ((bf16[32,16,128]{2,1,0:T(8,128)(2,1)}), bf16[32,16,128]{2,1,0:T(8,128)(2,1)S(1)}, u32[]{:S(2)}, u32[]{:S(2)}) async-start(bf16[32,16,128]{2,1,0:T(8,128)(2,1)} %shard_map.112), calls=%async_computation.2 | async-start | bytes 262144 | tf_op jit(solution)/shard_map/all_to_all | solution.py:363
  62.1 2.8 %collective-permute-start.7 = (bf16[16,16,128]{2,1,0:T(8,128)(2,1)S(1)}, bf16[16,16,128]{2,1,0:T(8,128)(2,1)S(1)}, u32[]{:S(2)}, u32[]{:S(2)}) collective-permute-start(bf16[16,16,128]{2,1,0:T(8,128)(2,1)S(1)} %get-tuple-element.20), channel_id=1, source_target_pairs={{0,8},{8,0},{1,9},{9,1},{2,10},{10,2},{3,11},{11,3},{4,12},{12,4},... | collective-permute-start | bytes 196616 | tf_op jit(solution)/shard_map/ppermute | solution.py:348
  64.9 0.9 collective-permute-done.7.other_ref
  65.8 3.0 %shard_map.111 = (f32[4,128,512]{2,1,0:T(8,128)S(1)}, bf16[4,128,128]{2,1,0:T(8,128)(2,1)S(1)}, f32[4,128,512]{2,1,0:T(8,128)S(1)}) custom-call(s32[1]{0:T(128)} %bitcast.core_ref, bf16[16,184,128]{2,1,0:T(8,128)(2,1)S(1)} %all-to-all-done.r_ref, bf16[16,16,128]{2,1,0:T(8,128)(2,1)S(1)} %collective-permute-done.7.other_ref, ...), custom_call_target="tpu_custom_call" | custom-call | flops 1000000000 | bytes 8000000 | tf_op jit(solution)/shard_map/pallas_call | solution.py:350
  68.8 2.6 %all-to-all-done.2 = bf16[32,16,128]{2,1,0:T(8,128)(2,1)S(1)} async-done(((bf16[32,16,128]{2,1,0:T(8,128)(2,1)}), bf16[32,16,128]{2,1,0:T(8,128)(2,1)S(1)}, u32[]{:S(2)}, u32[]{:S(2)}) %all-to-all-start.2) | async-done | bytes 131104 | tf_op jit(solution)/shard_map/all_to_all | solution.py:363
  71.4 1.0 %shard_map.113 = bf16[512,512]{1,0:T(8,128)(2,1)} custom-call(f32[4,128,512]{2,1,0:T(8,128)S(1)} %get-tuple-element.21.part_ref, bf16[4,128,128]{2,1,0:T(8,128)(2,1)S(1)} %get-tuple-element.22.c_ref, f32[4,128,512]{2,1,0:T(8,128)S(1)} %get-tuple-element.23.scale_ref, bf16[4,128,128]{2,1,0:T(8,128)(2,1)S(1)} %bitcast.9), custom_call_target="tpu_custom_call" | custom-call | flops 100000000 | bytes 3000000 | tf_op jit(solution)/shard_map/pallas_call | solution.py:365
  72.4 0.0 copy-start.2
  72.4 0.0 copy-start.1
  72.4 6.5 %all-to-all-start.3 = ((bf16[16,32,512]{2,1,0:T(8,128)(2,1)}), bf16[16,32,512]{2,1,0:T(8,128)(2,1)S(1)}, u32[]{:S(2)}, u32[]{:S(2)}) async-start(bf16[16,32,512]{2,1,0:T(8,128)(2,1)} %bitcast.5), calls=%async_computation.3 | async-start | bytes 1048576 | tf_op jit(solution)/shard_map/all_to_all | solution.py:373
  79.0 0.0 copy-done.2
  79.0 0.0 copy-done.1
  79.0 0.2 shard_map.114.gate_ref
  79.2 14.5 %all-to-all-done.3.values_ref = bf16[16,32,512]{2,1,0:T(8,128)(2,1)S(1)} async-done(((bf16[16,32,512]{2,1,0:T(8,128)(2,1)}), bf16[16,32,512]{2,1,0:T(8,128)(2,1)S(1)}, u32[]{:S(2)}, u32[]{:S(2)}) %all-to-all-start.3) | async-done | bytes 524320 | tf_op jit(solution)/shard_map/all_to_all | solution.py:373
  93.7 1.0 %shard_map.115 = bf16[32,8192]{1,0:T(8,128)(2,1)} custom-call(bf16[16,32,512]{2,1,0:T(8,128)(2,1)S(1)} %all-to-all-done.3.values_ref, f32[32,8192]{1,0:T(8,128)S(1)} %shard_map.114.gate_ref, bf16[1,8192]{1,0:T(2,128)(2,1)S(1)} %reshape.19.gain_ref), custom_call_target="tpu_custom_call" | custom-call | flops 10000000 | bytes 2000000 | tf_op jit(solution)/shard_map/pallas_call | solution.py:378
  (8 shorter events, 0.1 us)
Async XLA Ops:
  0.0 17.0 %copy-start = (bf16[4,1024]{1,0:T(4,128)(2,1)S(1)}, bf16[4,1024]{1,0:T(4,128)(2,1)}, u32[]{:S(2)}) copy-start(bf16[4,1024]{1,0:T(4,128)(2,1)} %param.17) | copy-start | bytes 24580
  2.2 12.0 %copy-start.8 = (bf16[4,24,128]{2,1,0:T(8,128)(2,1)S(1)}, bf16[4,24,128]{2,1,0:T(8,128)(2,1)}, u32[]{:S(2)}) copy-start(bf16[4,24,128]{2,1,0:T(8,128)(2,1)} %get-tuple-element.16) | copy-start | bytes 73732
  2.2 12.7 %copy-start.7 = (bf16[4,24,128]{2,1,0:T(8,128)(2,1)S(1)}, bf16[4,24,128]{2,1,0:T(8,128)(2,1)}, u32[]{:S(2)}) copy-start(bf16[4,24,128]{2,1,0:T(8,128)(2,1)} %get-tuple-element.17) | copy-start | bytes 73732
  2.2 13.4 %copy-start.6 = (bf16[4,24,128]{2,1,0:T(8,128)(2,1)S(1)}, bf16[4,24,128]{2,1,0:T(8,128)(2,1)}, u32[]{:S(2)}) copy-start(bf16[4,24,128]{2,1,0:T(8,128)(2,1)} %get-tuple-element.18) | copy-start | bytes 73732
  2.2 14.0 %copy-start.5 = (bf16[4,24,128]{2,1,0:T(8,128)(2,1)S(1)}, bf16[4,24,128]{2,1,0:T(8,128)(2,1)}, u32[]{:S(2)}) copy-start(bf16[4,24,128]{2,1,0:T(8,128)(2,1)} %get-tuple-element.19) | copy-start | bytes 73732
  2.2 32.4 %all-to-all-start = ((bf16[16,184,128]{2,1,0:T(8,128)(2,1)}), bf16[16,184,128]{2,1,0:T(8,128)(2,1)S(1)}, u32[]{:S(2)}, u32[]{:S(2)}) async-start(bf16[16,184,128]{2,1,0:T(8,128)(2,1)} %get-tuple-element.15), calls=%async_computation | async-start | bytes 1507328 | tf_op jit(solution)/shard_map/all_to_all | solution.py:322
  14.2 4.4 %collective-permute-start = (bf16[4,24,128]{2,1,0:T(8,128)(2,1)S(1)}, bf16[4,24,128]{2,1,0:T(8,128)(2,1)S(1)}, u32[]{:S(2)}, u32[]{:S(2)}) collective-permute-start(bf16[4,24,128]{2,1,0:T(8,128)(2,1)S(1)} %copy-done.8), channel_id=1, source_target_pairs={{15,23},{31,39},{47,55},{63,71},{79,87},{95,103},{111,119},{127,13... | collective-permute-start | bytes 73736 | tf_op jit(solution)/shard_map/ppermute | solution.py:328
  14.9 3.7 %collective-permute-start.1 = (bf16[4,24,128]{2,1,0:T(8,128)(2,1)S(1)}, bf16[4,24,128]{2,1,0:T(8,128)(2,1)S(1)}, u32[]{:S(2)}, u32[]{:S(2)}) collective-permute-start(bf16[4,24,128]{2,1,0:T(8,128)(2,1)S(1)} %copy-done.7), channel_id=1, source_target_pairs={{15,16},{31,32},{47,48},{63,64},{79,80},{95,96},{111,112},{127,128... | collective-permute-start | bytes 73736 | tf_op jit(solution)/shard_map/ppermute | solution.py:328
  15.6 3.1 %collective-permute-start.2 = (bf16[4,24,128]{2,1,0:T(8,128)(2,1)S(1)}, bf16[4,24,128]{2,1,0:T(8,128)(2,1)S(1)}, u32[]{:S(2)}, u32[]{:S(2)}) collective-permute-start(bf16[4,24,128]{2,1,0:T(8,128)(2,1)S(1)} %copy-done.6), channel_id=1, source_target_pairs={{15,31},{31,47},{47,63},{63,79},{79,95},{95,111},{111,127},{127,14... | collective-permute-start | bytes 73736 | tf_op jit(solution)/shard_map/ppermute | solution.py:328
  16.3 2.4 %collective-permute-start.3 = (bf16[4,24,128]{2,1,0:T(8,128)(2,1)S(1)}, bf16[4,24,128]{2,1,0:T(8,128)(2,1)S(1)}, u32[]{:S(2)}, u32[]{:S(2)}) collective-permute-start(bf16[4,24,128]{2,1,0:T(8,128)(2,1)S(1)} %copy-done.5), channel_id=1, source_target_pairs={{15,24},{31,40},{47,56},{63,72},{79,88},{95,104},{111,120},{127,13... | collective-permute-start | bytes 73736 | tf_op jit(solution)/shard_map/ppermute | solution.py:328
  17.0 0.7 copy-start.3
  17.0 0.7 copy-start.4
  17.7 0.7 copy-start.9
  18.7 9.4 %collective-permute-start.4 = (bf16[24,128]{1,0:T(8,128)(2,1)S(1)}, bf16[24,128]{1,0:T(8,128)(2,1)S(1)}, u32[]{:S(2)}, u32[]{:S(2)}) collective-permute-start(bf16[24,128]{1,0:T(8,128)(2,1)S(1)} %get-tuple-element.27), channel_id=1, source_target_pairs={{7,6},{0,1},{15,14},{8,9},{23,22},{16,17},{31,30},{24,25},{39,38},... | collective-permute-start | bytes 18440 | tf_op jit(solution)/shard_map/ppermute | solution.py:333
  22.0 6.4 %collective-permute-start.5 = (bf16[24,128]{1,0:T(8,128)(2,1)S(1)}, bf16[24,128]{1,0:T(8,128)(2,1)S(1)}, u32[]{:S(2)}, u32[]{:S(2)}) collective-permute-start(bf16[24,128]{1,0:T(8,128)(2,1)S(1)} %get-tuple-element.26), channel_id=1, source_target_pairs={{7,5},{0,2},{15,13},{8,10},{23,21},{16,18},{31,29},{24,26},{39,37}... | collective-permute-start | bytes 18440 | tf_op jit(solution)/shard_map/ppermute | solution.py:333
  23.6 5.3 %collective-permute-start.6 = (bf16[24,128]{1,0:T(8,128)(2,1)S(1)}, bf16[24,128]{1,0:T(8,128)(2,1)S(1)}, u32[]{:S(2)}, u32[]{:S(2)}) collective-permute-start(bf16[24,128]{1,0:T(8,128)(2,1)S(1)} %get-tuple-element.25), channel_id=1, source_target_pairs={{7,4},{0,3},{15,12},{8,11},{23,20},{16,19},{31,28},{24,27},{39,36}... | collective-permute-start | bytes 18440 | tf_op jit(solution)/shard_map/ppermute | solution.py:333
  56.7 14.7 %all-to-all-start.2 = ((bf16[32,16,128]{2,1,0:T(8,128)(2,1)}), bf16[32,16,128]{2,1,0:T(8,128)(2,1)S(1)}, u32[]{:S(2)}, u32[]{:S(2)}) async-start(bf16[32,16,128]{2,1,0:T(8,128)(2,1)} %shard_map.112), calls=%async_computation.2 | async-start | bytes 262144 | tf_op jit(solution)/shard_map/all_to_all | solution.py:363
  62.1 3.7 %collective-permute-start.7 = (bf16[16,16,128]{2,1,0:T(8,128)(2,1)S(1)}, bf16[16,16,128]{2,1,0:T(8,128)(2,1)S(1)}, u32[]{:S(2)}, u32[]{:S(2)}) collective-permute-start(bf16[16,16,128]{2,1,0:T(8,128)(2,1)S(1)} %get-tuple-element.20), channel_id=1, source_target_pairs={{0,8},{8,0},{1,9},{9,1},{2,10},{10,2},{3,11},{11,3},{4,12},{12,4},... | collective-permute-start | bytes 196616 | tf_op jit(solution)/shard_map/ppermute | solution.py:348
  72.4 6.6 %copy-start.2 = (bf16[8192]{0:T(1024)(128)(2,1)S(1)}, bf16[8192]{0:T(1024)(128)(2,1)}, u32[]{:S(2)}) copy-start(bf16[8192]{0:T(1024)(128)(2,1)} %param.21) | copy-start | bytes 49156
  72.4 6.6 %copy-start.1 = (bf16[32,8192]{1,0:T(8,128)(2,1)S(1)}, bf16[32,8192]{1,0:T(8,128)(2,1)}, u32[]{:S(2)}) copy-start(bf16[32,8192]{1,0:T(8,128)(2,1)} %z_ref.1) | copy-start | bytes 1572868
  72.4 21.3 %all-to-all-start.3 = ((bf16[16,32,512]{2,1,0:T(8,128)(2,1)}), bf16[16,32,512]{2,1,0:T(8,128)(2,1)S(1)}, u32[]{:S(2)}, u32[]{:S(2)}) async-start(bf16[16,32,512]{2,1,0:T(8,128)(2,1)} %bitcast.5), calls=%async_computation.3 | async-start | bytes 1048576 | tf_op jit(solution)/shard_map/all_to_all | solution.py:373

commit v5 on v4

--- a/solution.py
+++ b/solution.py
@@ -127,11 +127,10 @@
 
 def conv_silu(taps_ref, pad_ref, span, tile):
     lanes = slice(tile * 128, (tile + 1) * 128)
-    at = span * SPAN
-    whole = pad_ref[tile, at : at + SPAN + 8, :]
-    total = whole[8:] * taps_ref[3:4, lanes]
-    for tap in range(3):
-        total = total + pltpu.roll(whole, 3 - tap, 0)[8:] * taps_ref[tap : tap + 1, lanes]
+    at = 8 - BORDER + span * SPAN
+    total = pad_ref[tile, at : at + SPAN, :] * taps_ref[0:1, lanes]
+    for tap in range(1, BORDER + 1):
+        total = total + pad_ref[tile, at + tap : at + tap + SPAN, :] * taps_ref[tap : tap + 1, lanes]
     return silu(total).astype(BF16)
 
 
@@ -263,21 +262,16 @@
             state = state * (here[CUT : CUT + 1] + here[CUT + 1 : CUT + 2]) + here[:CUT]
 
 
-def finish_kernel(part_ref, c_ref, scale_ref, state_ref, out_hbm, out_ref, sent):
+def finish_kernel(part_ref, c_ref, scale_ref, state_ref, out_ref):
     state = jnp.concatenate([state_ref[tile] for tile in range(TILES)], 1)
-    copies = []
     for span in range(SPANS):
-        rows = slice(span * SPAN, (span + 1) * SPAN)
         inter = jnp.dot(c_ref[span], state, preferred_element_type=F32)
-        out_ref[rows, :] = (part_ref[span] + inter * scale_ref[span]).astype(BF16)
-        copies.append(pltpu.make_async_copy(out_ref.at[rows, :], out_hbm.at[rows, :], sent.at[span]))
-        copies[-1].start()
-    for copy in copies:
-        copy.wait()
-
-
-def gate_kernel(z_ref, out_ref):
-    out_ref[...] = silu(z_ref[...].astype(F32))
+        out_ref[span * SPAN : (span + 1) * SPAN, :] = (part_ref[span] + inter * scale_ref[span]).astype(BF16)
+
+
+def gate_kernel(z_ref, gain_ref, gate_ref, row_ref):
+    gate_ref[...] = silu(z_ref[...].astype(F32))
+    row_ref[...] = gain_ref[...].astype(F32)
 
 
 def norm_kernel(values_ref, gate_ref, gain_ref, out_hbm, out_ref, sent):
@@ -288,7 +282,7 @@
         here = here.astype(F32) * gate_ref[:, whole]
         square = jnp.sum(here * here, axis=1, keepdims=True)
         scale = lax.rsqrt(square * (1.0 / (CORES * WIDE)) + 1e-05)
-        out_ref[:, whole] = (here * scale * gain_ref[:, whole].astype(F32)).astype(BF16)
+        out_ref[:, whole] = (here * scale * gain_ref[:, whole]).astype(BF16)
         copies.append(pltpu.make_async_copy(out_ref.at[:, whole], out_hbm.at[:, whole], sent.at[group]))
         copies[-1].start()
     for copy in copies:
@@ -337,6 +331,8 @@
     skip_row = jnp.pad(skip, (0, 2 * STATE))[None]
     taps = jnp.concatenate([taps, skip_row, jnp.zeros((3, WIDE + 2 * STATE), F32)], 0)
     pad = pltpu.VMEM((TILES + 2, TOKENS + 8, 128), F32)
+    width = HEADS * HEAD_DIM
+    taps, gain_held = lax.optimization_barrier((taps, norm_gain.reshape(1, width)))
     message, half = call(
         state_kernel,
         (like((RUNS, CUT + 8, 128), BF16), like((PEERS, HALF, 128), BF16)),
@@ -359,6 +355,11 @@
         [pad],
         in_specs=[pl.BlockSpec(memory_space=pltpu.SMEM)] + [vmem] * (3 + MEMBERS),
     )(core.astype(jnp.int32).reshape(1), got, other, taps, *handed)
+    z_held, slices = lax.optimization_barrier((z_stream, slices))
+    gate, gain = call(
+        gate_kernel, (like((ROWS, width), F32), like((1, width), F32)), 10**7, 2 * 10**6
+    )(z_held, gain_held)
+    part, gate, gain = lax.optimization_barrier((part, gate, gain))
     chained = call(chain_kernel, like((RUNS, CUT, 128), BF16), 10**7, 10**6)(slices)
     state = lax.all_to_all(chained, "seq", split_axis=0, concat_axis=0, tiled=True)
     hbm = pl.BlockSpec(memory_space=pltpu.HBM)
@@ -367,14 +368,10 @@
         like((TOKENS, WIDE), BF16),
         10**8,
         3 * 10**6,
-        [pltpu.VMEM((TOKENS, WIDE), BF16), pltpu.SemaphoreType.DMA((SPANS,))],
-        out_specs=hbm,
     )(part, c_conv, scale, state.reshape(TILES, STATE, 128))
     home = lax.all_to_all(
         values.reshape(PEERS, ROWS, WIDE), ("core", "head"), split_axis=0, concat_axis=0, tiled=True
     )
-    width = HEADS * HEAD_DIM
-    gate = call(gate_kernel, like((ROWS, width), F32), 10**7, 2 * 10**6)(z_stream)
     return call(
         norm_kernel,
         like((ROWS, width), BF16),
@@ -382,7 +379,7 @@
         2 * 10**6,
         [pltpu.VMEM((ROWS, width), BF16), pltpu.SemaphoreType.DMA((GROUPS,))],
         out_specs=hbm,
-    )(home, gate, norm_gain.reshape(1, width))
+    )(home, gate, gain)
 
 
 def solution(mesh):

time: 95.4 us -> 94.1 us (0.986)
  blocking collectives: 19.6 us -> 40.6 us
  waiting for transfers between devices: 27.5 us -> 12.8 us
  starting transfers between devices: 35.8 us -> 29.3 us
    all_to_all x0 -> x1, blocking collectives: none -> 21 us  [shards(): lax.all_to_all(values.reshape(PEERS, ROWS, WIDE), ('core', 'head'), split...]
    all_to_all x1 -> x0, waiting for transfers between devices: 14.5 us -> none  [shards(): lax.all_to_all(values.reshape(PEERS, ROWS, WIDE), ('core', 'head'), split...]
    all_to_all x1 -> x0, starting transfers between devices: 6.53 us -> none  [shards(): lax.all_to_all(values.reshape(PEERS, ROWS, WIDE), ('core', 'head'), split...]
  transfers between devices with their start and end apart: 11 -> 10, of which waited for: 7 -> 6; matrix products, arithmetic and copies ran while one was open for 0% -> 0% of each run, Pallas kernels for 3% -> 3%
where the time goes in v5:
time: 94.1 us; the launch traced here: 93.5 us
  blocking collectives  40.6 us (43%)
  starting transfers between devices  29.3 us (31%)
  waiting for transfers between devices  12.8 us (14%)
  Pallas kernels  8.77 us (9%)
  local copies, waits for them, and re-layouts  1.7 us (2%)
    all_to_all x1, blocking collectives, shards(): lax.all_to_all(values.reshape(PEERS, ROWS, WIDE), ('core', 'head'), split...  21 us
    all_to_all x1, blocking collectives, shards(): lax.all_to_all(message, 'seq', split_axis=0, concat_axis=0, tiled=True)  19.7 us
    all_to_all x1, starting transfers between devices, shards(): lax.all_to_all(packed, ('core', 'head'), split_axis=0, concat_axis=0, til...  12 us
    ppermute x3, starting transfers between devices, shards(): handed.append(lax.ppermute(led[member], everyone, pairs))  6.41 us
    all_to_all x1, waiting for transfers between devices, shards(): lax.all_to_all(packed, ('core', 'head'), split_axis=0, concat_axis=0, til...  5.8 us
    all_to_all x1, starting transfers between devices, shards(): lax.all_to_all(chained, 'seq', split_axis=0, concat_axis=0, tiled=True)  5.44 us
    ppermute x3, waiting for transfers between devices, shards(): handed.append(lax.ppermute(led[member], everyone, pairs))  3.59 us
    pallas_call x1, Pallas kernels, shards(): call(local_kernel, (like((SPANS, SPAN, WIDE), F32), like((SPANS, SPAN, ST...  2.82 us
  transfers between devices with their start and end apart: 10, of which 6 were waited for; matrix products, arithmetic and copies ran while one was open for 0% of the time, Pallas kernels for 3%

profile of v5, /device:TPU:1, one launch (start us, length us, event | category | flops | bytes accessed | tf_op | source)
XLA Modules:
  0.0 93.5 jit_solution(15879467307152494653)
XLA Ops:
  0.0 0.0 copy-start
  0.0 2.2 %shard_map.109 = (bf16[16,184,128]{2,1,0:T(8,128)(2,1)}, bf16[4,24,128]{2,1,0:T(8,128)(2,1)}, bf16[4,24,128]{2,1,0:T(8,128)(2,1)}, bf16[4,24,128]{2,1,0:T(8,128)(2,1)}, bf16[4,24,128]{2,1,0:T(8,128)(2,1)}) custom-call(bf16[32,8192]{1,0:T(8,128)(2,1)} %x_hbm.1, bf16[32,1024]{1,0:T(8,128)(2,1)} %b_hbm.1, bf16[32,1024]{1,0:T(8,128)(2,1)} %c_hbm.1, ...), custom_call_target="tpu_custom_call" | custom-call | bytes 1507328 | tf_op jit(solution)/shard_map/pallas_call | solution.py:307
  2.2 0.0 copy-start.8
  2.2 0.0 copy-start.7
  2.2 0.0 copy-start.6
  2.2 0.0 copy-start.5
  2.3 12.0 %all-to-all-start = ((bf16[16,184,128]{2,1,0:T(8,128)(2,1)}), bf16[16,184,128]{2,1,0:T(8,128)(2,1)S(1)}, u32[]{:S(2)}, u32[]{:S(2)}) async-start(bf16[16,184,128]{2,1,0:T(8,128)(2,1)} %get-tuple-element.24), calls=%async_computation | async-start | bytes 1507328 | tf_op jit(solution)/shard_map/all_to_all | solution.py:316
  14.2 0.0 copy-done.8
  14.2 0.7 collective-permute-start
  14.9 0.0 copy-done.7
  14.9 0.7 collective-permute-start.1
  15.6 0.0 copy-done.6
  15.6 0.7 collective-permute-start.2
  16.3 0.0 copy-done.5
  16.3 0.7 collective-permute-start.3
  17.0 0.0 copy-done
  17.0 0.0 copy-start.3
  17.0 0.0 copy-start.4
  17.0 0.6 copy-done.3
  17.6 0.0 copy-done.4
  17.7 0.0 copy-start.9
  17.7 0.7 copy-done.9
  18.3 0.1 dynamic_slice.7
  18.4 0.1 broadcast_in_dim.9
  18.5 0.1 reshape.16
  18.6 0.1 pad.7.clone
  18.6 0.0 collective-permute-done
  18.6 0.0 collective-permute-done.1
  18.7 0.0 collective-permute-done.2
  18.7 0.0 collective-permute-done.3
  18.7 3.3 %collective-permute-start.4 = (bf16[24,128]{1,0:T(8,128)(2,1)S(1)}, bf16[24,128]{1,0:T(8,128)(2,1)S(1)}, u32[]{:S(2)}, u32[]{:S(2)}) collective-permute-start(bf16[24,128]{1,0:T(8,128)(2,1)S(1)} %get-tuple-element.45), channel_id=1, source_target_pairs={{7,6},{0,1},{15,14},{8,9},{23,22},{16,17},{31,30},{24,25},{39,38},... | collective-permute-start | bytes 18440 | tf_op jit(solution)/shard_map/ppermute | solution.py:327
  22.0 1.6 %collective-permute-start.5 = (bf16[24,128]{1,0:T(8,128)(2,1)S(1)}, bf16[24,128]{1,0:T(8,128)(2,1)S(1)}, u32[]{:S(2)}, u32[]{:S(2)}) collective-permute-start(bf16[24,128]{1,0:T(8,128)(2,1)S(1)} %get-tuple-element.44), channel_id=1, source_target_pairs={{7,5},{0,2},{15,13},{8,10},{23,21},{16,18},{31,29},{24,26},{39,37}... | collective-permute-start | bytes 18440 | tf_op jit(solution)/shard_map/ppermute | solution.py:327
  23.6 0.0 copy-start.2
  23.6 1.6 %collective-permute-start.6 = (bf16[24,128]{1,0:T(8,128)(2,1)S(1)}, bf16[24,128]{1,0:T(8,128)(2,1)S(1)}, u32[]{:S(2)}, u32[]{:S(2)}) collective-permute-start(bf16[24,128]{1,0:T(8,128)(2,1)S(1)} %get-tuple-element.43), channel_id=1, source_target_pairs={{7,4},{0,3},{15,12},{8,11},{23,20},{16,19},{31,28},{24,27},{39,36}... | collective-permute-start | bytes 18440 | tf_op jit(solution)/shard_map/ppermute | solution.py:327
  25.1 0.1 maximum_maximum_fusion.taps_ref
  25.2 0.0 copy-done.2
  25.2 2.9 %collective-permute-done.4.rest_1_ = bf16[24,128]{1,0:T(8,128)(2,1)S(1)} collective-permute-done((bf16[24,128]{1,0:T(8,128)(2,1)S(1)}, bf16[24,128]{1,0:T(8,128)(2,1)S(1)}, u32[]{:S(2)}, u32[]{:S(2)}) %collective-permute-start.4) | collective-permute-done | bytes 6176 | tf_op jit(solution)/shard_map/ppermute | solution.py:327
  28.1 0.2 collective-permute-done.5.rest_2_
  28.4 0.5 collective-permute-done.6.rest_3_
  28.8 5.8 %all-to-all-done.r_ref = bf16[16,184,128]{2,1,0:T(8,128)(2,1)S(1)} async-done(((bf16[16,184,128]{2,1,0:T(8,128)(2,1)}), bf16[16,184,128]{2,1,0:T(8,128)(2,1)S(1)}, u32[]{:S(2)}, u32[]{:S(2)}) %all-to-all-start) | async-done | bytes 753696 | tf_op jit(solution)/shard_map/all_to_all | solution.py:316
  34.6 1.5 %shard_map.110 = (bf16[32,24,128]{2,1,0:T(8,128)(2,1)S(1)}, bf16[16,16,128]{2,1,0:T(8,128)(2,1)S(1)}) custom-call(bf16[16,184,128]{2,1,0:T(8,128)(2,1)S(1)} %all-to-all-done.r_ref, f32[8,768]{1,0:T(8,128)S(1)} %maximum_maximum_fusion.taps_ref, bf16[4,24,128]{2,1,0:T(8,128)(2,1)S(1)} %add_add_fusion.rest_0_, ...), custom_call_target="tpu_custom_call" | custom-call | flops 1000000000 | bytes 2000000 | tf_op jit(solution)/shard_map/pallas_call | solution.py:336
  36.2 19.7 %all_to_all.20.all_ref = bf16[32,24,128]{2,1,0:T(8,128)(2,1)S(1)} all-to-all(bf16[32,24,128]{2,1,0:T(8,128)(2,1)S(1)} %get-tuple-element.32), channel_id=1, replica_groups=mesh['seq'=32,'core'=2,'head'=8] {'seq'}, dimensions={0} | all-to-all | bytes 393216 | tf_op jit(solution)/shard_map/all_to_all | solution.py:343
  55.8 0.7 shard_map.113
  56.6 5.4 %all-to-all-start.2 = ((bf16[32,16,128]{2,1,0:T(8,128)(2,1)}), bf16[32,16,128]{2,1,0:T(8,128)(2,1)S(1)}, u32[]{:S(2)}, u32[]{:S(2)}) async-start(bf16[32,16,128]{2,1,0:T(8,128)(2,1)} %shard_map.113), calls=%async_computation.2 | async-start | bytes 262144 | tf_op jit(solution)/shard_map/all_to_all | solution.py:364
  62.0 2.8 %collective-permute-start.7 = (bf16[16,16,128]{2,1,0:T(8,128)(2,1)S(1)}, bf16[16,16,128]{2,1,0:T(8,128)(2,1)S(1)}, u32[]{:S(2)}, u32[]{:S(2)}) collective-permute-start(bf16[16,16,128]{2,1,0:T(8,128)(2,1)S(1)} %get-tuple-element.30), channel_id=1, source_target_pairs={{0,8},{8,0},{1,9},{9,1},{2,10},{10,2},{3,11},{11,3},{4,12},{12,4},... | collective-permute-start | bytes 196616 | tf_op jit(solution)/shard_map/ppermute | solution.py:344
  64.8 0.9 collective-permute-done.7.other_ref
  65.7 0.0 copy-start.1
  65.7 2.8 %shard_map.111 = (f32[4,128,512]{2,1,0:T(8,128)S(1)}, bf16[4,128,128]{2,1,0:T(8,128)(2,1)S(1)}, f32[4,128,512]{2,1,0:T(8,128)S(1)}) custom-call(s32[1]{0:T(128)} %bitcast.core_ref, bf16[16,184,128]{2,1,0:T(8,128)(2,1)S(1)} %all-to-all-done.r_ref, bf16[16,16,128]{2,1,0:T(8,128)(2,1)S(1)} %collective-permute-done.7.other_ref, ...), custom_call_target="tpu_custom_call" | custom-call | flops 1000000000 | bytes 8000000 | tf_op jit(solution)/shard_map/pallas_call | solution.py:346
  68.5 0.0 copy-done.1
  68.5 0.2 shard_map.112
  68.7 2.6 %all-to-all-done.2 = bf16[32,16,128]{2,1,0:T(8,128)(2,1)S(1)} async-done(((bf16[32,16,128]{2,1,0:T(8,128)(2,1)}), bf16[32,16,128]{2,1,0:T(8,128)(2,1)S(1)}, u32[]{:S(2)}, u32[]{:S(2)}) %all-to-all-start.2) | async-done | bytes 131104 | tf_op jit(solution)/shard_map/all_to_all | solution.py:364
  71.3 0.3 shard_map.114
  71.6 21.0 %all_to_all.21.values_ref = bf16[16,32,512]{2,1,0:T(8,128)(2,1)S(1)} all-to-all(bf16[16,32,512]{2,1,0:T(8,128)(2,1)S(1)} %bitcast.9), channel_id=1, replica_groups=mesh['seq'=32,'core'=2,'head'=8] {'core','head'}, dimensions={0} | all-to-all | bytes 1048576 | tf_op jit(solution)/shard_map/all_to_all | solution.py:372
  92.5 1.0 %shard_map.115 = bf16[32,8192]{1,0:T(8,128)(2,1)} custom-call(bf16[16,32,512]{2,1,0:T(8,128)(2,1)S(1)} %all_to_all.21.values_ref, f32[32,8192]{1,0:T(8,128)S(1)} %get-tuple-element.41.gate_ref, f32[1,8192]{1,0:T(1,128)S(1)} %get-tuple-element.42.gain_ref), custom_call_target="tpu_custom_call" | custom-call | flops 10000000 | bytes 2000000 | tf_op jit(solution)/shard_map/pallas_call | solution.py:375
  (8 shorter events, 0.1 us)
Async XLA Ops:
  0.0 17.0 %copy-start = (bf16[4,1024]{1,0:T(4,128)(2,1)S(1)}, bf16[4,1024]{1,0:T(4,128)(2,1)}, u32[]{:S(2)}) copy-start(bf16[4,1024]{1,0:T(4,128)(2,1)} %param.17) | copy-start | bytes 24580
  2.2 12.0 %copy-start.8 = (bf16[4,24,128]{2,1,0:T(8,128)(2,1)S(1)}, bf16[4,24,128]{2,1,0:T(8,128)(2,1)}, u32[]{:S(2)}) copy-start(bf16[4,24,128]{2,1,0:T(8,128)(2,1)} %get-tuple-element.26) | copy-start | bytes 73732
  2.2 12.7 %copy-start.7 = (bf16[4,24,128]{2,1,0:T(8,128)(2,1)S(1)}, bf16[4,24,128]{2,1,0:T(8,128)(2,1)}, u32[]{:S(2)}) copy-start(bf16[4,24,128]{2,1,0:T(8,128)(2,1)} %get-tuple-element.27) | copy-start | bytes 73732
  2.2 13.4 %copy-start.6 = (bf16[4,24,128]{2,1,0:T(8,128)(2,1)S(1)}, bf16[4,24,128]{2,1,0:T(8,128)(2,1)}, u32[]{:S(2)}) copy-start(bf16[4,24,128]{2,1,0:T(8,128)(2,1)} %get-tuple-element.28) | copy-start | bytes 73732
  2.2 14.0 %copy-start.5 = (bf16[4,24,128]{2,1,0:T(8,128)(2,1)S(1)}, bf16[4,24,128]{2,1,0:T(8,128)(2,1)}, u32[]{:S(2)}) copy-start(bf16[4,24,128]{2,1,0:T(8,128)(2,1)} %get-tuple-element.29) | copy-start | bytes 73732
  2.3 32.4 %all-to-all-start = ((bf16[16,184,128]{2,1,0:T(8,128)(2,1)}), bf16[16,184,128]{2,1,0:T(8,128)(2,1)S(1)}, u32[]{:S(2)}, u32[]{:S(2)}) async-start(bf16[16,184,128]{2,1,0:T(8,128)(2,1)} %get-tuple-element.24), calls=%async_computation | async-start | bytes 1507328 | tf_op jit(solution)/shard_map/all_to_all | solution.py:316
  14.2 4.4 %collective-permute-start = (bf16[4,24,128]{2,1,0:T(8,128)(2,1)S(1)}, bf16[4,24,128]{2,1,0:T(8,128)(2,1)S(1)}, u32[]{:S(2)}, u32[]{:S(2)}) collective-permute-start(bf16[4,24,128]{2,1,0:T(8,128)(2,1)S(1)} %copy-done.8), channel_id=1, source_target_pairs={{15,23},{31,39},{47,55},{63,71},{79,87},{95,103},{111,119},{127,13... | collective-permute-start | bytes 73736 | tf_op jit(solution)/shard_map/ppermute | solution.py:322
  14.9 3.7 %collective-permute-start.1 = (bf16[4,24,128]{2,1,0:T(8,128)(2,1)S(1)}, bf16[4,24,128]{2,1,0:T(8,128)(2,1)S(1)}, u32[]{:S(2)}, u32[]{:S(2)}) collective-permute-start(bf16[4,24,128]{2,1,0:T(8,128)(2,1)S(1)} %copy-done.7), channel_id=1, source_target_pairs={{15,16},{31,32},{47,48},{63,64},{79,80},{95,96},{111,112},{127,128... | collective-permute-start | bytes 73736 | tf_op jit(solution)/shard_map/ppermute | solution.py:322
  15.6 3.1 %collective-permute-start.2 = (bf16[4,24,128]{2,1,0:T(8,128)(2,1)S(1)}, bf16[4,24,128]{2,1,0:T(8,128)(2,1)S(1)}, u32[]{:S(2)}, u32[]{:S(2)}) collective-permute-start(bf16[4,24,128]{2,1,0:T(8,128)(2,1)S(1)} %copy-done.6), channel_id=1, source_target_pairs={{15,31},{31,47},{47,63},{63,79},{79,95},{95,111},{111,127},{127,14... | collective-permute-start | bytes 73736 | tf_op jit(solution)/shard_map/ppermute | solution.py:322
  16.3 2.4 %collective-permute-start.3 = (bf16[4,24,128]{2,1,0:T(8,128)(2,1)S(1)}, bf16[4,24,128]{2,1,0:T(8,128)(2,1)S(1)}, u32[]{:S(2)}, u32[]{:S(2)}) collective-permute-start(bf16[4,24,128]{2,1,0:T(8,128)(2,1)S(1)} %copy-done.5), channel_id=1, source_target_pairs={{15,24},{31,40},{47,56},{63,72},{79,88},{95,104},{111,120},{127,13... | collective-permute-start | bytes 73736 | tf_op jit(solution)/shard_map/ppermute | solution.py:322
  17.0 0.7 copy-start.3
  17.0 0.7 copy-start.4
  17.7 0.7 copy-start.9
  18.7 9.4 %collective-permute-start.4 = (bf16[24,128]{1,0:T(8,128)(2,1)S(1)}, bf16[24,128]{1,0:T(8,128)(2,1)S(1)}, u32[]{:S(2)}, u32[]{:S(2)}) collective-permute-start(bf16[24,128]{1,0:T(8,128)(2,1)S(1)} %get-tuple-element.45), channel_id=1, source_target_pairs={{7,6},{0,1},{15,14},{8,9},{23,22},{16,17},{31,30},{24,25},{39,38},... | collective-permute-start | bytes 18440 | tf_op jit(solution)/shard_map/ppermute | solution.py:327
  22.0 6.4 %collective-permute-start.5 = (bf16[24,128]{1,0:T(8,128)(2,1)S(1)}, bf16[24,128]{1,0:T(8,128)(2,1)S(1)}, u32[]{:S(2)}, u32[]{:S(2)}) collective-permute-start(bf16[24,128]{1,0:T(8,128)(2,1)S(1)} %get-tuple-element.44), channel_id=1, source_target_pairs={{7,5},{0,2},{15,13},{8,10},{23,21},{16,18},{31,29},{24,26},{39,37}... | collective-permute-start | bytes 18440 | tf_op jit(solution)/shard_map/ppermute | solution.py:327
  23.6 1.7 %copy-start.2 = (bf16[8192]{0:T(1024)(128)(2,1)S(1)}, bf16[8192]{0:T(1024)(128)(2,1)}, u32[]{:S(2)}) copy-start(bf16[8192]{0:T(1024)(128)(2,1)} %param.21) | copy-start | bytes 49156
  23.6 5.3 %collective-permute-start.6 = (bf16[24,128]{1,0:T(8,128)(2,1)S(1)}, bf16[24,128]{1,0:T(8,128)(2,1)S(1)}, u32[]{:S(2)}, u32[]{:S(2)}) collective-permute-start(bf16[24,128]{1,0:T(8,128)(2,1)S(1)} %get-tuple-element.43), channel_id=1, source_target_pairs={{7,4},{0,3},{15,12},{8,11},{23,20},{16,19},{31,28},{24,27},{39,36}... | collective-permute-start | bytes 18440 | tf_op jit(solution)/shard_map/ppermute | solution.py:327
  56.6 14.7 %all-to-all-start.2 = ((bf16[32,16,128]{2,1,0:T(8,128)(2,1)}), bf16[32,16,128]{2,1,0:T(8,128)(2,1)S(1)}, u32[]{:S(2)}, u32[]{:S(2)}) async-start(bf16[32,16,128]{2,1,0:T(8,128)(2,1)} %shard_map.113), calls=%async_computation.2 | async-start | bytes 262144 | tf_op jit(solution)/shard_map/all_to_all | solution.py:364
  62.0 3.7 %collective-permute-start.7 = (bf16[16,16,128]{2,1,0:T(8,128)(2,1)S(1)}, bf16[16,16,128]{2,1,0:T(8,128)(2,1)S(1)}, u32[]{:S(2)}, u32[]{:S(2)}) collective-permute-start(bf16[16,16,128]{2,1,0:T(8,128)(2,1)S(1)} %get-tuple-element.30), channel_id=1, source_target_pairs={{0,8},{8,0},{1,9},{9,1},{2,10},{10,2},{3,11},{11,3},{4,12},{12,4},... | collective-permute-start | bytes 196616 | tf_op jit(solution)/shard_map/ppermute | solution.py:344
  65.7 2.8 %copy-start.1 = (bf16[32,8192]{1,0:T(8,128)(2,1)S(1)}, bf16[32,8192]{1,0:T(8,128)(2,1)}, u32[]{:S(2)}) copy-start(bf16[32,8192]{1,0:T(8,128)(2,1)} %z_ref) | copy-start | bytes 1572868

commit v6 on v5

--- a/solution.py
+++ b/solution.py
@@ -187,16 +187,21 @@
     fill(r_ref, rims, pad_ref, range(TILES + 1))
     steps, running = rows_of(r_ref)
     lanes = own_lanes(2)
-    tails = jnp.exp(running[:, SPAN - 1 :] - running) * steps
-    last = [of_span(running, span)[:, SPAN - 1 :] for span in range(SPANS)]
-    factors = jnp.exp(jnp.concatenate(last + [last[0] + last[1] + last[2] + last[3]], 1))
-    factors = jnp.concatenate([factors, jnp.zeros((MINE, SPAN - SPANS - 1), F32)], 1)
-    factors = widen(factors, lanes, 2)
-    state = None
+    after = jnp.zeros((MINE, 1), F32)
+    tails = []
+    for span in reversed(range(SPANS)):
+        here = of_span(running, span)
+        tails.insert(0, jnp.exp(here[:, SPAN - 1 :] - here + after) * of_span(steps, span))
+        after = after + here[:, SPAN - 1 :]
+    scale = widen(jnp.exp(after + jnp.zeros((MINE, SPAN), F32)), lanes, 2)[:1]
+    weighted, turned = [], []
     for span in range(SPANS):
-        _, _, fresh = span_state(taps_ref, pad_ref, span, widen(of_span(tails, span), lanes, 2))
-        state = fresh if span == 0 else state * factors[span : span + 1] + fresh
-    scale = factors[SPANS : SPANS + 1]
+        tail = widen(tails[span], lanes, 2)
+        b_conv = conv_silu(taps_ref, pad_ref, span, TILES)
+        x_conv = jnp.concatenate([conv_silu(taps_ref, pad_ref, span, tile) for tile in range(TILES)], 1)
+        weighted.append((x_conv.astype(F32) * tail).astype(BF16))
+        turned.append(jnp.transpose(b_conv.astype(F32)).astype(BF16))
+    state = jnp.dot(jnp.concatenate(turned, 1), jnp.concatenate(weighted, 0), preferred_element_type=F32)
     coarse = scale.astype(BF16).astype(F32)
     tail = jnp.concatenate([coarse, scale - coarse, jnp.zeros((6, WIDE), F32)], 0)
     for tile in range(TILES):

time: 94.1 us -> 94 us (level)
  no operation moved by 1% of the time
where the time goes in v6:
time: 94 us; the launch traced here: 93.4 us
  blocking collectives  40.6 us (43%)
  starting transfers between devices  29.3 us (31%)
  waiting for transfers between devices  12.8 us (14%)
  Pallas kernels  8.6 us (9%)
  local copies, waits for them, and re-layouts  1.7 us (2%)
    all_to_all x1, blocking collectives, shards(): lax.all_to_all(values.reshape(PEERS, ROWS, WIDE), ('core', 'head'), split...  21 us
    all_to_all x1, blocking collectives, shards(): lax.all_to_all(message, 'seq', split_axis=0, concat_axis=0, tiled=True)  19.7 us
    all_to_all x1, starting transfers between devices, shards(): lax.all_to_all(packed, ('core', 'head'), split_axis=0, concat_axis=0, til...  12 us
    ppermute x3, starting transfers between devices, shards(): handed.append(lax.ppermute(led[member], everyone, pairs))  6.41 us
    all_to_all x1, waiting for transfers between devices, shards(): lax.all_to_all(packed, ('core', 'head'), split_axis=0, concat_axis=0, til...  5.8 us
    all_to_all x1, starting transfers between devices, shards(): lax.all_to_all(chained, 'seq', split_axis=0, concat_axis=0, tiled=True)  5.44 us
    ppermute x3, waiting for transfers between devices, shards(): handed.append(lax.ppermute(led[member], everyone, pairs))  3.59 us
    pallas_call x1, Pallas kernels, shards(): call(local_kernel, (like((SPANS, SPAN, WIDE), F32), like((SPANS, SPAN, ST...  2.82 us
  transfers between devices with their start and end apart: 10, of which 6 were waited for; matrix products, arithmetic and copies ran while one was open for 0% of the time, Pallas kernels for 3%

profile of v6, /device:TPU:1, one launch (start us, length us, event | category | flops | bytes accessed | tf_op | source)
XLA Modules:
  0.0 93.4 jit_solution(2528885415387315112)
XLA Ops:
  0.0 0.0 copy-start
  0.0 2.2 %shard_map.109 = (bf16[16,184,128]{2,1,0:T(8,128)(2,1)}, bf16[4,24,128]{2,1,0:T(8,128)(2,1)}, bf16[4,24,128]{2,1,0:T(8,128)(2,1)}, bf16[4,24,128]{2,1,0:T(8,128)(2,1)}, bf16[4,24,128]{2,1,0:T(8,128)(2,1)}) custom-call(bf16[32,8192]{1,0:T(8,128)(2,1)} %x_hbm.1, bf16[32,1024]{1,0:T(8,128)(2,1)} %b_hbm.1, bf16[32,1024]{1,0:T(8,128)(2,1)} %c_hbm.1, ...), custom_call_target="tpu_custom_call" | custom-call | bytes 1507328 | tf_op jit(solution)/shard_map/pallas_call | solution.py:312
  2.2 0.0 copy-start.8
  2.2 0.0 copy-start.7
  2.2 0.0 copy-start.6
  2.2 0.0 copy-start.5
  2.3 12.0 %all-to-all-start = ((bf16[16,184,128]{2,1,0:T(8,128)(2,1)}), bf16[16,184,128]{2,1,0:T(8,128)(2,1)S(1)}, u32[]{:S(2)}, u32[]{:S(2)}) async-start(bf16[16,184,128]{2,1,0:T(8,128)(2,1)} %get-tuple-element.24), calls=%async_computation | async-start | bytes 1507328 | tf_op jit(solution)/shard_map/all_to_all | solution.py:321
  14.2 0.0 copy-done.8
  14.2 0.7 collective-permute-start
  14.9 0.0 copy-done.7
  14.9 0.7 collective-permute-start.1
  15.6 0.0 copy-done.6
  15.6 0.7 collective-permute-start.2
  16.3 0.0 copy-done.5
  16.3 0.7 collective-permute-start.3
  17.0 0.0 copy-done
  17.0 0.0 copy-start.3
  17.0 0.0 copy-start.4
  17.0 0.6 copy-done.3
  17.6 0.0 copy-done.4
  17.7 0.0 copy-start.9
  17.7 0.7 copy-done.9
  18.3 0.1 dynamic_slice.7
  18.4 0.1 broadcast_in_dim.9
  18.5 0.1 reshape.16
  18.6 0.1 pad.7.clone
  18.6 0.0 collective-permute-done
  18.6 0.0 collective-permute-done.1
  18.7 0.0 collective-permute-done.2
  18.7 0.0 collective-permute-done.3
  18.7 3.3 %collective-permute-start.4 = (bf16[24,128]{1,0:T(8,128)(2,1)S(1)}, bf16[24,128]{1,0:T(8,128)(2,1)S(1)}, u32[]{:S(2)}, u32[]{:S(2)}) collective-permute-start(bf16[24,128]{1,0:T(8,128)(2,1)S(1)} %get-tuple-element.45), channel_id=1, source_target_pairs={{7,6},{0,1},{15,14},{8,9},{23,22},{16,17},{31,30},{24,25},{39,38},... | collective-permute-start | bytes 18440 | tf_op jit(solution)/shard_map/ppermute | solution.py:332
  22.0 1.6 %collective-permute-start.5 = (bf16[24,128]{1,0:T(8,128)(2,1)S(1)}, bf16[24,128]{1,0:T(8,128)(2,1)S(1)}, u32[]{:S(2)}, u32[]{:S(2)}) collective-permute-start(bf16[24,128]{1,0:T(8,128)(2,1)S(1)} %get-tuple-element.44), channel_id=1, source_target_pairs={{7,5},{0,2},{15,13},{8,10},{23,21},{16,18},{31,29},{24,26},{39,37}... | collective-permute-start | bytes 18440 | tf_op jit(solution)/shard_map/ppermute | solution.py:332
  23.6 0.0 copy-start.2
  23.6 1.6 %collective-permute-start.6 = (bf16[24,128]{1,0:T(8,128)(2,1)S(1)}, bf16[24,128]{1,0:T(8,128)(2,1)S(1)}, u32[]{:S(2)}, u32[]{:S(2)}) collective-permute-start(bf16[24,128]{1,0:T(8,128)(2,1)S(1)} %get-tuple-element.43), channel_id=1, source_target_pairs={{7,4},{0,3},{15,12},{8,11},{23,20},{16,19},{31,28},{24,27},{39,36}... | collective-permute-start | bytes 18440 | tf_op jit(solution)/shard_map/ppermute | solution.py:332
  25.1 0.1 maximum_maximum_fusion.taps_ref
  25.2 0.0 copy-done.2
  25.2 2.9 %collective-permute-done.4.rest_1_ = bf16[24,128]{1,0:T(8,128)(2,1)S(1)} collective-permute-done((bf16[24,128]{1,0:T(8,128)(2,1)S(1)}, bf16[24,128]{1,0:T(8,128)(2,1)S(1)}, u32[]{:S(2)}, u32[]{:S(2)}) %collective-permute-start.4) | collective-permute-done | bytes 6176 | tf_op jit(solution)/shard_map/ppermute | solution.py:332
  28.1 0.2 collective-permute-done.5.rest_2_
  28.4 0.5 collective-permute-done.6.rest_3_
  28.8 5.8 %all-to-all-done.r_ref = bf16[16,184,128]{2,1,0:T(8,128)(2,1)S(1)} async-done(((bf16[16,184,128]{2,1,0:T(8,128)(2,1)}), bf16[16,184,128]{2,1,0:T(8,128)(2,1)S(1)}, u32[]{:S(2)}, u32[]{:S(2)}) %all-to-all-start) | async-done | bytes 753696 | tf_op jit(solution)/shard_map/all_to_all | solution.py:321
  34.6 1.4 %shard_map.110 = (bf16[32,24,128]{2,1,0:T(8,128)(2,1)S(1)}, bf16[16,16,128]{2,1,0:T(8,128)(2,1)S(1)}) custom-call(bf16[16,184,128]{2,1,0:T(8,128)(2,1)S(1)} %all-to-all-done.r_ref, f32[8,768]{1,0:T(8,128)S(1)} %maximum_maximum_fusion.taps_ref, bf16[4,24,128]{2,1,0:T(8,128)(2,1)S(1)} %add_add_fusion.rest_0_, ...), custom_call_target="tpu_custom_call" | custom-call | flops 1000000000 | bytes 2000000 | tf_op jit(solution)/shard_map/pallas_call | solution.py:341
  36.0 19.7 %all_to_all.20.all_ref = bf16[32,24,128]{2,1,0:T(8,128)(2,1)S(1)} all-to-all(bf16[32,24,128]{2,1,0:T(8,128)(2,1)S(1)} %get-tuple-element.32), channel_id=1, replica_groups=mesh['seq'=32,'core'=2,'head'=8] {'seq'}, dimensions={0} | all-to-all | bytes 393216 | tf_op jit(solution)/shard_map/all_to_all | solution.py:348
  55.7 0.7 shard_map.113
  56.4 5.4 %all-to-all-start.2 = ((bf16[32,16,128]{2,1,0:T(8,128)(2,1)}), bf16[32,16,128]{2,1,0:T(8,128)(2,1)S(1)}, u32[]{:S(2)}, u32[]{:S(2)}) async-start(bf16[32,16,128]{2,1,0:T(8,128)(2,1)} %shard_map.113), calls=%async_computation.2 | async-start | bytes 262144 | tf_op jit(solution)/shard_map/all_to_all | solution.py:369
  61.8 2.8 %collective-permute-start.7 = (bf16[16,16,128]{2,1,0:T(8,128)(2,1)S(1)}, bf16[16,16,128]{2,1,0:T(8,128)(2,1)S(1)}, u32[]{:S(2)}, u32[]{:S(2)}) collective-permute-start(bf16[16,16,128]{2,1,0:T(8,128)(2,1)S(1)} %get-tuple-element.30), channel_id=1, source_target_pairs={{0,8},{8,0},{1,9},{9,1},{2,10},{10,2},{3,11},{11,3},{4,12},{12,4},... | collective-permute-start | bytes 196616 | tf_op jit(solution)/shard_map/ppermute | solution.py:349
  64.6 0.9 collective-permute-done.7.other_ref
  65.5 0.0 copy-start.1
  65.5 2.8 %shard_map.111 = (f32[4,128,512]{2,1,0:T(8,128)S(1)}, bf16[4,128,128]{2,1,0:T(8,128)(2,1)S(1)}, f32[4,128,512]{2,1,0:T(8,128)S(1)}) custom-call(s32[1]{0:T(128)} %bitcast.core_ref, bf16[16,184,128]{2,1,0:T(8,128)(2,1)S(1)} %all-to-all-done.r_ref, bf16[16,16,128]{2,1,0:T(8,128)(2,1)S(1)} %collective-permute-done.7.other_ref, ...), custom_call_target="tpu_custom_call" | custom-call | flops 1000000000 | bytes 8000000 | tf_op jit(solution)/shard_map/pallas_call | solution.py:351
  68.3 0.0 copy-done.1
  68.3 0.2 shard_map.112
  68.5 2.6 %all-to-all-done.2 = bf16[32,16,128]{2,1,0:T(8,128)(2,1)S(1)} async-done(((bf16[32,16,128]{2,1,0:T(8,128)(2,1)}), bf16[32,16,128]{2,1,0:T(8,128)(2,1)S(1)}, u32[]{:S(2)}, u32[]{:S(2)}) %all-to-all-start.2) | async-done | bytes 131104 | tf_op jit(solution)/shard_map/all_to_all | solution.py:369
  71.1 0.3 shard_map.114
  71.4 21.0 %all_to_all.21.values_ref = bf16[16,32,512]{2,1,0:T(8,128)(2,1)S(1)} all-to-all(bf16[16,32,512]{2,1,0:T(8,128)(2,1)S(1)} %bitcast.9), channel_id=1, replica_groups=mesh['seq'=32,'core'=2,'head'=8] {'core','head'}, dimensions={0} | all-to-all | bytes 1048576 | tf_op jit(solution)/shard_map/all_to_all | solution.py:377
  92.3 1.0 %shard_map.115 = bf16[32,8192]{1,0:T(8,128)(2,1)} custom-call(bf16[16,32,512]{2,1,0:T(8,128)(2,1)S(1)} %all_to_all.21.values_ref, f32[32,8192]{1,0:T(8,128)S(1)} %get-tuple-element.41.gate_ref, f32[1,8192]{1,0:T(1,128)S(1)} %get-tuple-element.42.gain_ref), custom_call_target="tpu_custom_call" | custom-call | flops 10000000 | bytes 2000000 | tf_op jit(solution)/shard_map/pallas_call | solution.py:380
  (8 shorter events, 0.1 us)
Async XLA Ops:
  0.0 17.0 %copy-start = (bf16[4,1024]{1,0:T(4,128)(2,1)S(1)}, bf16[4,1024]{1,0:T(4,128)(2,1)}, u32[]{:S(2)}) copy-start(bf16[4,1024]{1,0:T(4,128)(2,1)} %param.17) | copy-start | bytes 24580
  2.2 12.0 %copy-start.8 = (bf16[4,24,128]{2,1,0:T(8,128)(2,1)S(1)}, bf16[4,24,128]{2,1,0:T(8,128)(2,1)}, u32[]{:S(2)}) copy-start(bf16[4,24,128]{2,1,0:T(8,128)(2,1)} %get-tuple-element.26) | copy-start | bytes 73732
  2.2 12.7 %copy-start.7 = (bf16[4,24,128]{2,1,0:T(8,128)(2,1)S(1)}, bf16[4,24,128]{2,1,0:T(8,128)(2,1)}, u32[]{:S(2)}) copy-start(bf16[4,24,128]{2,1,0:T(8,128)(2,1)} %get-tuple-element.27) | copy-start | bytes 73732
  2.2 13.4 %copy-start.6 = (bf16[4,24,128]{2,1,0:T(8,128)(2,1)S(1)}, bf16[4,24,128]{2,1,0:T(8,128)(2,1)}, u32[]{:S(2)}) copy-start(bf16[4,24,128]{2,1,0:T(8,128)(2,1)} %get-tuple-element.28) | copy-start | bytes 73732
  2.2 14.0 %copy-start.5 = (bf16[4,24,128]{2,1,0:T(8,128)(2,1)S(1)}, bf16[4,24,128]{2,1,0:T(8,128)(2,1)}, u32[]{:S(2)}) copy-start(bf16[4,24,128]{2,1,0:T(8,128)(2,1)} %get-tuple-element.29) | copy-start | bytes 73732
  2.3 32.4 %all-to-all-start = ((bf16[16,184,128]{2,1,0:T(8,128)(2,1)}), bf16[16,184,128]{2,1,0:T(8,128)(2,1)S(1)}, u32[]{:S(2)}, u32[]{:S(2)}) async-start(bf16[16,184,128]{2,1,0:T(8,128)(2,1)} %get-tuple-element.24), calls=%async_computation | async-start | bytes 1507328 | tf_op jit(solution)/shard_map/all_to_all | solution.py:321
  14.2 4.4 %collective-permute-start = (bf16[4,24,128]{2,1,0:T(8,128)(2,1)S(1)}, bf16[4,24,128]{2,1,0:T(8,128)(2,1)S(1)}, u32[]{:S(2)}, u32[]{:S(2)}) collective-permute-start(bf16[4,24,128]{2,1,0:T(8,128)(2,1)S(1)} %copy-done.8), channel_id=1, source_target_pairs={{15,23},{31,39},{47,55},{63,71},{79,87},{95,103},{111,119},{127,13... | collective-permute-start | bytes 73736 | tf_op jit(solution)/shard_map/ppermute | solution.py:327
  14.9 3.7 %collective-permute-start.1 = (bf16[4,24,128]{2,1,0:T(8,128)(2,1)S(1)}, bf16[4,24,128]{2,1,0:T(8,128)(2,1)S(1)}, u32[]{:S(2)}, u32[]{:S(2)}) collective-permute-start(bf16[4,24,128]{2,1,0:T(8,128)(2,1)S(1)} %copy-done.7), channel_id=1, source_target_pairs={{15,16},{31,32},{47,48},{63,64},{79,80},{95,96},{111,112},{127,128... | collective-permute-start | bytes 73736 | tf_op jit(solution)/shard_map/ppermute | solution.py:327
  15.6 3.1 %collective-permute-start.2 = (bf16[4,24,128]{2,1,0:T(8,128)(2,1)S(1)}, bf16[4,24,128]{2,1,0:T(8,128)(2,1)S(1)}, u32[]{:S(2)}, u32[]{:S(2)}) collective-permute-start(bf16[4,24,128]{2,1,0:T(8,128)(2,1)S(1)} %copy-done.6), channel_id=1, source_target_pairs={{15,31},{31,47},{47,63},{63,79},{79,95},{95,111},{111,127},{127,14... | collective-permute-start | bytes 73736 | tf_op jit(solution)/shard_map/ppermute | solution.py:327
  16.3 2.4 %collective-permute-start.3 = (bf16[4,24,128]{2,1,0:T(8,128)(2,1)S(1)}, bf16[4,24,128]{2,1,0:T(8,128)(2,1)S(1)}, u32[]{:S(2)}, u32[]{:S(2)}) collective-permute-start(bf16[4,24,128]{2,1,0:T(8,128)(2,1)S(1)} %copy-done.5), channel_id=1, source_target_pairs={{15,24},{31,40},{47,56},{63,72},{79,88},{95,104},{111,120},{127,13... | collective-permute-start | bytes 73736 | tf_op jit(solution)/shard_map/ppermute | solution.py:327
  17.0 0.7 copy-start.3
  17.0 0.7 copy-start.4
  17.7 0.7 copy-start.9
  18.7 9.4 %collective-permute-start.4 = (bf16[24,128]{1,0:T(8,128)(2,1)S(1)}, bf16[24,128]{1,0:T(8,128)(2,1)S(1)}, u32[]{:S(2)}, u32[]{:S(2)}) collective-permute-start(bf16[24,128]{1,0:T(8,128)(2,1)S(1)} %get-tuple-element.45), channel_id=1, source_target_pairs={{7,6},{0,1},{15,14},{8,9},{23,22},{16,17},{31,30},{24,25},{39,38},... | collective-permute-start | bytes 18440 | tf_op jit(solution)/shard_map/ppermute | solution.py:332
  22.0 6.4 %collective-permute-start.5 = (bf16[24,128]{1,0:T(8,128)(2,1)S(1)}, bf16[24,128]{1,0:T(8,128)(2,1)S(1)}, u32[]{:S(2)}, u32[]{:S(2)}) collective-permute-start(bf16[24,128]{1,0:T(8,128)(2,1)S(1)} %get-tuple-element.44), channel_id=1, source_target_pairs={{7,5},{0,2},{15,13},{8,10},{23,21},{16,18},{31,29},{24,26},{39,37}... | collective-permute-start | bytes 18440 | tf_op jit(solution)/shard_map/ppermute | solution.py:332
  23.6 1.7 %copy-start.2 = (bf16[8192]{0:T(1024)(128)(2,1)S(1)}, bf16[8192]{0:T(1024)(128)(2,1)}, u32[]{:S(2)}) copy-start(bf16[8192]{0:T(1024)(128)(2,1)} %param.21) | copy-start | bytes 49156
  23.6 5.3 %collective-permute-start.6 = (bf16[24,128]{1,0:T(8,128)(2,1)S(1)}, bf16[24,128]{1,0:T(8,128)(2,1)S(1)}, u32[]{:S(2)}, u32[]{:S(2)}) collective-permute-start(bf16[24,128]{1,0:T(8,128)(2,1)S(1)} %get-tuple-element.43), channel_id=1, source_target_pairs={{7,4},{0,3},{15,12},{8,11},{23,20},{16,19},{31,28},{24,27},{39,36}... | collective-permute-start | bytes 18440 | tf_op jit(solution)/shard_map/ppermute | solution.py:332
  56.4 14.7 %all-to-all-start.2 = ((bf16[32,16,128]{2,1,0:T(8,128)(2,1)}), bf16[32,16,128]{2,1,0:T(8,128)(2,1)S(1)}, u32[]{:S(2)}, u32[]{:S(2)}) async-start(bf16[32,16,128]{2,1,0:T(8,128)(2,1)} %shard_map.113), calls=%async_computation.2 | async-start | bytes 262144 | tf_op jit(solution)/shard_map/all_to_all | solution.py:369
  61.8 3.7 %collective-permute-start.7 = (bf16[16,16,128]{2,1,0:T(8,128)(2,1)S(1)}, bf16[16,16,128]{2,1,0:T(8,128)(2,1)S(1)}, u32[]{:S(2)}, u32[]{:S(2)}) collective-permute-start(bf16[16,16,128]{2,1,0:T(8,128)(2,1)S(1)} %get-tuple-element.30), channel_id=1, source_target_pairs={{0,8},{8,0},{1,9},{9,1},{2,10},{10,2},{3,11},{11,3},{4,12},{12,4},... | collective-permute-start | bytes 196616 | tf_op jit(solution)/shard_map/ppermute | solution.py:349
  65.5 2.8 %copy-start.1 = (bf16[32,8192]{1,0:T(8,128)(2,1)S(1)}, bf16[32,8192]{1,0:T(8,128)(2,1)}, u32[]{:S(2)}) copy-start(bf16[32,8192]{1,0:T(8,128)(2,1)} %z_ref) | copy-start | bytes 1572868

commit v7 on v6

--- a/solution.py
+++ b/solution.py
@@ -63,16 +63,16 @@
 
 def pack_kernel(x_hbm, b_hbm, c_hbm, dt_hbm, decay_hbm, out_ref, *rest):
     rims, (x_ref, b_ref, c_ref, dt_ref, decay_ref, arrived) = rest[:LEADERS], rest[LEADERS:]
-    pairs = ((dt_hbm, dt_ref), (decay_hbm, decay_ref), (b_hbm, b_ref), (c_hbm, c_ref), (x_hbm, x_ref))
+    pairs = ((x_hbm, x_ref), (dt_hbm, dt_ref), (decay_hbm, decay_ref), (b_hbm, b_ref), (c_hbm, c_ref))
     copies = [pltpu.make_async_copy(a, b, arrived.at[i]) for i, (a, b) in enumerate(pairs)]
     for copy in copies:
         copy.start()
-    copies[0].wait()
     copies[1].wait()
+    copies[2].wait()
     steps = jnp.transpose(dt_ref[...].astype(F32))
     decays = jnp.transpose(decay_ref[...].astype(F32))
     at = TILES * ROWS
-    for copy in copies[2:4]:
+    for copy in copies[3:5]:
         copy.wait()
     for core in range(CORES):
         for ring in range(RING):
@@ -84,7 +84,7 @@
             rest = jnp.zeros((MINE, 128 - 2 * ROWS), F32)
             both = jnp.concatenate([steps[head : head + MINE], decays[head : head + MINE], rest], 1)
             out_ref[peer, at + ROWS + HALF :, :] = both.astype(BF16)
-    copies[4].wait()
+    copies[0].wait()
     for core in range(CORES):
         for ring in range(RING):
             for tile in range(TILES):
@@ -200,8 +200,13 @@
         b_conv = conv_silu(taps_ref, pad_ref, span, TILES)
         x_conv = jnp.concatenate([conv_silu(taps_ref, pad_ref, span, tile) for tile in range(TILES)], 1)
         weighted.append((x_conv.astype(F32) * tail).astype(BF16))
-        turned.append(jnp.transpose(b_conv.astype(F32)).astype(BF16))
-    state = jnp.dot(jnp.concatenate(turned, 1), jnp.concatenate(weighted, 0), preferred_element_type=F32)
+        turned.append(b_conv)
+    state = lax.dot_general(
+        jnp.concatenate(turned, 0),
+        jnp.concatenate(weighted, 0),
+        (((0,), (0,)), ((), ())),
+        preferred_element_type=F32,
+    )
     coarse = scale.astype(BF16).astype(F32)
     tail = jnp.concatenate([coarse, scale - coarse, jnp.zeros((6, WIDE), F32)], 0)
     for tile in range(TILES):

time: 94 us -> 93.9 us (level)
  no operation moved by 1% of the time
where the time goes in v7:
time: 93.9 us; the launch traced here: 93.3 us
  blocking collectives  40.6 us (43%)
  starting transfers between devices  29.3 us (31%)
  waiting for transfers between devices  12.8 us (14%)
  Pallas kernels  8.57 us (9%)
  local copies, waits for them, and re-layouts  1.7 us (2%)
    all_to_all x1, blocking collectives, shards(): lax.all_to_all(values.reshape(PEERS, ROWS, WIDE), ('core', 'head'), split...  21 us
    all_to_all x1, blocking collectives, shards(): lax.all_to_all(message, 'seq', split_axis=0, concat_axis=0, tiled=True)  19.6 us
    all_to_all x1, starting transfers between devices, shards(): lax.all_to_all(packed, ('core', 'head'), split_axis=0, concat_axis=0, til...  12 us
    ppermute x3, starting transfers between devices, shards(): handed.append(lax.ppermute(led[member], everyone, pairs))  6.41 us
    all_to_all x1, waiting for transfers between devices, shards(): lax.all_to_all(packed, ('core', 'head'), split_axis=0, concat_axis=0, til...  5.8 us
    all_to_all x1, starting transfers between devices, shards(): lax.all_to_all(chained, 'seq', split_axis=0, concat_axis=0, tiled=True)  5.44 us
    ppermute x3, waiting for transfers between devices, shards(): handed.append(lax.ppermute(led[member], everyone, pairs))  3.59 us
    pallas_call x1, Pallas kernels, shards(): call(local_kernel, (like((SPANS, SPAN, WIDE), F32), like((SPANS, SPAN, ST...  2.82 us
  transfers between devices with their start and end apart: 10, of which 6 were waited for; matrix products, arithmetic and copies ran while one was open for 0% of the time, Pallas kernels for 3%

profile of v7, /device:TPU:1, one launch (start us, length us, event | category | flops | bytes accessed | tf_op | source)
XLA Modules:
  0.0 93.3 jit_solution(10726241385500802651)
XLA Ops:
  0.0 0.0 copy-start
  0.0 2.2 %shard_map.109 = (bf16[16,184,128]{2,1,0:T(8,128)(2,1)}, bf16[4,24,128]{2,1,0:T(8,128)(2,1)}, bf16[4,24,128]{2,1,0:T(8,128)(2,1)}, bf16[4,24,128]{2,1,0:T(8,128)(2,1)}, bf16[4,24,128]{2,1,0:T(8,128)(2,1)}) custom-call(bf16[32,8192]{1,0:T(8,128)(2,1)} %x_hbm.1, bf16[32,1024]{1,0:T(8,128)(2,1)} %b_hbm.1, bf16[32,1024]{1,0:T(8,128)(2,1)} %c_hbm.1, ...), custom_call_target="tpu_custom_call" | custom-call | bytes 1507328 | tf_op jit(solution)/shard_map/pallas_call | solution.py:317
  2.2 0.0 copy-start.8
  2.2 0.0 copy-start.7
  2.2 0.0 copy-start.6
  2.2 0.0 copy-start.5
  2.2 12.0 %all-to-all-start = ((bf16[16,184,128]{2,1,0:T(8,128)(2,1)}), bf16[16,184,128]{2,1,0:T(8,128)(2,1)S(1)}, u32[]{:S(2)}, u32[]{:S(2)}) async-start(bf16[16,184,128]{2,1,0:T(8,128)(2,1)} %get-tuple-element.24), calls=%async_computation | async-start | bytes 1507328 | tf_op jit(solution)/shard_map/all_to_all | solution.py:326
  14.2 0.0 copy-done.8
  14.2 0.7 collective-permute-start
  14.9 0.0 copy-done.7
  14.9 0.7 collective-permute-start.1
  15.6 0.0 copy-done.6
  15.6 0.7 collective-permute-start.2
  16.3 0.0 copy-done.5
  16.3 0.7 collective-permute-start.3
  16.9 0.0 copy-done
  17.0 0.0 copy-start.3
  17.0 0.0 copy-start.4
  17.0 0.6 copy-done.3
  17.6 0.0 copy-done.4
  17.7 0.0 copy-start.9
  17.7 0.7 copy-done.9
  18.3 0.1 dynamic_slice.7
  18.4 0.1 broadcast_in_dim.9
  18.5 0.1 reshape.16
  18.6 0.1 pad.7.clone
  18.6 0.0 collective-permute-done
  18.6 0.0 collective-permute-done.1
  18.6 0.0 collective-permute-done.2
  18.6 0.0 collective-permute-done.3
  18.7 3.3 %collective-permute-start.4 = (bf16[24,128]{1,0:T(8,128)(2,1)S(1)}, bf16[24,128]{1,0:T(8,128)(2,1)S(1)}, u32[]{:S(2)}, u32[]{:S(2)}) collective-permute-start(bf16[24,128]{1,0:T(8,128)(2,1)S(1)} %get-tuple-element.45), channel_id=1, source_target_pairs={{7,6},{0,1},{15,14},{8,9},{23,22},{16,17},{31,30},{24,25},{39,38},... | collective-permute-start | bytes 18440 | tf_op jit(solution)/shard_map/ppermute | solution.py:337
  22.0 1.6 %collective-permute-start.5 = (bf16[24,128]{1,0:T(8,128)(2,1)S(1)}, bf16[24,128]{1,0:T(8,128)(2,1)S(1)}, u32[]{:S(2)}, u32[]{:S(2)}) collective-permute-start(bf16[24,128]{1,0:T(8,128)(2,1)S(1)} %get-tuple-element.44), channel_id=1, source_target_pairs={{7,5},{0,2},{15,13},{8,10},{23,21},{16,18},{31,29},{24,26},{39,37}... | collective-permute-start | bytes 18440 | tf_op jit(solution)/shard_map/ppermute | solution.py:337
  23.5 0.0 copy-start.2
  23.6 1.6 %collective-permute-start.6 = (bf16[24,128]{1,0:T(8,128)(2,1)S(1)}, bf16[24,128]{1,0:T(8,128)(2,1)S(1)}, u32[]{:S(2)}, u32[]{:S(2)}) collective-permute-start(bf16[24,128]{1,0:T(8,128)(2,1)S(1)} %get-tuple-element.43), channel_id=1, source_target_pairs={{7,4},{0,3},{15,12},{8,11},{23,20},{16,19},{31,28},{24,27},{39,36}... | collective-permute-start | bytes 18440 | tf_op jit(solution)/shard_map/ppermute | solution.py:337
  25.1 0.1 maximum_maximum_fusion.taps_ref
  25.2 0.0 copy-done.2
  25.2 2.9 %collective-permute-done.4.rest_1_ = bf16[24,128]{1,0:T(8,128)(2,1)S(1)} collective-permute-done((bf16[24,128]{1,0:T(8,128)(2,1)S(1)}, bf16[24,128]{1,0:T(8,128)(2,1)S(1)}, u32[]{:S(2)}, u32[]{:S(2)}) %collective-permute-start.4) | collective-permute-done | bytes 6176 | tf_op jit(solution)/shard_map/ppermute | solution.py:337
  28.1 0.2 collective-permute-done.5.rest_2_
  28.4 0.5 collective-permute-done.6.rest_3_
  28.8 5.8 %all-to-all-done.r_ref = bf16[16,184,128]{2,1,0:T(8,128)(2,1)S(1)} async-done(((bf16[16,184,128]{2,1,0:T(8,128)(2,1)}), bf16[16,184,128]{2,1,0:T(8,128)(2,1)S(1)}, u32[]{:S(2)}, u32[]{:S(2)}) %all-to-all-start) | async-done | bytes 753696 | tf_op jit(solution)/shard_map/all_to_all | solution.py:326
  34.6 1.3 %shard_map.110 = (bf16[32,24,128]{2,1,0:T(8,128)(2,1)S(1)}, bf16[16,16,128]{2,1,0:T(8,128)(2,1)S(1)}) custom-call(bf16[16,184,128]{2,1,0:T(8,128)(2,1)S(1)} %all-to-all-done.r_ref, f32[8,768]{1,0:T(8,128)S(1)} %maximum_maximum_fusion.taps_ref, bf16[4,24,128]{2,1,0:T(8,128)(2,1)S(1)} %add_add_fusion.rest_0_, ...), custom_call_target="tpu_custom_call" | custom-call | flops 1000000000 | bytes 2000000 | tf_op jit(solution)/shard_map/pallas_call | solution.py:346
  36.0 19.6 %all_to_all.20.all_ref = bf16[32,24,128]{2,1,0:T(8,128)(2,1)S(1)} all-to-all(bf16[32,24,128]{2,1,0:T(8,128)(2,1)S(1)} %get-tuple-element.32), channel_id=1, replica_groups=mesh['seq'=32,'core'=2,'head'=8] {'seq'}, dimensions={0} | all-to-all | bytes 393216 | tf_op jit(solution)/shard_map/all_to_all | solution.py:353
  55.6 0.7 shard_map.113
  56.3 5.4 %all-to-all-start.2 = ((bf16[32,16,128]{2,1,0:T(8,128)(2,1)}), bf16[32,16,128]{2,1,0:T(8,128)(2,1)S(1)}, u32[]{:S(2)}, u32[]{:S(2)}) async-start(bf16[32,16,128]{2,1,0:T(8,128)(2,1)} %shard_map.113), calls=%async_computation.2 | async-start | bytes 262144 | tf_op jit(solution)/shard_map/all_to_all | solution.py:374
  61.8 2.8 %collective-permute-start.7 = (bf16[16,16,128]{2,1,0:T(8,128)(2,1)S(1)}, bf16[16,16,128]{2,1,0:T(8,128)(2,1)S(1)}, u32[]{:S(2)}, u32[]{:S(2)}) collective-permute-start(bf16[16,16,128]{2,1,0:T(8,128)(2,1)S(1)} %get-tuple-element.30), channel_id=1, source_target_pairs={{0,8},{8,0},{1,9},{9,1},{2,10},{10,2},{3,11},{11,3},{4,12},{12,4},... | collective-permute-start | bytes 196616 | tf_op jit(solution)/shard_map/ppermute | solution.py:354
  64.6 0.9 collective-permute-done.7.other_ref
  65.5 0.0 copy-start.1
  65.5 2.8 %shard_map.111 = (f32[4,128,512]{2,1,0:T(8,128)S(1)}, bf16[4,128,128]{2,1,0:T(8,128)(2,1)S(1)}, f32[4,128,512]{2,1,0:T(8,128)S(1)}) custom-call(s32[1]{0:T(128)} %bitcast.core_ref, bf16[16,184,128]{2,1,0:T(8,128)(2,1)S(1)} %all-to-all-done.r_ref, bf16[16,16,128]{2,1,0:T(8,128)(2,1)S(1)} %collective-permute-done.7.other_ref, ...), custom_call_target="tpu_custom_call" | custom-call | flops 1000000000 | bytes 8000000 | tf_op jit(solution)/shard_map/pallas_call | solution.py:356
  68.3 0.0 copy-done.1
  68.3 0.2 shard_map.112
  68.5 2.6 %all-to-all-done.2 = bf16[32,16,128]{2,1,0:T(8,128)(2,1)S(1)} async-done(((bf16[32,16,128]{2,1,0:T(8,128)(2,1)}), bf16[32,16,128]{2,1,0:T(8,128)(2,1)S(1)}, u32[]{:S(2)}, u32[]{:S(2)}) %all-to-all-start.2) | async-done | bytes 131104 | tf_op jit(solution)/shard_map/all_to_all | solution.py:374
  71.1 0.3 shard_map.114
  71.3 21.0 %all_to_all.21.values_ref = bf16[16,32,512]{2,1,0:T(8,128)(2,1)S(1)} all-to-all(bf16[16,32,512]{2,1,0:T(8,128)(2,1)S(1)} %bitcast.9), channel_id=1, replica_groups=mesh['seq'=32,'core'=2,'head'=8] {'core','head'}, dimensions={0} | all-to-all | bytes 1048576 | tf_op jit(solution)/shard_map/all_to_all | solution.py:382
  92.3 1.0 %shard_map.115 = bf16[32,8192]{1,0:T(8,128)(2,1)} custom-call(bf16[16,32,512]{2,1,0:T(8,128)(2,1)S(1)} %all_to_all.21.values_ref, f32[32,8192]{1,0:T(8,128)S(1)} %get-tuple-element.41.gate_ref, f32[1,8192]{1,0:T(1,128)S(1)} %get-tuple-element.42.gain_ref), custom_call_target="tpu_custom_call" | custom-call | flops 10000000 | bytes 2000000 | tf_op jit(solution)/shard_map/pallas_call | solution.py:385
  (8 shorter events, 0.1 us)
Async XLA Ops:
  0.0 16.9 %copy-start = (bf16[4,1024]{1,0:T(4,128)(2,1)S(1)}, bf16[4,1024]{1,0:T(4,128)(2,1)}, u32[]{:S(2)}) copy-start(bf16[4,1024]{1,0:T(4,128)(2,1)} %param.17) | copy-start | bytes 24580
  2.2 12.0 %copy-start.8 = (bf16[4,24,128]{2,1,0:T(8,128)(2,1)S(1)}, bf16[4,24,128]{2,1,0:T(8,128)(2,1)}, u32[]{:S(2)}) copy-start(bf16[4,24,128]{2,1,0:T(8,128)(2,1)} %get-tuple-element.26) | copy-start | bytes 73732
  2.2 12.7 %copy-start.7 = (bf16[4,24,128]{2,1,0:T(8,128)(2,1)S(1)}, bf16[4,24,128]{2,1,0:T(8,128)(2,1)}, u32[]{:S(2)}) copy-start(bf16[4,24,128]{2,1,0:T(8,128)(2,1)} %get-tuple-element.27) | copy-start | bytes 73732
  2.2 13.4 %copy-start.6 = (bf16[4,24,128]{2,1,0:T(8,128)(2,1)S(1)}, bf16[4,24,128]{2,1,0:T(8,128)(2,1)}, u32[]{:S(2)}) copy-start(bf16[4,24,128]{2,1,0:T(8,128)(2,1)} %get-tuple-element.28) | copy-start | bytes 73732
  2.2 14.0 %copy-start.5 = (bf16[4,24,128]{2,1,0:T(8,128)(2,1)S(1)}, bf16[4,24,128]{2,1,0:T(8,128)(2,1)}, u32[]{:S(2)}) copy-start(bf16[4,24,128]{2,1,0:T(8,128)(2,1)} %get-tuple-element.29) | copy-start | bytes 73732
  2.2 32.4 %all-to-all-start = ((bf16[16,184,128]{2,1,0:T(8,128)(2,1)}), bf16[16,184,128]{2,1,0:T(8,128)(2,1)S(1)}, u32[]{:S(2)}, u32[]{:S(2)}) async-start(bf16[16,184,128]{2,1,0:T(8,128)(2,1)} %get-tuple-element.24), calls=%async_computation | async-start | bytes 1507328 | tf_op jit(solution)/shard_map/all_to_all | solution.py:326
  14.2 4.4 %collective-permute-start = (bf16[4,24,128]{2,1,0:T(8,128)(2,1)S(1)}, bf16[4,24,128]{2,1,0:T(8,128)(2,1)S(1)}, u32[]{:S(2)}, u32[]{:S(2)}) collective-permute-start(bf16[4,24,128]{2,1,0:T(8,128)(2,1)S(1)} %copy-done.8), channel_id=1, source_target_pairs={{15,23},{31,39},{47,55},{63,71},{79,87},{95,103},{111,119},{127,13... | collective-permute-start | bytes 73736 | tf_op jit(solution)/shard_map/ppermute | solution.py:332
  14.9 3.7 %collective-permute-start.1 = (bf16[4,24,128]{2,1,0:T(8,128)(2,1)S(1)}, bf16[4,24,128]{2,1,0:T(8,128)(2,1)S(1)}, u32[]{:S(2)}, u32[]{:S(2)}) collective-permute-start(bf16[4,24,128]{2,1,0:T(8,128)(2,1)S(1)} %copy-done.7), channel_id=1, source_target_pairs={{15,16},{31,32},{47,48},{63,64},{79,80},{95,96},{111,112},{127,128... | collective-permute-start | bytes 73736 | tf_op jit(solution)/shard_map/ppermute | solution.py:332
  15.6 3.1 %collective-permute-start.2 = (bf16[4,24,128]{2,1,0:T(8,128)(2,1)S(1)}, bf16[4,24,128]{2,1,0:T(8,128)(2,1)S(1)}, u32[]{:S(2)}, u32[]{:S(2)}) collective-permute-start(bf16[4,24,128]{2,1,0:T(8,128)(2,1)S(1)} %copy-done.6), channel_id=1, source_target_pairs={{15,31},{31,47},{47,63},{63,79},{79,95},{95,111},{111,127},{127,14... | collective-permute-start | bytes 73736 | tf_op jit(solution)/shard_map/ppermute | solution.py:332
  16.3 2.4 %collective-permute-start.3 = (bf16[4,24,128]{2,1,0:T(8,128)(2,1)S(1)}, bf16[4,24,128]{2,1,0:T(8,128)(2,1)S(1)}, u32[]{:S(2)}, u32[]{:S(2)}) collective-permute-start(bf16[4,24,128]{2,1,0:T(8,128)(2,1)S(1)} %copy-done.5), channel_id=1, source_target_pairs={{15,24},{31,40},{47,56},{63,72},{79,88},{95,104},{111,120},{127,13... | collective-permute-start | bytes 73736 | tf_op jit(solution)/shard_map/ppermute | solution.py:332
  17.0 0.7 copy-start.3
  17.0 0.7 copy-start.4
  17.7 0.7 copy-start.9
  18.7 9.4 %collective-permute-start.4 = (bf16[24,128]{1,0:T(8,128)(2,1)S(1)}, bf16[24,128]{1,0:T(8,128)(2,1)S(1)}, u32[]{:S(2)}, u32[]{:S(2)}) collective-permute-start(bf16[24,128]{1,0:T(8,128)(2,1)S(1)} %get-tuple-element.45), channel_id=1, source_target_pairs={{7,6},{0,1},{15,14},{8,9},{23,22},{16,17},{31,30},{24,25},{39,38},... | collective-permute-start | bytes 18440 | tf_op jit(solution)/shard_map/ppermute | solution.py:337
  22.0 6.4 %collective-permute-start.5 = (bf16[24,128]{1,0:T(8,128)(2,1)S(1)}, bf16[24,128]{1,0:T(8,128)(2,1)S(1)}, u32[]{:S(2)}, u32[]{:S(2)}) collective-permute-start(bf16[24,128]{1,0:T(8,128)(2,1)S(1)} %get-tuple-element.44), channel_id=1, source_target_pairs={{7,5},{0,2},{15,13},{8,10},{23,21},{16,18},{31,29},{24,26},{39,37}... | collective-permute-start | bytes 18440 | tf_op jit(solution)/shard_map/ppermute | solution.py:337
  23.5 1.7 %copy-start.2 = (bf16[8192]{0:T(1024)(128)(2,1)S(1)}, bf16[8192]{0:T(1024)(128)(2,1)}, u32[]{:S(2)}) copy-start(bf16[8192]{0:T(1024)(128)(2,1)} %param.21) | copy-start | bytes 49156
  23.6 5.3 %collective-permute-start.6 = (bf16[24,128]{1,0:T(8,128)(2,1)S(1)}, bf16[24,128]{1,0:T(8,128)(2,1)S(1)}, u32[]{:S(2)}, u32[]{:S(2)}) collective-permute-start(bf16[24,128]{1,0:T(8,128)(2,1)S(1)} %get-tuple-element.43), channel_id=1, source_target_pairs={{7,4},{0,3},{15,12},{8,11},{23,20},{16,19},{31,28},{24,27},{39,36}... | collective-permute-start | bytes 18440 | tf_op jit(solution)/shard_map/ppermute | solution.py:337
  56.3 14.7 %all-to-all-start.2 = ((bf16[32,16,128]{2,1,0:T(8,128)(2,1)}), bf16[32,16,128]{2,1,0:T(8,128)(2,1)S(1)}, u32[]{:S(2)}, u32[]{:S(2)}) async-start(bf16[32,16,128]{2,1,0:T(8,128)(2,1)} %shard_map.113), calls=%async_computation.2 | async-start | bytes 262144 | tf_op jit(solution)/shard_map/all_to_all | solution.py:374
  61.8 3.7 %collective-permute-start.7 = (bf16[16,16,128]{2,1,0:T(8,128)(2,1)S(1)}, bf16[16,16,128]{2,1,0:T(8,128)(2,1)S(1)}, u32[]{:S(2)}, u32[]{:S(2)}) collective-permute-start(bf16[16,16,128]{2,1,0:T(8,128)(2,1)S(1)} %get-tuple-element.30), channel_id=1, source_target_pairs={{0,8},{8,0},{1,9},{9,1},{2,10},{10,2},{3,11},{11,3},{4,12},{12,4},... | collective-permute-start | bytes 196616 | tf_op jit(solution)/shard_map/ppermute | solution.py:354
  65.5 2.8 %copy-start.1 = (bf16[32,8192]{1,0:T(8,128)(2,1)S(1)}, bf16[32,8192]{1,0:T(8,128)(2,1)}, u32[]{:S(2)}) copy-start(bf16[32,8192]{1,0:T(8,128)(2,1)} %z_ref) | copy-start | bytes 1572868

commit v8 on v7

--- a/solution.py
+++ b/solution.py
@@ -208,12 +208,13 @@
         preferred_element_type=F32,
     )
     coarse = scale.astype(BF16).astype(F32)
-    tail = jnp.concatenate([coarse, scale - coarse, jnp.zeros((6, WIDE), F32)], 0)
+    tail = jnp.concatenate([coarse, scale - coarse, jnp.zeros((6, WIDE), F32)], 0).astype(BF16)
+    state = state.astype(BF16)
     for tile in range(TILES):
         here = slice(tile * 128, (tile + 1) * 128)
         for cut in range(STATE // CUT):
-            whole = jnp.concatenate([state[cut * CUT : (cut + 1) * CUT, here], tail[:, here]], 0)
-            message_ref[tile * (STATE // CUT) + cut] = whole.astype(BF16)
+            message_ref[tile * (STATE // CUT) + cut, :CUT] = state[cut * CUT : (cut + 1) * CUT, here]
+            message_ref[tile * (STATE // CUT) + cut, CUT:] = tail[:, here]
 
 
 def local_kernel(core_ref, r_ref, other_ref, taps_ref, *rest):

time: 93.9 us -> 93.9 us (level)
  no operation moved by 1% of the time
where the time goes in v8:
time: 93.9 us; the launch traced here: 93.3 us
  blocking collectives  40.6 us (43%)
  starting transfers between devices  29.3 us (31%)
  waiting for transfers between devices  12.8 us (14%)
  Pallas kernels  8.57 us (9%)
  local copies, waits for them, and re-layouts  1.7 us (2%)
    all_to_all x1, blocking collectives, shards(): lax.all_to_all(values.reshape(PEERS, ROWS, WIDE), ('core', 'head'), split...  21 us
    all_to_all x1, blocking collectives, shards(): lax.all_to_all(message, 'seq', split_axis=0, concat_axis=0, tiled=True)  19.6 us
    all_to_all x1, starting transfers between devices, shards(): lax.all_to_all(packed, ('core', 'head'), split_axis=0, concat_axis=0, til...  12 us
    ppermute x3, starting transfers between devices, shards(): handed.append(lax.ppermute(led[member], everyone, pairs))  6.41 us
    all_to_all x1, waiting for transfers between devices, shards(): lax.all_to_all(packed, ('core', 'head'), split_axis=0, concat_axis=0, til...  5.8 us
    all_to_all x1, starting transfers between devices, shards(): lax.all_to_all(chained, 'seq', split_axis=0, concat_axis=0, tiled=True)  5.44 us
    ppermute x3, waiting for transfers between devices, shards(): handed.append(lax.ppermute(led[member], everyone, pairs))  3.59 us
    pallas_call x1, Pallas kernels, shards(): call(local_kernel, (like((SPANS, SPAN, WIDE), F32), like((SPANS, SPAN, ST...  2.82 us
  transfers between devices with their start and end apart: 10, of which 6 were waited for; matrix products, arithmetic and copies ran while one was open for 0% of the time, Pallas kernels for 3%

profile of v8, /device:TPU:1, one launch (start us, length us, event | category | flops | bytes accessed | tf_op | source)
XLA Modules:
  0.0 93.3 jit_solution(10726241385500802651)
XLA Ops:
  0.0 0.0 copy-start
  0.0 2.2 %shard_map.109 = (bf16[16,184,128]{2,1,0:T(8,128)(2,1)}, bf16[4,24,128]{2,1,0:T(8,128)(2,1)}, bf16[4,24,128]{2,1,0:T(8,128)(2,1)}, bf16[4,24,128]{2,1,0:T(8,128)(2,1)}, bf16[4,24,128]{2,1,0:T(8,128)(2,1)}) custom-call(bf16[32,8192]{1,0:T(8,128)(2,1)} %x_hbm.1, bf16[32,1024]{1,0:T(8,128)(2,1)} %b_hbm.1, bf16[32,1024]{1,0:T(8,128)(2,1)} %c_hbm.1, ...), custom_call_target="tpu_custom_call" | custom-call | bytes 1507328 | tf_op jit(solution)/shard_map/pallas_call | solution.py:318
  2.2 0.0 copy-start.8
  2.2 0.0 copy-start.7
  2.2 0.0 copy-start.6
  2.2 0.0 copy-start.5
  2.2 12.0 %all-to-all-start = ((bf16[16,184,128]{2,1,0:T(8,128)(2,1)}), bf16[16,184,128]{2,1,0:T(8,128)(2,1)S(1)}, u32[]{:S(2)}, u32[]{:S(2)}) async-start(bf16[16,184,128]{2,1,0:T(8,128)(2,1)} %get-tuple-element.24), calls=%async_computation | async-start | bytes 1507328 | tf_op jit(solution)/shard_map/all_to_all | solution.py:327
  14.2 0.0 copy-done.8
  14.2 0.7 collective-permute-start
  14.9 0.0 copy-done.7
  14.9 0.7 collective-permute-start.1
  15.6 0.0 copy-done.6
  15.6 0.7 collective-permute-start.2
  16.3 0.0 copy-done.5
  16.3 0.7 collective-permute-start.3
  16.9 0.0 copy-done
  17.0 0.0 copy-start.3
  17.0 0.0 copy-start.4
  17.0 0.6 copy-done.3
  17.6 0.0 copy-done.4
  17.7 0.0 copy-start.9
  17.7 0.7 copy-done.9
  18.3 0.1 dynamic_slice.7
  18.4 0.1 broadcast_in_dim.9
  18.5 0.1 reshape.16
  18.6 0.1 pad.7.clone
  18.6 0.0 collective-permute-done
  18.6 0.0 collective-permute-done.1
  18.6 0.0 collective-permute-done.2
  18.6 0.0 collective-permute-done.3
  18.7 3.3 %collective-permute-start.4 = (bf16[24,128]{1,0:T(8,128)(2,1)S(1)}, bf16[24,128]{1,0:T(8,128)(2,1)S(1)}, u32[]{:S(2)}, u32[]{:S(2)}) collective-permute-start(bf16[24,128]{1,0:T(8,128)(2,1)S(1)} %get-tuple-element.45), channel_id=1, source_target_pairs={{7,6},{0,1},{15,14},{8,9},{23,22},{16,17},{31,30},{24,25},{39,38},... | collective-permute-start | bytes 18440 | tf_op jit(solution)/shard_map/ppermute | solution.py:338
  22.0 1.6 %collective-permute-start.5 = (bf16[24,128]{1,0:T(8,128)(2,1)S(1)}, bf16[24,128]{1,0:T(8,128)(2,1)S(1)}, u32[]{:S(2)}, u32[]{:S(2)}) collective-permute-start(bf16[24,128]{1,0:T(8,128)(2,1)S(1)} %get-tuple-element.44), channel_id=1, source_target_pairs={{7,5},{0,2},{15,13},{8,10},{23,21},{16,18},{31,29},{24,26},{39,37}... | collective-permute-start | bytes 18440 | tf_op jit(solution)/shard_map/ppermute | solution.py:338
  23.5 0.0 copy-start.2
  23.6 1.6 %collective-permute-start.6 = (bf16[24,128]{1,0:T(8,128)(2,1)S(1)}, bf16[24,128]{1,0:T(8,128)(2,1)S(1)}, u32[]{:S(2)}, u32[]{:S(2)}) collective-permute-start(bf16[24,128]{1,0:T(8,128)(2,1)S(1)} %get-tuple-element.43), channel_id=1, source_target_pairs={{7,4},{0,3},{15,12},{8,11},{23,20},{16,19},{31,28},{24,27},{39,36}... | collective-permute-start | bytes 18440 | tf_op jit(solution)/shard_map/ppermute | solution.py:338
  25.1 0.1 maximum_maximum_fusion.taps_ref
  25.2 0.0 copy-done.2
  25.2 2.9 %collective-permute-done.4.rest_1_ = bf16[24,128]{1,0:T(8,128)(2,1)S(1)} collective-permute-done((bf16[24,128]{1,0:T(8,128)(2,1)S(1)}, bf16[24,128]{1,0:T(8,128)(2,1)S(1)}, u32[]{:S(2)}, u32[]{:S(2)}) %collective-permute-start.4) | collective-permute-done | bytes 6176 | tf_op jit(solution)/shard_map/ppermute | solution.py:338
  28.1 0.2 collective-permute-done.5.rest_2_
  28.4 0.5 collective-permute-done.6.rest_3_
  28.8 5.8 %all-to-all-done.r_ref = bf16[16,184,128]{2,1,0:T(8,128)(2,1)S(1)} async-done(((bf16[16,184,128]{2,1,0:T(8,128)(2,1)}), bf16[16,184,128]{2,1,0:T(8,128)(2,1)S(1)}, u32[]{:S(2)}, u32[]{:S(2)}) %all-to-all-start) | async-done | bytes 753696 | tf_op jit(solution)/shard_map/all_to_all | solution.py:327
  34.6 1.3 %shard_map.110 = (bf16[32,24,128]{2,1,0:T(8,128)(2,1)S(1)}, bf16[16,16,128]{2,1,0:T(8,128)(2,1)S(1)}) custom-call(bf16[16,184,128]{2,1,0:T(8,128)(2,1)S(1)} %all-to-all-done.r_ref, f32[8,768]{1,0:T(8,128)S(1)} %maximum_maximum_fusion.taps_ref, bf16[4,24,128]{2,1,0:T(8,128)(2,1)S(1)} %add_add_fusion.rest_0_, ...), custom_call_target="tpu_custom_call" | custom-call | flops 1000000000 | bytes 2000000 | tf_op jit(solution)/shard_map/pallas_call | solution.py:347
  36.0 19.6 %all_to_all.20.all_ref = bf16[32,24,128]{2,1,0:T(8,128)(2,1)S(1)} all-to-all(bf16[32,24,128]{2,1,0:T(8,128)(2,1)S(1)} %get-tuple-element.32), channel_id=1, replica_groups=mesh['seq'=32,'core'=2,'head'=8] {'seq'}, dimensions={0} | all-to-all | bytes 393216 | tf_op jit(solution)/shard_map/all_to_all | solution.py:354
  55.6 0.7 shard_map.113
  56.3 5.4 %all-to-all-start.2 = ((bf16[32,16,128]{2,1,0:T(8,128)(2,1)}), bf16[32,16,128]{2,1,0:T(8,128)(2,1)S(1)}, u32[]{:S(2)}, u32[]{:S(2)}) async-start(bf16[32,16,128]{2,1,0:T(8,128)(2,1)} %shard_map.113), calls=%async_computation.2 | async-start | bytes 262144 | tf_op jit(solution)/shard_map/all_to_all | solution.py:375
  61.8 2.8 %collective-permute-start.7 = (bf16[16,16,128]{2,1,0:T(8,128)(2,1)S(1)}, bf16[16,16,128]{2,1,0:T(8,128)(2,1)S(1)}, u32[]{:S(2)}, u32[]{:S(2)}) collective-permute-start(bf16[16,16,128]{2,1,0:T(8,128)(2,1)S(1)} %get-tuple-element.30), channel_id=1, source_target_pairs={{0,8},{8,0},{1,9},{9,1},{2,10},{10,2},{3,11},{11,3},{4,12},{12,4},... | collective-permute-start | bytes 196616 | tf_op jit(solution)/shard_map/ppermute | solution.py:355
  64.6 0.9 collective-permute-done.7.other_ref
  65.5 0.0 copy-start.1
  65.5 2.8 %shard_map.111 = (f32[4,128,512]{2,1,0:T(8,128)S(1)}, bf16[4,128,128]{2,1,0:T(8,128)(2,1)S(1)}, f32[4,128,512]{2,1,0:T(8,128)S(1)}) custom-call(s32[1]{0:T(128)} %bitcast.core_ref, bf16[16,184,128]{2,1,0:T(8,128)(2,1)S(1)} %all-to-all-done.r_ref, bf16[16,16,128]{2,1,0:T(8,128)(2,1)S(1)} %collective-permute-done.7.other_ref, ...), custom_call_target="tpu_custom_call" | custom-call | flops 1000000000 | bytes 8000000 | tf_op jit(solution)/shard_map/pallas_call | solution.py:357
  68.3 0.0 copy-done.1
  68.3 0.2 shard_map.112
  68.5 2.6 %all-to-all-done.2 = bf16[32,16,128]{2,1,0:T(8,128)(2,1)S(1)} async-done(((bf16[32,16,128]{2,1,0:T(8,128)(2,1)}), bf16[32,16,128]{2,1,0:T(8,128)(2,1)S(1)}, u32[]{:S(2)}, u32[]{:S(2)}) %all-to-all-start.2) | async-done | bytes 131104 | tf_op jit(solution)/shard_map/all_to_all | solution.py:375
  71.1 0.3 shard_map.114
  71.3 21.0 %all_to_all.21.values_ref = bf16[16,32,512]{2,1,0:T(8,128)(2,1)S(1)} all-to-all(bf16[16,32,512]{2,1,0:T(8,128)(2,1)S(1)} %bitcast.9), channel_id=1, replica_groups=mesh['seq'=32,'core'=2,'head'=8] {'core','head'}, dimensions={0} | all-to-all | bytes 1048576 | tf_op jit(solution)/shard_map/all_to_all | solution.py:383
  92.3 1.0 %shard_map.115 = bf16[32,8192]{1,0:T(8,128)(2,1)} custom-call(bf16[16,32,512]{2,1,0:T(8,128)(2,1)S(1)} %all_to_all.21.values_ref, f32[32,8192]{1,0:T(8,128)S(1)} %get-tuple-element.41.gate_ref, f32[1,8192]{1,0:T(1,128)S(1)} %get-tuple-element.42.gain_ref), custom_call_target="tpu_custom_call" | custom-call | flops 10000000 | bytes 2000000 | tf_op jit(solution)/shard_map/pallas_call | solution.py:386
  (8 shorter events, 0.1 us)
Async XLA Ops:
  0.0 16.9 %copy-start = (bf16[4,1024]{1,0:T(4,128)(2,1)S(1)}, bf16[4,1024]{1,0:T(4,128)(2,1)}, u32[]{:S(2)}) copy-start(bf16[4,1024]{1,0:T(4,128)(2,1)} %param.17) | copy-start | bytes 24580
  2.2 12.0 %copy-start.8 = (bf16[4,24,128]{2,1,0:T(8,128)(2,1)S(1)}, bf16[4,24,128]{2,1,0:T(8,128)(2,1)}, u32[]{:S(2)}) copy-start(bf16[4,24,128]{2,1,0:T(8,128)(2,1)} %get-tuple-element.26) | copy-start | bytes 73732
  2.2 12.7 %copy-start.7 = (bf16[4,24,128]{2,1,0:T(8,128)(2,1)S(1)}, bf16[4,24,128]{2,1,0:T(8,128)(2,1)}, u32[]{:S(2)}) copy-start(bf16[4,24,128]{2,1,0:T(8,128)(2,1)} %get-tuple-element.27) | copy-start | bytes 73732
  2.2 13.4 %copy-start.6 = (bf16[4,24,128]{2,1,0:T(8,128)(2,1)S(1)}, bf16[4,24,128]{2,1,0:T(8,128)(2,1)}, u32[]{:S(2)}) copy-start(bf16[4,24,128]{2,1,0:T(8,128)(2,1)} %get-tuple-element.28) | copy-start | bytes 73732
  2.2 14.0 %copy-start.5 = (bf16[4,24,128]{2,1,0:T(8,128)(2,1)S(1)}, bf16[4,24,128]{2,1,0:T(8,128)(2,1)}, u32[]{:S(2)}) copy-start(bf16[4,24,128]{2,1,0:T(8,128)(2,1)} %get-tuple-element.29) | copy-start | bytes 73732
  2.2 32.4 %all-to-all-start = ((bf16[16,184,128]{2,1,0:T(8,128)(2,1)}), bf16[16,184,128]{2,1,0:T(8,128)(2,1)S(1)}, u32[]{:S(2)}, u32[]{:S(2)}) async-start(bf16[16,184,128]{2,1,0:T(8,128)(2,1)} %get-tuple-element.24), calls=%async_computation | async-start | bytes 1507328 | tf_op jit(solution)/shard_map/all_to_all | solution.py:327
  14.2 4.4 %collective-permute-start = (bf16[4,24,128]{2,1,0:T(8,128)(2,1)S(1)}, bf16[4,24,128]{2,1,0:T(8,128)(2,1)S(1)}, u32[]{:S(2)}, u32[]{:S(2)}) collective-permute-start(bf16[4,24,128]{2,1,0:T(8,128)(2,1)S(1)} %copy-done.8), channel_id=1, source_target_pairs={{15,23},{31,39},{47,55},{63,71},{79,87},{95,103},{111,119},{127,13... | collective-permute-start | bytes 73736 | tf_op jit(solution)/shard_map/ppermute | solution.py:333
  14.9 3.7 %collective-permute-start.1 = (bf16[4,24,128]{2,1,0:T(8,128)(2,1)S(1)}, bf16[4,24,128]{2,1,0:T(8,128)(2,1)S(1)}, u32[]{:S(2)}, u32[]{:S(2)}) collective-permute-start(bf16[4,24,128]{2,1,0:T(8,128)(2,1)S(1)} %copy-done.7), channel_id=1, source_target_pairs={{15,16},{31,32},{47,48},{63,64},{79,80},{95,96},{111,112},{127,128... | collective-permute-start | bytes 73736 | tf_op jit(solution)/shard_map/ppermute | solution.py:333
  15.6 3.1 %collective-permute-start.2 = (bf16[4,24,128]{2,1,0:T(8,128)(2,1)S(1)}, bf16[4,24,128]{2,1,0:T(8,128)(2,1)S(1)}, u32[]{:S(2)}, u32[]{:S(2)}) collective-permute-start(bf16[4,24,128]{2,1,0:T(8,128)(2,1)S(1)} %copy-done.6), channel_id=1, source_target_pairs={{15,31},{31,47},{47,63},{63,79},{79,95},{95,111},{111,127},{127,14... | collective-permute-start | bytes 73736 | tf_op jit(solution)/shard_map/ppermute | solution.py:333
  16.3 2.4 %collective-permute-start.3 = (bf16[4,24,128]{2,1,0:T(8,128)(2,1)S(1)}, bf16[4,24,128]{2,1,0:T(8,128)(2,1)S(1)}, u32[]{:S(2)}, u32[]{:S(2)}) collective-permute-start(bf16[4,24,128]{2,1,0:T(8,128)(2,1)S(1)} %copy-done.5), channel_id=1, source_target_pairs={{15,24},{31,40},{47,56},{63,72},{79,88},{95,104},{111,120},{127,13... | collective-permute-start | bytes 73736 | tf_op jit(solution)/shard_map/ppermute | solution.py:333
  17.0 0.7 copy-start.3
  17.0 0.7 copy-start.4
  17.7 0.7 copy-start.9
  18.7 9.4 %collective-permute-start.4 = (bf16[24,128]{1,0:T(8,128)(2,1)S(1)}, bf16[24,128]{1,0:T(8,128)(2,1)S(1)}, u32[]{:S(2)}, u32[]{:S(2)}) collective-permute-start(bf16[24,128]{1,0:T(8,128)(2,1)S(1)} %get-tuple-element.45), channel_id=1, source_target_pairs={{7,6},{0,1},{15,14},{8,9},{23,22},{16,17},{31,30},{24,25},{39,38},... | collective-permute-start | bytes 18440 | tf_op jit(solution)/shard_map/ppermute | solution.py:338
  22.0 6.4 %collective-permute-start.5 = (bf16[24,128]{1,0:T(8,128)(2,1)S(1)}, bf16[24,128]{1,0:T(8,128)(2,1)S(1)}, u32[]{:S(2)}, u32[]{:S(2)}) collective-permute-start(bf16[24,128]{1,0:T(8,128)(2,1)S(1)} %get-tuple-element.44), channel_id=1, source_target_pairs={{7,5},{0,2},{15,13},{8,10},{23,21},{16,18},{31,29},{24,26},{39,37}... | collective-permute-start | bytes 18440 | tf_op jit(solution)/shard_map/ppermute | solution.py:338
  23.5 1.7 %copy-start.2 = (bf16[8192]{0:T(1024)(128)(2,1)S(1)}, bf16[8192]{0:T(1024)(128)(2,1)}, u32[]{:S(2)}) copy-start(bf16[8192]{0:T(1024)(128)(2,1)} %param.21) | copy-start | bytes 49156
  23.6 5.3 %collective-permute-start.6 = (bf16[24,128]{1,0:T(8,128)(2,1)S(1)}, bf16[24,128]{1,0:T(8,128)(2,1)S(1)}, u32[]{:S(2)}, u32[]{:S(2)}) collective-permute-start(bf16[24,128]{1,0:T(8,128)(2,1)S(1)} %get-tuple-element.43), channel_id=1, source_target_pairs={{7,4},{0,3},{15,12},{8,11},{23,20},{16,19},{31,28},{24,27},{39,36}... | collective-permute-start | bytes 18440 | tf_op jit(solution)/shard_map/ppermute | solution.py:338
  56.3 14.7 %all-to-all-start.2 = ((bf16[32,16,128]{2,1,0:T(8,128)(2,1)}), bf16[32,16,128]{2,1,0:T(8,128)(2,1)S(1)}, u32[]{:S(2)}, u32[]{:S(2)}) async-start(bf16[32,16,128]{2,1,0:T(8,128)(2,1)} %shard_map.113), calls=%async_computation.2 | async-start | bytes 262144 | tf_op jit(solution)/shard_map/all_to_all | solution.py:375
  61.8 3.7 %collective-permute-start.7 = (bf16[16,16,128]{2,1,0:T(8,128)(2,1)S(1)}, bf16[16,16,128]{2,1,0:T(8,128)(2,1)S(1)}, u32[]{:S(2)}, u32[]{:S(2)}) collective-permute-start(bf16[16,16,128]{2,1,0:T(8,128)(2,1)S(1)} %get-tuple-element.30), channel_id=1, source_target_pairs={{0,8},{8,0},{1,9},{9,1},{2,10},{10,2},{3,11},{11,3},{4,12},{12,4},... | collective-permute-start | bytes 196616 | tf_op jit(solution)/shard_map/ppermute | solution.py:355
  65.5 2.8 %copy-start.1 = (bf16[32,8192]{1,0:T(8,128)(2,1)S(1)}, bf16[32,8192]{1,0:T(8,128)(2,1)}, u32[]{:S(2)}) copy-start(bf16[32,8192]{1,0:T(8,128)(2,1)} %z_ref) | copy-start | bytes 1572868
